TPU v7x, 32 devices: a whole 2x2x4 slice. The times are simulated.
32 devices in a mesh: dp: 4 (over y, x), fsdp: 8 (over z, core).
Axes of the slice: x: 2, y: 2, z: 4, core: 2. Of those that a mesh axis runs over, the one named last changes fastest.
Arguments:
- prefix_in: bfloat16 [16, 816, 2048], P('fsdp', 'dp'), may hold values from -6 to 6
- action_in: bfloat16 [16, 48, 1024], P('fsdp', 'dp'), may hold values from -6 to 6
- valid_count: int32 [16], P('fsdp'), may hold values from 1 to 48, as said below
- prefix_before: bfloat16 [2048], P('fsdp'), may hold values from 0.5 to 1.5
- prefix_query: bfloat16 [2048, 2048], P('fsdp'), may hold values from -0.125 to 0.125
- prefix_key: bfloat16 [2048, 256], P('fsdp'), may hold values from -0.125 to 0.125
- prefix_value: bfloat16 [2048, 256], P('fsdp'), may hold values from -0.125 to 0.125
- prefix_output: bfloat16 [2048, 2048], P('fsdp'), may hold values from -4 to 4
- prefix_middle: bfloat16 [2048], P('fsdp'), may hold values from 0.5 to 1.5
- prefix_gate: bfloat16 [2048, 16384], P(None, 'fsdp'), may hold values from -0.125 to 0.125
- prefix_up: bfloat16 [2048, 16384], P(None, 'fsdp'), may hold values from -0.125 to 0.125
- prefix_down: bfloat16 [16384, 2048], P('fsdp'), may hold values from -0.046875 to 0.046875
- action_before: bfloat16 [1024], P('fsdp'), may hold values from 0.5 to 1.5
- action_query: bfloat16 [1024, 2048], P('fsdp'), may hold values from -0.1875 to 0.1875
- action_key: bfloat16 [1024, 256], P('fsdp'), may hold values from -0.1875 to 0.1875
- action_value: bfloat16 [1024, 256], P('fsdp'), may hold values from -0.1875 to 0.1875
- action_output: bfloat16 [2048, 1024], P('fsdp'), may hold values from -4 to 4
- action_middle: bfloat16 [1024], P('fsdp'), may hold values from 0.5 to 1.5
- action_gate: bfloat16 [1024, 4096], P(None, 'fsdp'), may hold values from -0.1875 to 0.1875
- action_up: bfloat16 [1024, 4096], P(None, 'fsdp'), may hold values from -0.1875 to 0.1875
- action_down: bfloat16 [4096, 1024], P('fsdp'), may hold values from -0.09375 to 0.09375
- prefix_cotangent: bfloat16 [16, 816, 2048], P('fsdp', 'dp'), may hold values from -6 to 6
- action_cotangent: bfloat16 [16, 48, 1024], P('fsdp', 'dp'), may hold values from -6 to 6
Outputs:
- prefix_out: bfloat16 [16, 816, 2048], P('fsdp', 'dp')
- action_out: bfloat16 [16, 48, 1024], P('fsdp', 'dp')
- prefix_grad: float32 [16, 816, 2048], P('fsdp', 'dp')
- action_grad: float32 [16, 48, 1024], P('fsdp', 'dp')
- prefix_before_grad: float32 [2048], P('fsdp')
- prefix_query_grad: float32 [2048, 2048], P('fsdp')
- prefix_key_grad: float32 [2048, 256], P('fsdp')
- prefix_value_grad: float32 [2048, 256], P('fsdp')
- prefix_output_grad: float32 [2048, 2048], P('fsdp')
- prefix_middle_grad: float32 [2048], P('fsdp')
- prefix_gate_grad: float32 [2048, 16384], P(None, 'fsdp')
- prefix_up_grad: float32 [2048, 16384], P(None, 'fsdp')
- prefix_down_grad: float32 [16384, 2048], P('fsdp')
- action_before_grad: float32 [1024], P('fsdp')
- action_query_grad: float32 [1024, 2048], P('fsdp')
- action_key_grad: float32 [1024, 256], P('fsdp')
- action_value_grad: float32 [1024, 256], P('fsdp')
- action_output_grad: float32 [2048, 1024], P('fsdp')
- action_middle_grad: float32 [1024], P('fsdp')
- action_gate_grad: float32 [1024, 4096], P(None, 'fsdp')
- action_up_grad: float32 [1024, 4096], P(None, 'fsdp')
- action_down_grad: float32 [4096, 1024], P('fsdp')
Inputs may be any that keep to these rules, and one draw needn't show every extreme that they name: The first valid_count of an item's 48 action tokens are valid. In every draw some item has exactly 48 valid action tokens and another exactly 1.
All inputs are finite; a program needn't handle non-finite values.
Results may differ from a plain program's by a relative error of at most 0.022.
Values may be sent and summed in bfloat16 or wider, within the bound.
A program may use at most 384 MiB of HBM per device.

v0:
```python
import jax
import jax.numpy as jnp
from jax import lax
from jax.sharding import PartitionSpec as P

EPS = 1e-06
NEGATIVE = -1e30


def normalize(rows, gain):
    return rows * lax.rsqrt(jnp.mean(rows * rows, axis=-1, keepdims=True) + EPS) * gain


def multiply(left, right):
    return jnp.dot(left, right, preferred_element_type=jnp.float32)


def multiply_left(left, right):
    return lax.dot_general(
        left, right, (((0,), (0,)), ((), ())), preferred_element_type=jnp.float32
    )


def multiply_right(left, right):
    return lax.dot_general(
        left, right, (((1,), (1,)), ((), ())), preferred_element_type=jnp.float32
    )


def activate(gate, upper):
    return jax.nn.gelu(gate, approximate=True) * upper


def feed_forward(rows, gate_weight, up_weight, down_weight):
    gate = multiply(rows, gate_weight)
    upper = multiply(rows, up_weight)
    inner = activate(gate, upper).astype(jnp.bfloat16)
    return (gate, upper, inner, multiply(inner, down_weight))


def feed_backward(rows, back, gate, upper, inner, gate_weight, up_weight, down_weight):
    down_grad = multiply_left(inner, back)
    inner_grad = multiply_right(back, down_weight)
    _, pull = jax.vjp(activate, gate, upper)
    gate_grad, up_grad = pull(inner_grad)
    gate_grad = gate_grad.astype(jnp.bfloat16)
    up_grad = up_grad.astype(jnp.bfloat16)
    rows_grad = multiply_right(gate_grad, gate_weight) + multiply_right(up_grad, up_weight)
    return (rows_grad, multiply_left(rows, gate_grad), multiply_left(rows, up_grad), down_grad)


def attention_scores(queries, keys, allowed, scale):
    scores = jnp.einsum("ithd,isd->ihts", queries, keys, preferred_element_type=jnp.float32) * scale
    return jnp.where(allowed[:, None], scores, NEGATIVE)


def body(
    prefix_in,
    action_in,
    valid_count,
    prefix_before,
    prefix_query,
    prefix_key,
    prefix_value,
    prefix_output,
    prefix_middle,
    prefix_gate,
    prefix_up,
    prefix_down,
    action_before,
    action_query,
    action_key,
    action_value,
    action_output,
    action_middle,
    action_gate,
    action_up,
    action_down,
    prefix_cotangent,
    action_cotangent,
):
    items, prefix_rows, width = prefix_in.shape
    action_rows = action_in.shape[1]
    action_width = action_in.shape[2]
    head_size = prefix_key.shape[1]
    features = prefix_query.shape[1]
    heads = features // head_size
    prefix_length = prefix_rows * lax.axis_size("dp")
    action_length = action_rows * lax.axis_size("dp")
    scale = head_size ** (-0.5)
    place = lax.axis_index("dp")
    weights = (
        lax.all_gather(prefix_before, "fsdp", axis=0, tiled=True),
        lax.all_gather(prefix_query, "fsdp", axis=0, tiled=True),
        lax.all_gather(prefix_key, "fsdp", axis=0, tiled=True),
        lax.all_gather(prefix_value, "fsdp", axis=0, tiled=True),
        lax.all_gather(prefix_output, "fsdp", axis=0, tiled=True),
        lax.all_gather(prefix_middle, "fsdp", axis=0, tiled=True),
        lax.all_gather(action_before, "fsdp", axis=0, tiled=True),
        lax.all_gather(action_query, "fsdp", axis=0, tiled=True),
        lax.all_gather(action_key, "fsdp", axis=0, tiled=True),
        lax.all_gather(action_value, "fsdp", axis=0, tiled=True),
        lax.all_gather(action_output, "fsdp", axis=0, tiled=True),
        lax.all_gather(action_middle, "fsdp", axis=0, tiled=True),
    )
    prefix_flat = prefix_in.reshape(items * prefix_rows, width).astype(jnp.float32)
    action_flat = action_in.reshape(items * action_rows, action_width).astype(jnp.float32)
    prefix_hidden = normalize(prefix_flat, weights[0].astype(jnp.float32)).astype(jnp.bfloat16)
    action_hidden = normalize(action_flat, weights[6].astype(jnp.float32)).astype(jnp.bfloat16)
    prefix_queries = multiply(prefix_hidden, weights[1]).astype(jnp.bfloat16)
    prefix_keys = multiply(prefix_hidden, weights[2]).astype(jnp.bfloat16)
    prefix_values = multiply(prefix_hidden, weights[3]).astype(jnp.bfloat16)
    action_queries = multiply(action_hidden, weights[7]).astype(jnp.bfloat16)
    action_keys = multiply(action_hidden, weights[8]).astype(jnp.bfloat16)
    action_values = multiply(action_hidden, weights[9]).astype(jnp.bfloat16)
    item_parts = (
        lax.all_gather(
            prefix_keys.reshape(items, prefix_rows, head_size), "dp", axis=1, tiled=True
        ),
        lax.all_gather(
            prefix_values.reshape(items, prefix_rows, head_size), "dp", axis=1, tiled=True
        ),
        lax.all_gather(
            action_keys.reshape(items, action_rows, head_size), "dp", axis=1, tiled=True
        ),
        lax.all_gather(
            action_values.reshape(items, action_rows, head_size), "dp", axis=1, tiled=True
        ),
    )
    all_keys = jnp.concatenate([item_parts[0], item_parts[2]], axis=1)
    all_values = jnp.concatenate([item_parts[1], item_parts[3]], axis=1)
    queries = jnp.concatenate(
        [
            prefix_queries.reshape(items, prefix_rows, heads, head_size),
            action_queries.reshape(items, action_rows, heads, head_size),
        ],
        axis=1,
    )
    query_place = jnp.concatenate(
        [
            place * prefix_rows + jnp.arange(prefix_rows),
            prefix_length + place * action_rows + jnp.arange(action_rows),
        ]
    )
    key_place = jnp.arange(prefix_length + action_length)
    later = (query_place[:, None] >= prefix_length) & (key_place[None, :] <= query_place[:, None])
    allowed = (key_place[None, None, :] < prefix_length) | later[None] & (
        key_place[None, None, :] < prefix_length + valid_count[:, None, None]
    )
    scores = attention_scores(queries, all_keys, allowed, scale)
    top = jnp.max(scores, axis=-1, keepdims=True)
    logsum = top + jnp.log(jnp.sum(jnp.exp(scores - top), axis=-1, keepdims=True))
    probs = jnp.exp(scores - logsum).astype(jnp.bfloat16)
    mixed = jnp.einsum(
        "ihts,isd->ithd", probs, all_values, preferred_element_type=jnp.float32
    ).astype(jnp.bfloat16)
    prefix_mixed = mixed[:, :prefix_rows].reshape(items * prefix_rows, features)
    action_mixed = mixed[:, prefix_rows:].reshape(items * action_rows, features)
    prefix_mid = prefix_flat + multiply(prefix_mixed, weights[4])
    action_mid = action_flat + multiply(action_mixed, weights[10])
    prefix_gain = weights[5].astype(jnp.float32)
    action_gain = weights[11].astype(jnp.float32)
    spread = (
        lax.all_gather(
            normalize(prefix_mid, prefix_gain).astype(jnp.bfloat16), "fsdp", axis=0, tiled=True
        ),
        lax.all_gather(
            normalize(action_mid, action_gain).astype(jnp.bfloat16), "fsdp", axis=0, tiled=True
        ),
    )
    prefix_gate_rows, prefix_up_rows, prefix_inner, prefix_part = feed_forward(
        spread[0], prefix_gate, prefix_up, prefix_down
    )
    action_gate_rows, action_up_rows, action_inner, action_part = feed_forward(
        spread[1], action_gate, action_up, action_down
    )
    sums = (
        lax.psum_scatter(
            prefix_part.astype(jnp.bfloat16), "fsdp", scatter_dimension=0, tiled=True
        ).astype(jnp.float32),
        lax.psum_scatter(
            action_part.astype(jnp.bfloat16), "fsdp", scatter_dimension=0, tiled=True
        ).astype(jnp.float32),
    )
    prefix_out = (prefix_mid + sums[0]).astype(jnp.bfloat16).reshape(items, prefix_rows, width)
    action_out = (
        (action_mid + sums[1]).astype(jnp.bfloat16).reshape(items, action_rows, action_width)
    )
    live = (place * action_rows + jnp.arange(action_rows))[None, :] < valid_count[:, None]
    action_back = jnp.where(
        live[:, :, None], action_cotangent, jnp.zeros_like(action_cotangent)
    ).reshape(items * action_rows, action_width)
    prefix_back = prefix_cotangent.reshape(items * prefix_rows, width)
    spread_back = (
        lax.all_gather(prefix_back, "fsdp", axis=0, tiled=True),
        lax.all_gather(action_back, "fsdp", axis=0, tiled=True),
    )
    feed_prefix = feed_backward(
        spread[0],
        spread_back[0],
        prefix_gate_rows,
        prefix_up_rows,
        prefix_inner,
        prefix_gate,
        prefix_up,
        prefix_down,
    )
    feed_action = feed_backward(
        spread[1],
        spread_back[1],
        action_gate_rows,
        action_up_rows,
        action_inner,
        action_gate,
        action_up,
        action_down,
    )
    feed_back = (
        lax.psum_scatter(feed_prefix[0], "fsdp", scatter_dimension=0, tiled=True),
        lax.psum_scatter(feed_action[0], "fsdp", scatter_dimension=0, tiled=True),
    )
    feed_totals = (
        feed_prefix[1],
        feed_prefix[2],
        feed_prefix[3],
        feed_action[1],
        feed_action[2],
        feed_action[3],
    )
    _, pull = jax.vjp(normalize, prefix_mid, prefix_gain)
    prefix_inner_grad, prefix_middle_part = pull(feed_back[0])
    _, pull = jax.vjp(normalize, action_mid, action_gain)
    action_inner_grad, action_middle_part = pull(feed_back[1])
    prefix_mid_grad = prefix_back.astype(jnp.float32) + prefix_inner_grad
    action_mid_grad = action_back.astype(jnp.float32) + action_inner_grad
    weights_back = (
        lax.all_gather(prefix_before, "fsdp", axis=0, tiled=True),
        lax.all_gather(prefix_query, "fsdp", axis=0, tiled=True),
        lax.all_gather(prefix_key, "fsdp", axis=0, tiled=True),
        lax.all_gather(prefix_value, "fsdp", axis=0, tiled=True),
        lax.all_gather(prefix_output, "fsdp", axis=0, tiled=True),
        lax.all_gather(prefix_middle, "fsdp", axis=0, tiled=True),
        lax.all_gather(action_before, "fsdp", axis=0, tiled=True),
        lax.all_gather(action_query, "fsdp", axis=0, tiled=True),
        lax.all_gather(action_key, "fsdp", axis=0, tiled=True),
        lax.all_gather(action_value, "fsdp", axis=0, tiled=True),
        lax.all_gather(action_output, "fsdp", axis=0, tiled=True),
        lax.all_gather(action_middle, "fsdp", axis=0, tiled=True),
    )
    prefix_low = prefix_mid_grad.astype(jnp.bfloat16)
    action_low = action_mid_grad.astype(jnp.bfloat16)
    mixed_grad = jnp.concatenate(
        [
            multiply_right(prefix_low, weights_back[4])
            .astype(jnp.bfloat16)
            .reshape(items, prefix_rows, heads, head_size),
            multiply_right(action_low, weights_back[10])
            .astype(jnp.bfloat16)
            .reshape(items, action_rows, heads, head_size),
        ],
        axis=1,
    )
    scores = attention_scores(queries, all_keys, allowed, scale)
    softmax = jnp.exp(scores - logsum)
    probs_grad = jnp.einsum(
        "ithd,isd->ihts", mixed_grad, all_values, preferred_element_type=jnp.float32
    )
    delta = jnp.sum(softmax * probs_grad, axis=-1, keepdims=True)
    score_grad = (softmax * (probs_grad - delta)).astype(jnp.bfloat16)
    query_grad = (
        jnp.einsum("ihts,isd->ithd", score_grad, all_keys, preferred_element_type=jnp.float32)
        * scale
    ).astype(jnp.bfloat16)
    key_grad = (
        jnp.einsum("ihts,ithd->isd", score_grad, queries, preferred_element_type=jnp.float32)
        * scale
    )
    value_grad = jnp.einsum(
        "ihts,ithd->isd",
        softmax.astype(jnp.bfloat16),
        mixed_grad,
        preferred_element_type=jnp.float32,
    )
    owner_parts = (
        lax.psum_scatter(
            key_grad[:, :prefix_length].astype(jnp.bfloat16), "dp", scatter_dimension=1, tiled=True
        ).astype(jnp.float32),
        lax.psum_scatter(
            value_grad[:, :prefix_length].astype(jnp.bfloat16),
            "dp",
            scatter_dimension=1,
            tiled=True,
        ).astype(jnp.float32),
        lax.psum_scatter(
            key_grad[:, prefix_length:].astype(jnp.bfloat16), "dp", scatter_dimension=1, tiled=True
        ).astype(jnp.float32),
        lax.psum_scatter(
            value_grad[:, prefix_length:].astype(jnp.bfloat16),
            "dp",
            scatter_dimension=1,
            tiled=True,
        ).astype(jnp.float32),
    )
    prefix_key_grad = owner_parts[0].reshape(items * prefix_rows, head_size).astype(jnp.bfloat16)
    prefix_value_grad = owner_parts[1].reshape(items * prefix_rows, head_size).astype(jnp.bfloat16)
    action_key_grad = owner_parts[2].reshape(items * action_rows, head_size).astype(jnp.bfloat16)
    action_value_grad = owner_parts[3].reshape(items * action_rows, head_size).astype(jnp.bfloat16)
    prefix_query_grad = query_grad[:, :prefix_rows].reshape(items * prefix_rows, features)
    action_query_grad = query_grad[:, prefix_rows:].reshape(items * action_rows, features)
    prefix_hidden_grad = (
        multiply_right(prefix_query_grad, weights_back[1])
        + multiply_right(prefix_key_grad, weights_back[2])
        + multiply_right(prefix_value_grad, weights_back[3])
    )
    action_hidden_grad = (
        multiply_right(action_query_grad, weights_back[7])
        + multiply_right(action_key_grad, weights_back[8])
        + multiply_right(action_value_grad, weights_back[9])
    )
    _, pull = jax.vjp(normalize, prefix_flat, weights_back[0].astype(jnp.float32))
    prefix_entry_grad, prefix_before_part = pull(prefix_hidden_grad)
    _, pull = jax.vjp(normalize, action_flat, weights_back[6].astype(jnp.float32))
    action_entry_grad, action_before_part = pull(action_hidden_grad)
    prefix_grad = (prefix_mid_grad + prefix_entry_grad).reshape(items, prefix_rows, width)
    action_grad = (action_mid_grad + action_entry_grad).reshape(items, action_rows, action_width)
    owned = (
        lax.psum_scatter(
            prefix_before_part.astype(jnp.bfloat16), "fsdp", scatter_dimension=0, tiled=True
        ).astype(jnp.float32),
        lax.psum_scatter(
            multiply_left(prefix_hidden, prefix_query_grad).astype(jnp.bfloat16),
            "fsdp",
            scatter_dimension=0,
            tiled=True,
        ).astype(jnp.float32),
        lax.psum_scatter(
            multiply_left(prefix_hidden, prefix_key_grad).astype(jnp.bfloat16),
            "fsdp",
            scatter_dimension=0,
            tiled=True,
        ).astype(jnp.float32),
        lax.psum_scatter(
            multiply_left(prefix_hidden, prefix_value_grad).astype(jnp.bfloat16),
            "fsdp",
            scatter_dimension=0,
            tiled=True,
        ).astype(jnp.float32),
        lax.psum_scatter(
            multiply_left(prefix_mixed, prefix_low).astype(jnp.bfloat16),
            "fsdp",
            scatter_dimension=0,
            tiled=True,
        ).astype(jnp.float32),
        lax.psum_scatter(
            prefix_middle_part.astype(jnp.bfloat16), "fsdp", scatter_dimension=0, tiled=True
        ).astype(jnp.float32),
        lax.psum_scatter(
            action_before_part.astype(jnp.bfloat16), "fsdp", scatter_dimension=0, tiled=True
        ).astype(jnp.float32),
        lax.psum_scatter(
            multiply_left(action_hidden, action_query_grad).astype(jnp.bfloat16),
            "fsdp",
            scatter_dimension=0,
            tiled=True,
        ).astype(jnp.float32),
        lax.psum_scatter(
            multiply_left(action_hidden, action_key_grad).astype(jnp.bfloat16),
            "fsdp",
            scatter_dimension=0,
            tiled=True,
        ).astype(jnp.float32),
        lax.psum_scatter(
            multiply_left(action_hidden, action_value_grad).astype(jnp.bfloat16),
            "fsdp",
            scatter_dimension=0,
            tiled=True,
        ).astype(jnp.float32),
        lax.psum_scatter(
            multiply_left(action_mixed, action_low).astype(jnp.bfloat16),
            "fsdp",
            scatter_dimension=0,
            tiled=True,
        ).astype(jnp.float32),
        lax.psum_scatter(
            action_middle_part.astype(jnp.bfloat16), "fsdp", scatter_dimension=0, tiled=True
        ).astype(jnp.float32),
    )
    summed = (
        lax.psum(owned[0].astype(jnp.bfloat16), "dp").astype(jnp.float32),
        lax.psum(owned[1].astype(jnp.bfloat16), "dp").astype(jnp.float32),
        lax.psum(owned[2].astype(jnp.bfloat16), "dp").astype(jnp.float32),
        lax.psum(owned[3].astype(jnp.bfloat16), "dp").astype(jnp.float32),
        lax.psum(owned[4].astype(jnp.bfloat16), "dp").astype(jnp.float32),
        lax.psum(owned[5].astype(jnp.bfloat16), "dp").astype(jnp.float32),
        lax.psum(owned[6].astype(jnp.bfloat16), "dp").astype(jnp.float32),
        lax.psum(owned[7].astype(jnp.bfloat16), "dp").astype(jnp.float32),
        lax.psum(owned[8].astype(jnp.bfloat16), "dp").astype(jnp.float32),
        lax.psum(owned[9].astype(jnp.bfloat16), "dp").astype(jnp.float32),
        lax.psum(owned[10].astype(jnp.bfloat16), "dp").astype(jnp.float32),
        lax.psum(owned[11].astype(jnp.bfloat16), "dp").astype(jnp.float32),
        lax.psum(feed_totals[0].astype(jnp.bfloat16), "dp").astype(jnp.float32),
        lax.psum(feed_totals[1].astype(jnp.bfloat16), "dp").astype(jnp.float32),
        lax.psum(feed_totals[2].astype(jnp.bfloat16), "dp").astype(jnp.float32),
        lax.psum(feed_totals[3].astype(jnp.bfloat16), "dp").astype(jnp.float32),
        lax.psum(feed_totals[4].astype(jnp.bfloat16), "dp").astype(jnp.float32),
        lax.psum(feed_totals[5].astype(jnp.bfloat16), "dp").astype(jnp.float32),
    )
    owned = summed[:12]
    feed_totals = summed[12:]
    return (
        prefix_out,
        action_out,
        prefix_grad,
        action_grad,
        owned[0],
        owned[1],
        owned[2],
        owned[3],
        owned[4],
        owned[5],
        feed_totals[0],
        feed_totals[1],
        feed_totals[2],
        owned[6],
        owned[7],
        owned[8],
        owned[9],
        owned[10],
        owned[11],
        feed_totals[3],
        feed_totals[4],
        feed_totals[5],
    )


def solution(mesh):
    return jax.shard_map(
        body,
        mesh=mesh,
        in_specs=(
            P("fsdp", "dp", None),
            P("fsdp", "dp", None),
            P("fsdp"),
            P("fsdp"),
            P("fsdp", None),
            P("fsdp", None),
            P("fsdp", None),
            P("fsdp", None),
            P("fsdp"),
            P(None, "fsdp"),
            P(None, "fsdp"),
            P("fsdp", None),
            P("fsdp"),
            P("fsdp", None),
            P("fsdp", None),
            P("fsdp", None),
            P("fsdp", None),
            P("fsdp"),
            P(None, "fsdp"),
            P(None, "fsdp"),
            P("fsdp", None),
            P("fsdp", "dp", None),
            P("fsdp", "dp", None),
        ),
        out_specs=(
            P("fsdp", "dp", None),
            P("fsdp", "dp", None),
            P("fsdp", "dp", None),
            P("fsdp", "dp", None),
            P("fsdp"),
            P("fsdp", None),
            P("fsdp", None),
            P("fsdp", None),
            P("fsdp", None),
            P("fsdp"),
            P(None, "fsdp"),
            P(None, "fsdp"),
            P("fsdp", None),
            P("fsdp"),
            P("fsdp", None),
            P("fsdp", None),
            P("fsdp", None),
            P("fsdp", None),
            P("fsdp"),
            P(None, "fsdp"),
            P(None, "fsdp"),
            P("fsdp", None),
        ),
        check_vma=False,
    )
```

profile of v0, /device:TPU:0, one launch (start us, length us, event | category | flops | bytes accessed | tf_op | source)
XLA Modules:
  0.0 2300.2 jit_solution(17318629598475093865)
XLA Ops:
  148.1 47.4 %all-gather.17.cloned.1.call-done = bf16[2048,2048]{1,0:T(8,128)(2,1)} async-done(((bf16[256,2048]{1,0:T(8,128)(2,1)}), bf16[2048,2048]{1,0:T(8,128)(2,1)}) %all-gather.17.cloned.1.call-update) | async-done | bytes 8388624 | tf_op jit(solution)/shard_map/all_gather | solution.py:94
  216.6 60.9 %all-gather.21.cloned.1.call-done = bf16[2048,2048]{1,0:T(8,128)(2,1)} async-done(((bf16[256,2048]{1,0:T(8,128)(2,1)}), bf16[2048,2048]{1,0:T(8,128)(2,1)}) %all-gather.21.cloned.1.call-update) | async-done | bytes 8388624 | tf_op jit(solution)/shard_map/all_gather | solution.py:97
  302.2 17.3 all_gather.89
  352.4 100.1 %all-gather.23.cloned.1.call-done = bf16[3264,2048]{1,0:T(8,128)(2,1)} async-done(((bf16[408,2048]{1,0:T(8,128)(2,1)}), bf16[3264,2048]{1,0:T(8,128)(2,1)}) %all-gather.23.cloned.1.call-update) | async-done | bytes 13369360 | tf_op jit(solution)/shard_map/all_gather | solution.py:164
  452.4 35.6 %fusion.57 = f32[3264,2048]{1,0:T(8,128)} fusion(bf16[3264,2048]{1,0:T(8,128)(2,1)} %all-gather.23.cloned.1.call-done, bf16[2048,2048]{1,0:T(8,128)(2,1)} %param.32), kind=kOutput, calls=%fused_computation.157 | convolution fusion | flops 27380416512 | bytes 48496640 | tf_op jit(solution)/shard_map/dot_general | solution.py:15
  488.0 33.0 %fusion.58 = f32[3264,2048]{1,0:T(8,128)} fusion(bf16[3264,2048]{1,0:T(8,128)(2,1)S(1)} %copy-done.118, bf16[2048,2048]{1,0:T(8,128)(2,1)} %param.33), kind=kOutput, calls=%fused_computation.158 | convolution fusion | flops 27380416512 | bytes 48496640 | tf_op jit(solution)/shard_map/dot_general | solution.py:15
  521.0 55.6 %all-gather.27.cloned.1.call-done = bf16[3264,2048]{1,0:T(8,128)(2,1)} async-done(((bf16[408,2048]{1,0:T(8,128)(2,1)}), bf16[3264,2048]{1,0:T(8,128)(2,1)}) %all-gather.27.cloned.1.call-update) | async-done | bytes 13369360 | tf_op jit(solution)/shard_map/all_gather | solution.py:195
  576.6 56.4 %multiply_convert_fusion = (bf16[3264,2048]{1,0:T(8,128)(2,1)}, bf16[3264,2048]{1,0:T(8,128)(2,1)}, bf16[3264,2048]{1,0:T(8,128)(2,1)}) fusion(f32[3264,2048]{1,0:T(8,128)} %fusion.57, f32[3264,2048]{1,0:T(8,128)} %fusion.58, bf16[3264,2048]{1,0:T(8,128)(2,1)} %all-gather.27.cloned.1.call-done, bf16[2048,2048]{1,0:T(8,128)(2,1)} %param.34), kind=kOutput, calls=%fused_computation.9 | convolution fusion | flops 27554217984 | bytes 115343360 | tf_op jit(solution)/shard_map/dot_general | solution.py:25
  633.0 35.6 %fusion.61 = f32[3264,2048]{1,0:T(8,128)} fusion(bf16[3264,2048]{1,0:T(8,128)(2,1)} %get-tuple-element.147, bf16[2048,2048]{1,0:T(8,128)(2,1)} %param.32), kind=kOutput, calls=%fused_computation.161 | convolution fusion | flops 27380416512 | bytes 48496640 | tf_op jit(solution)/shard_map/dot_general | solution.py:25
  668.6 37.3 %convolution_add_fusion = f32[3264,2048]{1,0:T(8,128)} fusion(f32[3264,2048]{1,0:T(8,128)} %fusion.61, bf16[3264,2048]{1,0:T(8,128)(2,1)} %get-tuple-element.146, bf16[2048,2048]{1,0:T(8,128)(2,1)} %param.33), kind=kOutput, calls=%fused_computation.12 | convolution fusion | flops 27387101184 | bytes 75235328 | tf_op jit(solution)/shard_map/dot_general | solution.py:25
  705.9 34.1 %convolution_convert_fusion = bf16[3264,2048]{1,0:T(8,128)(2,1)} fusion(bf16[3264,2048]{1,0:T(8,128)(2,1)} %get-tuple-element.148, bf16[2048,2048]{1,0:T(8,128)(2,1)} %param.34), kind=kOutput, calls=%fused_computation.13 | convolution fusion | flops 27387101184 | bytes 35127296 | tf_op jit(solution)/shard_map/dot_general | solution.py:15
  747.6 218.6 %reduce-scatter.17.cloned.1.call-done = f32[408,2048]{1,0:T(8,128)} async-done(((f32[3264,2048]{1,0:T(8,128)}), f32[408,2048]{1,0:T(8,128)}) %reduce-scatter.17.cloned.1.call-update) | async-done | bytes 3342352 | tf_op jit(solution)/shard_map/reduce_scatter | solution.py:219
  970.7 132.8 %reduce-scatter.13.cloned.1.call-done = bf16[408,2048]{1,0:T(8,128)(2,1)} async-done(((bf16[3264,2048]{1,0:T(8,128)(2,1)}), bf16[408,2048]{1,0:T(8,128)(2,1)}) %reduce-scatter.13.cloned.1.call-update) | async-done | bytes 1671184 | tf_op jit(solution)/shard_map/reduce_scatter | solution.py:178
  1154.2 32.3 %all-reduce.17.cloned.1.call-done = (bf16[2,48,256]{2,0,1:T(2,128)(2,1)}, bf16[2,48,256]{2,0,1:T(2,128)(2,1)}) async-done(((bf16[2,48,256]{2,0,1:T(2,128)(2,1)}, bf16[2,48,256]{2,0,1:T(2,128)(2,1)}), (bf16[2,48,256]{2,0,1:T(2,128)(2,1)}, bf16[2,48,256]{2,0,1:T(2,128)(2,1)})) %all-reduce.17.cloned.1.call-update) | async-done | bytes 98320
  1194.5 59.3 %all-reduce.21.cloned.1.call-done = (bf16[2,816,256]{2,0,1:T(2,128)(2,1)}, bf16[2,816,256]{2,0,1:T(2,128)(2,1)}) async-done(((bf16[2,816,256]{2,0,1:T(2,128)(2,1)}, bf16[2,816,256]{2,0,1:T(2,128)(2,1)}), (bf16[2,816,256]{2,0,1:T(2,128)(2,1)}, bf16[2,816,256]{2,0,1:T(2,128)(2,1)})) %all-reduce.21.cloned.1.call-update) | async-done | bytes 1671184
  1302.0 36.7 %convolution_convert_fusion.2 = bf16[2048,2048]{1,0:T(8,128)(2,1)} fusion(bf16[3264,2048]{1,0:T(8,128)(2,1)} %all-gather.23.cloned.1.call-done, bf16[3264,2048]{1,0:T(8,128)(2,1)} %get-tuple-element.146), kind=kOutput, calls=%fused_computation.24 | convolution fusion | flops 27384610816 | bytes 35127296 | tf_op jit(solution)/shard_map/dot_general | solution.py:19
  1338.7 34.2 %convolution_convert_fusion.3 = bf16[2048,2048]{1,0:T(8,128)(2,1)} fusion(bf16[3264,2048]{1,0:T(8,128)(2,1)S(1)} %bitcast.210, bf16[3264,2048]{1,0:T(8,128)(2,1)} %get-tuple-element.147), kind=kOutput, calls=%fused_computation.25 | convolution fusion | flops 27384610816 | bytes 35127296 | tf_op jit(solution)/shard_map/dot_general | solution.py:19
  1372.9 37.2 %convolution_convert_fusion.1 = bf16[2048,2048]{1,0:T(8,128)(2,1)} fusion(bf16[3264,2048]{1,0:T(8,128)(2,1)} %get-tuple-element.148, bf16[3264,2048]{1,0:T(8,128)(2,1)} %all-gather.27.cloned.1.call-done), kind=kOutput, calls=%fused_computation.23 | convolution fusion | flops 27384610816 | bytes 35127296 | tf_op jit(solution)/shard_map/dot_general | solution.py:19
  1410.2 25.4 %reduce-scatter.25.cloned.1.call-done = bf16[256,256]{1,0:T(8,128)(2,1)} async-done(((bf16[2048,256]{1,0:T(8,128)(2,1)}), bf16[256,256]{1,0:T(8,128)(2,1)}) %reduce-scatter.25.cloned.1.call-update) | async-done | bytes 131088 | tf_op jit(solution)/shard_map/reduce_scatter | solution.py:342
  1435.6 50.6 %reduce-scatter.29.cloned.1.call-done = bf16[128,2048]{1,0:T(8,128)(2,1)} async-done(((bf16[1024,2048]{1,0:T(8,128)(2,1)}), bf16[128,2048]{1,0:T(8,128)(2,1)}) %reduce-scatter.29.cloned.1.call-update) | async-done | bytes 524304 | tf_op jit(solution)/shard_map/reduce_scatter | solution.py:360
  1486.2 90.2 %reduce-scatter.21.cloned.1.call-done = bf16[256,2048]{1,0:T(8,128)(2,1)} async-done(((bf16[2048,2048]{1,0:T(8,128)(2,1)}), bf16[256,2048]{1,0:T(8,128)(2,1)}) %reduce-scatter.21.cloned.1.call-update) | async-done | bytes 1048592 | tf_op jit(solution)/shard_map/reduce_scatter | solution.py:330
  1576.4 90.4 %reduce-scatter.27.cloned.1.call-done = bf16[256,2048]{1,0:T(8,128)(2,1)} async-done(((bf16[2048,2048]{1,0:T(8,128)(2,1)}), bf16[256,2048]{1,0:T(8,128)(2,1)}) %reduce-scatter.27.cloned.1.call-update) | async-done | bytes 1048592 | tf_op jit(solution)/shard_map/reduce_scatter | solution.py:348
  1696.0 26.2 %all-reduce.8 = (bf16[2048]{0:T(1024)(128)(2,1)S(1)}, bf16[2048]{0:T(1024)(128)(2,1)S(1)}, bf16[1024]{0:T(1024)(128)(2,1)S(1)}, bf16[1024]{0:T(1024)(128)(2,1)S(1)}) all-reduce(bf16[2048]{0:T(1024)(128)(2,1)S(1)} %get-tuple-element.112, bf16[2048]{0:T(1024)(128)(2,1)S(1)} %copy-done.104, ...), channel_id=10, replica_groups=mesh['dp'=4,'fsdp'=8] {'fsdp'}, use_global_device_ids=true, to_apply=%region_20.21.clone | all-reduce | flops 6144 | bytes 24576
  1751.9 493.6 %all-reduce.19.cloned.1.call-done = (bf16[256,2048]{1,0:T(8,128)(2,1)}, bf16[256,256]{1,0:T(8,128)(2,1)}, bf16[256,256]{1,0:T(8,128)(2,1)}, bf16[256,2048]{1,0:T...) async-done(((bf16[256,2048]{1,0:T(8,128)(2,1)}, ...) | async-done | bytes 31850512 | tf_op jit(solution)/shard_map/psum | solution.py:390
  (512 shorter events, 441.0 us)
Async XLA Ops:
  7.2 104.2 %all-gather.15.cloned.1.call-start = ((), (), s32[]{:S(2)}) async-start(), calls=%async_computation.13 | async-start | bytes 1179648 | tf_op jit(solution)/shard_map/all_gather | solution.py:95
  8.0 120.2 %all-gather.13.cloned.1.call-start = ((), (), s32[]{:S(2)}) async-start(), calls=%async_computation.12 | async-start | bytes 1179648 | tf_op jit(solution)/shard_map/all_gather | solution.py:96
  8.7 136.4 %all-gather.19.cloned.1.call-start = ((), (), s32[]{:S(2)}) async-start(), calls=%async_computation.15 | async-start | bytes 4718592 | tf_op jit(solution)/shard_map/all_gather | solution.py:100
  9.4 186.0 %all-gather.17.cloned.1.call-start = ((), (), s32[]{:S(2)}) async-start(), calls=%async_computation.14 | async-start | bytes 9437184 | tf_op jit(solution)/shard_map/all_gather | solution.py:94
  10.0 267.5 %all-gather.21.cloned.1.call-start = ((), (), s32[]{:S(2)}) async-start(), calls=%async_computation.16 | async-start | bytes 9437184 | tf_op jit(solution)/shard_map/all_gather | solution.py:97
  10.6 317.1 %all-gather.25.cloned.1.call-start = ((), (), s32[]{:S(2)}) async-start(), calls=%async_computation.19 | async-start | bytes 4718592 | tf_op jit(solution)/shard_map/all_gather | solution.py:103
  11.2 441.2 %all-gather.23.cloned.1.call-start = ((), (), s32[]{:S(2)}) async-start(), calls=%async_computation.17 | async-start | bytes 15040512 | tf_op jit(solution)/shard_map/all_gather | solution.py:164
  289.0 287.7 %all-gather.27.cloned.1.call-start = ((), (), s32[]{:S(2)}) async-start(), calls=%async_computation.21 | async-start | bytes 15040512 | tf_op jit(solution)/shard_map/all_gather | solution.py:195
  292.7 447.7 %reduce-scatter.19.cloned.1.call-start = ((), (), s32[]{:S(2)}) async-start(), calls=%async_computation.23 | async-start | bytes 884736 | tf_op jit(solution)/shard_map/reduce_scatter | solution.py:220
  351.1 391.4 %reduce-scatter.15.cloned.1.call-start = ((), (), s32[]{:S(2)}) async-start(), calls=%async_computation.20 | async-start | bytes 442368 | tf_op jit(solution)/shard_map/reduce_scatter | solution.py:181
  352.3 613.9 %reduce-scatter.17.cloned.1.call-start = ((), (), s32[]{:S(2)}) async-start(), calls=%async_computation.22 | async-start | bytes 30081024 | tf_op jit(solution)/shard_map/reduce_scatter | solution.py:219
  705.9 397.5 %reduce-scatter.13.cloned.1.call-start = ((), (), s32[]{:S(2)}) async-start(), calls=%async_computation.18 | async-start | bytes 15040512 | tf_op jit(solution)/shard_map/reduce_scatter | solution.py:178
  740.1 446.3 %all-reduce.17.cloned.1.call-start = ((), (), s32[]{:S(2)}) async-start(), calls=%async_computation.32 | async-start | bytes 196608
  744.1 405.4 %copy-start.34 = (f32[24,1024]{1,0:T(8,128)}, f32[24,1024]{1,0:T(8,128)S(1)}, u32[]{:S(2)}) copy-start(f32[24,1024]{1,0:T(8,128)S(1)} %get-tuple-element.154) | copy-start | bytes 294916
  1146.1 107.8 %all-reduce.21.cloned.1.call-start = ((), (), s32[]{:S(2)}) async-start(), calls=%async_computation.34 | async-start | bytes 3342336
  1149.4 260.7 %reduce-scatter.35.cloned.1.call-start = ((), (), s32[]{:S(2)}) async-start(), calls=%async_computation.31 | async-start | bytes 4718592 | tf_op jit(solution)/shard_map/reduce_scatter | solution.py:378
  1152.8 257.4 %reduce-scatter.31.cloned.1.call-start = ((), (), s32[]{:S(2)}) async-start(), calls=%async_computation.29 | async-start | bytes 589824 | tf_op jit(solution)/shard_map/reduce_scatter | solution.py:366
  1188.4 221.7 %reduce-scatter.33.cloned.1.call-start = ((), (), s32[]{:S(2)}) async-start(), calls=%async_computation.30 | async-start | bytes 589824 | tf_op jit(solution)/shard_map/reduce_scatter | solution.py:372
  1190.3 219.8 %reduce-scatter.23.cloned.1.call-start = ((), (), s32[]{:S(2)}) async-start(), calls=%async_computation.25 | async-start | bytes 1179648 | tf_op jit(solution)/shard_map/reduce_scatter | solution.py:336
  1258.7 176.9 %reduce-scatter.25.cloned.1.call-start = ((), (), s32[]{:S(2)}) async-start(), calls=%async_computation.26 | async-start | bytes 1179648 | tf_op jit(solution)/shard_map/reduce_scatter | solution.py:342
  1262.0 224.1 %reduce-scatter.29.cloned.1.call-start = ((), (), s32[]{:S(2)}) async-start(), calls=%async_computation.28 | async-start | bytes 4718592 | tf_op jit(solution)/shard_map/reduce_scatter | solution.py:360
  1271.6 304.8 %reduce-scatter.21.cloned.1.call-start = ((), (), s32[]{:S(2)}) async-start(), calls=%async_computation.24 | async-start | bytes 9437184 | tf_op jit(solution)/shard_map/reduce_scatter | solution.py:330
  1286.4 380.4 %reduce-scatter.27.cloned.1.call-start = ((), (), s32[]{:S(2)}) async-start(), calls=%async_computation.27 | async-start | bytes 9437184 | tf_op jit(solution)/shard_map/reduce_scatter | solution.py:348
  1296.6 948.9 %all-reduce.19.cloned.1.call-start = ((), (), s32[]{:S(2)}) async-start(), calls=%async_computation.33 | async-start | bytes 63700992 | tf_op jit(solution)/shard_map/psum | solution.py:390
  (129 other events, 3822.0 us)
Sparse Core Ops, SparseCore 0:
  9.7 24.7 all-gather.14
  36.1 24.7 all-gather.12
  62.5 50.4 all-gather.18
  114.4 80.9 all-gather.16
  196.9 80.5 all-gather.20
  279.0 48.7 all-gather.24
  330.0 122.4 all-gather.22
  454.6 121.9 all-gather.26
  579.5 29.7 reduce-scatter.18
  612.0 28.7 reduce-scatter.14
  706.0 260.1 reduce-scatter.16
  968.4 134.9 reduce-scatter.12
  1146.2 40.2 all-reduce.16
  1191.0 62.8 all-reduce.20
  1256.1 49.9 reduce-scatter.34
  1308.3 29.0 reduce-scatter.30
  1339.6 29.0 reduce-scatter.32
  1371.5 30.3 reduce-scatter.22
  1404.9 30.6 reduce-scatter.24
  1437.8 48.3 reduce-scatter.28
  1488.6 87.7 reduce-scatter.20
  1578.8 87.9 reduce-scatter.26
  1675.3 570.1 all-reduce.18
where the time goes:
time: 2310 us; the launch traced here: 2300 us
  waiting for transfers between devices  1470 us (64%)
  matrix products  468 us (20%)
  blocking collectives  186 us (8%)
  other arithmetic  91.3 us (4%)
  local copies, waits for them, and re-layouts  66.1 us (3%)
    psum x1, waiting for transfers between devices, body(): lax.psum(owned[1].astype(jnp.bfloat16), 'dp').astype(jnp.float32)  494 us
    reduce_scatter x1, waiting for transfers between devices, body(): lax.psum_scatter(feed_prefix[0], 'fsdp', scatter_dimension=0, tiled=True)  219 us
    dot_general x14, matrix products, multiply_right(): lax.dot_general(left, right, (((1,), (1,)), ((), ())), preferred_element_...  163 us
    dot_general x14, matrix products, multiply_left(): lax.dot_general(left, right, (((0,), (0,)), ((), ())), preferred_element_...  143 us
    reduce_scatter x1, waiting for transfers between devices, body(): lax.psum_scatter(prefix_part.astype(jnp.bfloat16), 'fsdp', scatter_dimens...  133 us
    dot_general x14, matrix products, multiply(): return jnp.dot(left, right, preferred_element_type=jnp.float32)  131 us
    all_gather x1, waiting for transfers between devices, body(): lax.all_gather(normalize(prefix_mid, prefix_gain).astype(jnp.bfloat16), '...  100 us
    unnamed x25, waiting for transfers between devices  95.5 us
  transfers between devices with their start and end apart: 23, of which 14 were waited for; matrix products, arithmetic and copies ran while one was open for 23% of the time, Pallas kernels for 0%

commit v1 on v0

v1 whole, which is shorter than its diff:
```python
import functools
import math

import jax
import jax.numpy as jnp
from jax import lax
from jax.experimental import pallas as pl
from jax.experimental.pallas import tpu as pltpu
from jax.sharding import PartitionSpec as P

EPS = 1e-06
NEGATIVE = -1e30
LOW = jnp.bfloat16
FULL = jnp.float32
TILE = 16
MIB = 1 << 20


def normalize(rows, gain):
    return rows * lax.rsqrt(jnp.mean(rows * rows, axis=-1, keepdims=True) + EPS) * gain


def multiply(left, right):
    return jnp.dot(left, right, preferred_element_type=FULL)


def multiply_left(left, right):
    return lax.dot_general(
        left, right, (((0,), (0,)), ((), ())), preferred_element_type=FULL
    )


def multiply_right(left, right):
    return lax.dot_general(
        left, right, (((1,), (1,)), ((), ())), preferred_element_type=FULL
    )


def activate(gate, upper):
    return jax.nn.gelu(gate, approximate=True) * upper


class Line:
    def __init__(self):
        self.size = lax.axis_size("fsdp")
        self.chips = self.size // 2
        self.place = lax.axis_index("fsdp")
        self.chip = self.place // 2
        self.core = self.place % 2
        self.order = [
            sorted(range(self.chips), key=lambda other: (abs(other - chip), other))
            for chip in range(self.chips)
        ]

    def is_one_of(self, chips):
        found = self.chip == chips[0]
        for chip in chips[1:]:
            found = found | (self.chip == chip)
        return found

    def move(self, value, chips, step):
        pairs = [
            (2 * chip + core, 2 * (chip + step) + core) for chip in chips for core in range(2)
        ]
        return lax.ppermute(value, "fsdp", pairs)

    def partner(self, value):
        return lax.ppermute(value, "fsdp", [(i, i ^ 1) for i in range(self.size)])

    def choose(self, options):
        items = list(options.values())
        result = items[-1][1]
        for chips, value in items[:-1]:
            result = jnp.where(self.is_one_of(chips), value, result)
        return result

    def gather(self, block):
        count = self.chips
        from_left, from_right = {0: block}, {0: block}
        for step in range(1, count):
            from_left[step] = self.move(from_left[step - 1], range(step - 1, count - 1), 1)
            from_right[step] = self.move(from_right[step - 1], range(1, count - step + 1), -1)
        chunks = [(block, self.partner(block))]
        for position in range(1, count):
            options = {}
            for chip in range(count):
                source = self.order[chip][position]
                key = source - chip
                value = from_left[-key] if key < 0 else from_right[key]
                options.setdefault(key, ([], value))[0].append(chip)
            mine = self.choose(options)
            chunks.append((mine, self.partner(mine)))
        return chunks

    def scatter(self, far, own):
        count = self.chips
        total = own.astype(FULL)
        for side in (1, -1):
            arrived = None
            for step in range(1, count):
                payload = far(step, side)
                if arrived is not None:
                    payload = (payload.astype(FULL) + arrived.astype(FULL)).astype(LOW)
                chips = range(0, step) if side == 1 else range(count - step, count)
                arrived = self.move(payload, chips, side)
            if arrived is not None:
                total = total + arrived.astype(FULL)
        return total

    def scatter_chunks(self, chunks):
        summed = [
            mine.astype(FULL) + self.partner(other).astype(FULL) for mine, other in chunks
        ]
        low = [value.astype(LOW) for value in summed]

        def far(step, side):
            options = {}
            for chip in range(self.chips):
                target = chip + side * (self.chips - step)
                if 0 <= target < self.chips:
                    position = self.order[chip].index(target)
                    options.setdefault(position, ([], low[position]))[0].append(chip)
            return self.choose(options)

        return self.scatter(far, summed[0])

    def scatter_rows(self, rows):
        pairs = rows.reshape(self.chips, 2, *rows.shape[1:])
        mine = lax.dynamic_index_in_dim(pairs, self.core, 1, keepdims=False)
        other = lax.dynamic_index_in_dim(pairs, 1 - self.core, 1, keepdims=False)
        summed = (mine.astype(FULL) + self.partner(other).astype(FULL)).astype(LOW)

        def far(step, side):
            target = jnp.clip(self.chip + side * (self.chips - step), 0, self.chips - 1)
            return lax.dynamic_index_in_dim(summed, target, 0, keepdims=False)

        own = lax.dynamic_index_in_dim(summed, self.chip, 0, keepdims=False)
        return self.scatter(far, own)


def gather_copies(value, shift_back=False):
    count = lax.axis_size("dp")
    return [value] + [
        lax.ppermute(value, "dp", [(i, (i + k) % count) for i in range(count)])
        for k in range(1, count)
    ]


def scatter_copies(blocks):
    count = lax.axis_size("dp")
    total = blocks[0]
    for k in range(1, count):
        sent = blocks[k].astype(LOW)
        total = total + lax.ppermute(
            sent, "dp", [(i, (i - k) % count) for i in range(count)]
        ).astype(FULL)
    return total


def rounded(count, unit=TILE):
    return -(-count // unit) * unit


def gather_kernel(shares, *refs):
    count = len(shares)
    shards, wholes = refs[:count], refs[count : 2 * count]
    local_sem, pair_send, pair_recv = refs[2 * count : 2 * count + 3]
    line_send, line_recv, copy_send, copy_recv, core_send, core_recv = refs[2 * count + 3 :]
    mesh = pl.DeviceIdType.MESH
    copies = lax.axis_size("dp")
    place = lax.axis_index("dp")
    size = lax.axis_size("fsdp")
    chips = size // 2
    me = lax.axis_index("fsdp")
    chip, core = me // 2, me % 2
    partner = 2 * chip + 1 - core
    has_left, has_right = chip > 0, chip < chips - 1

    barrier = pltpu.get_barrier_semaphore()
    pl.semaphore_signal(barrier, inc=1, device_id=(place, partner), device_id_type=mesh)
    for k in range(1, copies):
        peer = lax.rem(place + k, copies)
        pl.semaphore_signal(barrier, inc=1, device_id=(peer, me), device_id_type=mesh)

    @pl.when(has_left)
    def _():
        pl.semaphore_signal(barrier, inc=1, device_id=(place, me - 2), device_id_type=mesh)

    @pl.when(has_right)
    def _():
        pl.semaphore_signal(barrier, inc=1, device_id=(place, me + 2), device_id_type=mesh)

    neighbours = jnp.minimum(chip, 1) + jnp.minimum(chips - 1 - chip, 1)
    pl.semaphore_wait(barrier, copies + neighbours)

    def rows(a, owner, share):
        whole = shards[a].shape[0]
        part = whole // shares[a]
        return pl.ds(pl.multiple_of(owner * whole + share * part, TILE), part)

    def remote(source, target, send, recv, device):
        return pltpu.make_async_remote_copy(
            src_ref=source,
            dst_ref=target,
            send_sem=send,
            recv_sem=recv,
            device_id=device,
            device_id_type=mesh,
        )

    def my_share(a):
        return place if shares[a] > 1 else 0

    def line_copy(a, side, step):
        owner = me - 2 * step if side == 0 else me + 2 * step
        where = rows(a, owner, my_share(a))
        target = me + 2 if side == 0 else me - 2
        return remote(
            wholes[a].at[where],
            wholes[a].at[where],
            line_send.at[a, side, step],
            line_recv.at[a, side, step],
            (place, target),
        )

    def first_copy(a, side):
        part = shards[a].shape[0] // shares[a]
        target = me + 2 if side == 0 else me - 2
        return remote(
            shards[a].at[pl.ds(pl.multiple_of(my_share(a) * part, TILE), part)],
            wholes[a].at[rows(a, me, my_share(a))],
            line_send.at[a, side, 0],
            line_recv.at[a, side, 0],
            (place, target),
        )

    def owner_of(side, step):
        return me - 2 * step if side == 0 else me + 2 * step

    def peer_copy(a, side, step, k):
        where = rows(a, owner_of(side, step), place)
        return remote(
            wholes[a].at[where],
            wholes[a].at[where],
            copy_send.at[a, side, step, k],
            copy_recv.at[a, side, step, k],
            (lax.rem(place + k, copies), me),
        )

    def core_copy(a, side, step, k):
        share = lax.rem(place + copies - k, copies) if shares[a] > 1 else 0
        where = rows(a, owner_of(side, step), share)
        return remote(
            wholes[a].at[where],
            wholes[a].at[where],
            core_send.at[a, side, step, k],
            core_recv.at[a, side, step, k],
            (place, partner),
        )

    def pair_copy(a):
        return remote(
            shards[a],
            wholes[a].at[rows_all(a)],
            pair_send.at[a],
            pair_recv.at[a],
            (place, partner),
        )

    def rows_all(a):
        whole = shards[a].shape[0]
        return pl.ds(pl.multiple_of(me * whole, TILE), whole)

    def local_copy(a):
        return pltpu.make_async_copy(shards[a], wholes[a].at[rows_all(a)], local_sem.at[a])

    def sends(side):
        return has_right if side == 0 else has_left

    def has(side, step):
        return chip >= step if side == 0 else chip + step <= chips - 1

    for a in range(count):
        for side in range(2):

            @pl.when(sends(side))
            def _(a=a, side=side):
                first_copy(a, side).start()

    for a in range(count):
        pair_copy(a).start()
        local_copy(a).start()

    def peers(a):
        return range(1, copies) if shares[a] > 1 else range(0)

    def hand_over(a, side, step):
        for k in peers(a):
            peer_copy(a, side, step, k).wait_recv()
            core_copy(a, side, step, k).start()

    def advance(step, _):
        for a in range(count):
            for side in range(2):

                @pl.when(has(side, step))
                def _(a=a, side=side):
                    line_copy(a, side, step - 1).wait_recv()

                    @pl.when(sends(side))
                    def _():
                        line_copy(a, side, step).start()

                    for k in peers(a):
                        peer_copy(a, side, step, k).start()
                    core_copy(a, side, step, 0).start()

        for a in range(count):
            for side in range(2):

                @pl.when((step > 1) & has(side, step - 1))
                def _(a=a, side=side):
                    hand_over(a, side, step - 1)

        return 0

    lax.fori_loop(1, chips, advance, 0)
    for a in range(count):
        for side in range(2):

            @pl.when(has(side, chips - 1))
            def _(a=a, side=side):
                hand_over(a, side, chips - 1)

    def finish(step, _):
        for a in range(count):
            for side in range(2):

                @pl.when(has(side, step))
                def _(a=a, side=side):
                    @pl.when(sends(side))
                    def _():
                        line_copy(a, side, step).wait_send()

                    for k in peers(a):
                        peer_copy(a, side, step, k).wait_send()
                        core_copy(a, side, step, k).wait_send()
                        core_copy(a, side, step, k).wait_recv()
                    core_copy(a, side, step, 0).wait_send()
                    core_copy(a, side, step, 0).wait_recv()

        return 0

    lax.fori_loop(1, chips, finish, 0)
    for a in range(count):
        for side in range(2):

            @pl.when(sends(side))
            def _(a=a, side=side):
                first_copy(a, side).wait_send()

        pair_copy(a).wait_send()
        pair_copy(a).wait_recv()
        local_copy(a).wait()


def gather_shards(*shards):
    copies, size = lax.axis_size("dp"), lax.axis_size("fsdp")
    chips = size // 2
    shares = [copies if shard.shape[0] % (TILE * copies) == 0 else 1 for shard in shards]
    count = len(shards)
    dma = pltpu.SemaphoreType.DMA
    anywhere = pl.BlockSpec(memory_space=pl.ANY)
    return pl.pallas_call(
        functools.partial(gather_kernel, shares),
        out_shape=[
            jax.ShapeDtypeStruct((size * shard.shape[0], *shard.shape[1:]), shard.dtype)
            for shard in shards
        ],
        in_specs=[anywhere] * count,
        out_specs=[anywhere] * count,
        scratch_shapes=[
            dma((count,)),
            dma((count,)),
            dma((count,)),
            dma((count, 2, chips)),
            dma((count, 2, chips)),
            dma((count, 2, chips, copies)),
            dma((count, 2, chips, copies)),
            dma((count, 2, chips, copies)),
            dma((count, 2, chips, copies)),
        ],
        compiler_params=pltpu.CompilerParams(collective_id=0, has_side_effects=True),
        name="gather_shards",
    )(*shards)


def feed_kernel(
    valid,
    mine_ref,
    other_ref,
    back_mine_ref,
    back_other_ref,
    gate_ref,
    up_ref,
    down_ref,
    *refs,
):
    inner_ref, gate_grad_ref, up_grad_ref, rows_ref, back_ref = refs[-5:]
    root = math.sqrt(2.0 / math.pi)
    for half, (rows, back) in enumerate(((mine_ref, back_mine_ref), (other_ref, back_other_ref))):
        where = slice(half * valid, (half + 1) * valid)
        rows, back = rows[:valid], back[:valid]

        @pl.when(pl.program_id(0) == 0)
        def _():
            rows_ref[where] = rows
            back_ref[where] = back

        gate = multiply(rows, gate_ref[...])
        upper = multiply(rows, up_ref[...])
        inner_grad = multiply_right(back, down_ref[...])
        square = gate * gate
        bent = jnp.tanh(root * gate * (1.0 + 0.044715 * square))
        half_up = 0.5 + 0.5 * bent
        active = gate * half_up
        slope = half_up + (0.5 * root) * gate * (1.0 - bent * bent) * (1.0 + 0.134145 * square)
        inner_ref[where] = (active * upper).astype(LOW)
        gate_grad_ref[where] = (inner_grad * upper * slope).astype(LOW)
        up_grad_ref[where] = (inner_grad * active).astype(LOW)


def feed_chunk(position, chunks, valid, pair, back_pair, gate, up, down, before):
    block, width = pair[0].shape
    hidden = gate.shape[1]
    tile = math.gcd(hidden, 512)
    whole = pl.BlockSpec((block, width), lambda j: (0, 0))
    column = pl.BlockSpec((width, tile), lambda j: (0, j))
    outs = [pl.BlockSpec((2 * valid, tile), lambda j: (position, j))] * 3
    outs += [pl.BlockSpec((2 * valid, width), lambda j: (position, 0))] * 2
    shapes = [jax.ShapeDtypeStruct((chunks * 2 * valid, hidden), LOW)] * 3
    shapes += [jax.ShapeDtypeStruct((chunks * 2 * valid, width), LOW)] * 2
    extra = [] if before is None else list(before)
    return pl.pallas_call(
        functools.partial(feed_kernel, valid),
        out_shape=shapes,
        grid=(hidden // tile,),
        in_specs=[whole] * 4
        + [column, column, pl.BlockSpec((tile, width), lambda j: (j, 0))]
        + [pl.BlockSpec(memory_space=pl.ANY)] * len(extra),
        out_specs=outs,
        input_output_aliases={7 + i: i for i in range(len(extra))},
        compiler_params=pltpu.CompilerParams(vmem_limit_bytes=56 * MIB),
        cost_estimate=pl.CostEstimate(
            flops=12 * valid * width * hidden,
            bytes_accessed=2 * (3 * width * hidden + 10 * valid * width + 6 * valid * hidden),
            transcendentals=2 * valid * hidden,
        ),
        name="feed_chunk",
    )(*pair, *back_pair, gate, up, down, *extra)


def back_kernel(valid, gate_grad_ref, up_grad_ref, gate_ref, up_ref, small_ref, mine_ref, other_ref):
    for half, out in enumerate((mine_ref, other_ref)):
        where = slice(half * valid, (half + 1) * valid)
        part = multiply_right(gate_grad_ref[where], gate_ref[...])
        part = part + multiply_right(up_grad_ref[where], up_ref[...])
        out[:valid] = part.astype(LOW)
        out[valid:] = small_ref[half]


def down_kernel(valid, inner_ref, down_ref, small_ref, mine_ref, other_ref):
    for half, out in enumerate((mine_ref, other_ref)):
        where = slice(half * valid, (half + 1) * valid)
        out[:valid] = multiply(inner_ref[where], down_ref[...]).astype(LOW)
        out[valid:] = small_ref[half]


def part_chunk(kernel, position, valid, grads, weights, weight_block, small, width):
    hidden = grads[0].shape[1]
    tile = math.gcd(width, 512)
    extra = small.shape[1]
    rows = pl.BlockSpec((2 * valid, hidden), lambda j: (position, 0))
    out = pl.BlockSpec((valid + extra, tile), lambda j: (0, j))
    return pl.pallas_call(
        functools.partial(kernel, valid),
        out_shape=[jax.ShapeDtypeStruct((valid + extra, width), LOW)] * 2,
        grid=(width // tile,),
        in_specs=[rows] * len(grads)
        + [weight_block(tile)] * len(weights)
        + [pl.BlockSpec((2, extra, tile), lambda j: (0, 0, j))],
        out_specs=[out] * 2,
        compiler_params=pltpu.CompilerParams(vmem_limit_bytes=48 * MIB),
        cost_estimate=pl.CostEstimate(
            flops=4 * len(grads) * valid * width * hidden,
            bytes_accessed=2 * len(grads) * (width * hidden + 2 * valid * hidden)
            + 4 * valid * width,
            transcendentals=0,
        ),
        name="part_chunk",
    )(*grads, *weights, small)


def stacked(refs, columns=slice(None)):
    return jnp.concatenate([ref[0, :, columns] for ref in refs], axis=0)


def softmax_of(queries, keys, bias, scale):
    scores = multiply_right(queries, keys) * scale + bias
    raised = jnp.exp(scores - jnp.max(scores, axis=-1, keepdims=True))
    return raised / jnp.sum(raised, axis=-1, keepdims=True)


def mix_kernel(scale, head_size, *refs):
    prefix_ref, action_ref, bias_ref = refs[:3]
    prefix_out, action_out = refs[-2:]
    queries = stacked((prefix_ref, action_ref))
    kv = stacked(refs[3:-2])
    probs = softmax_of(queries, kv[:, :head_size], bias_ref[0], scale).astype(LOW)
    mixed = multiply(probs, kv[:, head_size:]).astype(LOW)
    rows = prefix_ref.shape[1]
    prefix_out[0] = mixed[:rows]
    action_out[0] = mixed[rows:]


def mix_back_kernel(scale, head_size, *refs):
    prefix_ref, action_ref, prefix_grad_ref, action_grad_ref, bias_ref = refs[:5]
    prefix_out, action_out, kv_out = refs[-3:]
    queries = stacked((prefix_ref, action_ref))
    grads = stacked((prefix_grad_ref, action_grad_ref))
    kv = stacked(refs[5:-3])
    keys, values = kv[:, :head_size], kv[:, head_size:]
    probs = softmax_of(queries, keys, bias_ref[0], scale)
    probs_grad = multiply_right(grads, values)
    delta = jnp.sum(probs * probs_grad, axis=-1, keepdims=True)
    score_grad = (probs * (probs_grad - delta)).astype(LOW)
    query_grad = (multiply(score_grad, keys) * scale).astype(LOW)
    rows = prefix_ref.shape[1]
    prefix_out[0] = query_grad[:rows]
    action_out[0] = query_grad[rows:]

    @pl.when(pl.program_id(1) == 0)
    def _():
        kv_out[...] = jnp.zeros_like(kv_out)

    kv_out[0, :, :head_size] += multiply_left(score_grad, queries) * scale
    kv_out[0, :, head_size:] += multiply_left(probs.astype(LOW), grads)


def mix_call(backward, scale, head_size, heads, prefix, action, kv_blocks, bias, grads=()):
    items, prefix_rows, _ = prefix.shape
    action_rows = action.shape[1]
    rows = prefix_rows + action_rows
    length = bias.shape[2]
    per_head = [
        pl.BlockSpec((1, prefix_rows, head_size), lambda i, h: (i, 0, h)),
        pl.BlockSpec((1, action_rows, head_size), lambda i, h: (i, 0, h)),
    ]
    in_specs = per_head * (2 if backward else 1)
    in_specs += [pl.BlockSpec((1, rows, length), lambda i, h: (i, 0, 0))]
    in_specs += [pl.BlockSpec((1, rows, 2 * head_size), lambda i, h: (i, 0, 0))] * len(kv_blocks)
    out_specs = list(per_head)
    shapes = [
        jax.ShapeDtypeStruct((items, prefix_rows, heads * head_size), LOW),
        jax.ShapeDtypeStruct((items, action_rows, heads * head_size), LOW),
    ]
    if backward:
        out_specs += [pl.BlockSpec((1, length, 2 * head_size), lambda i, h: (i, 0, 0))]
        shapes += [jax.ShapeDtypeStruct((items, length, 2 * head_size), FULL)]
    kernel = mix_back_kernel if backward else mix_kernel
    dots = 5 if backward else 2
    return pl.pallas_call(
        functools.partial(kernel, scale, head_size),
        out_shape=shapes,
        grid=(items, heads),
        in_specs=in_specs,
        out_specs=out_specs,
        compiler_params=pltpu.CompilerParams(vmem_limit_bytes=48 * MIB),
        cost_estimate=pl.CostEstimate(
            flops=2 * dots * items * heads * rows * length * head_size,
            bytes_accessed=8 * items * rows * heads * head_size,
            transcendentals=items * heads * rows * length,
        ),
        name="mix_back" if backward else "mix",
    )(prefix, action, *grads, bias, *kv_blocks)


def body(
    prefix_in,
    action_in,
    valid_count,
    prefix_before,
    prefix_query,
    prefix_key,
    prefix_value,
    prefix_output,
    prefix_middle,
    prefix_gate,
    prefix_up,
    prefix_down,
    action_before,
    action_query,
    action_key,
    action_value,
    action_output,
    action_middle,
    action_gate,
    action_up,
    action_down,
    prefix_cotangent,
    action_cotangent,
):
    line = Line()
    shards = line.size
    copies = lax.axis_size("dp")
    items, prefix_rows, width = prefix_in.shape
    action_rows = action_in.shape[1]
    action_width = action_in.shape[2]
    head_size = prefix_key.shape[1]
    features = prefix_query.shape[1]
    heads = features // head_size
    columns = features + 2 * head_size
    prefix_length = prefix_rows * copies
    scale = head_size ** (-0.5)
    place = lax.axis_index("dp")
    prefix_pad, action_pad = rounded(prefix_rows), rounded(action_rows)
    prefix_tokens, action_tokens = items * prefix_pad, items * action_pad
    folded = action_tokens * action_width // width
    folded_pad = rounded(folded)

    def padded(prefix, action):
        prefix = jnp.pad(prefix, ((0, 0), (0, prefix_pad - prefix_rows), (0, 0)))
        action = jnp.pad(action, ((0, 0), (0, action_pad - action_rows), (0, 0)))
        return prefix.reshape(prefix_tokens, width), action.reshape(action_tokens, action_width)

    def trimmed(prefix, action):
        prefix = prefix.reshape(items, prefix_pad, width)[:, :prefix_rows]
        return prefix, action.reshape(items, action_pad, action_width)[:, :action_rows]

    def fold(action):
        rows = action.reshape(-1, folded, width)
        return jnp.pad(rows, ((0, 0), (0, folded_pad - folded), (0, 0)))

    def unfold(rows):
        return rows[:folded].reshape(action_tokens, action_width)

    def pack(prefix, action):
        return jnp.concatenate([prefix, fold(action)[0]], axis=0)

    def unpack(packed):
        return packed[:prefix_tokens], unfold(packed[prefix_tokens:])

    share, action_share = prefix_before.shape[0], action_before.shape[0]
    cuts = [0, share, 2 * share, 2 * share + action_share, 2 * share + 2 * action_share]
    gain_rows = rounded(-(-cuts[4] // 128))
    gains = jnp.concatenate([prefix_before, prefix_middle, action_before, action_middle])
    gains = jnp.pad(gains, (0, gain_rows * 128 - cuts[4])).reshape(gain_rows, 128)
    prefix_qkv, action_qkv, prefix_o, action_o, gains = gather_shards(
        jnp.concatenate([prefix_query, prefix_key, prefix_value], axis=1),
        jnp.concatenate([action_query, action_key, action_value], axis=1),
        prefix_output,
        action_output,
        gains,
    )
    gains = gains.reshape(shards, gain_rows * 128).astype(FULL)
    prefix_gain_in, prefix_gain, action_gain_in, action_gain = (
        gains[:, cuts[i] : cuts[i + 1]].reshape(-1) for i in range(4)
    )

    live = (place * action_rows + jnp.arange(action_rows))[None, :] < valid_count[:, None]
    prefix_back, action_back = padded(
        prefix_cotangent,
        jnp.where(live[:, :, None], action_cotangent, jnp.zeros_like(action_cotangent)),
    )
    back_chunks = line.gather(pack(prefix_back, action_back))

    prefix_flat, action_flat = padded(prefix_in.astype(FULL), action_in.astype(FULL))
    prefix_hidden = normalize(prefix_flat, prefix_gain_in).astype(LOW)
    action_hidden = normalize(action_flat, action_gain_in).astype(LOW)
    prefix_all = multiply(prefix_hidden, prefix_qkv).astype(LOW)
    prefix_all = prefix_all.reshape(items, prefix_pad, columns)
    action_all = multiply(action_hidden, action_qkv).astype(LOW)
    action_all = action_all.reshape(items, action_pad, columns)
    kv = jnp.concatenate([prefix_all[:, :, features:], action_all[:, :, features:]], axis=1)
    kv_blocks = gather_copies(kv)

    far = copies * (prefix_rows + action_rows)

    def places(owner):
        prefix = jnp.arange(prefix_pad)
        action = jnp.arange(action_pad)
        return jnp.concatenate(
            [
                jnp.where(prefix < prefix_rows, owner * prefix_rows + prefix, far),
                jnp.where(
                    action < action_rows, prefix_length + owner * action_rows + action, far
                ),
            ]
        )

    query_place = places(place)
    key_place = jnp.concatenate([places((place + copies - k) % copies) for k in range(copies)])
    later = (query_place[:, None] >= prefix_length) & (key_place[None, :] <= query_place[:, None])
    allowed = (key_place[None, None, :] < prefix_length) | later[None] & (
        key_place[None, None, :] < prefix_length + valid_count[:, None, None]
    )
    bias = jnp.where(allowed, 0.0, NEGATIVE).astype(FULL)
    mix = functools.partial(
        mix_call,
        scale=scale,
        head_size=head_size,
        heads=heads,
        prefix=prefix_all,
        action=action_all,
        kv_blocks=kv_blocks,
        bias=bias,
    )
    prefix_mixed, action_mixed = mix(False)
    prefix_mixed = prefix_mixed.reshape(prefix_tokens, features)
    action_mixed = action_mixed.reshape(action_tokens, features)
    prefix_mid = prefix_flat + multiply(prefix_mixed, prefix_o)
    action_mid = action_flat + multiply(action_mixed, action_o)

    hidden_chunks = line.gather(
        pack(
            normalize(prefix_mid, prefix_gain).astype(LOW),
            normalize(action_mid, action_gain).astype(LOW),
        )
    )
    arrays = None
    for position in range(line.chips):
        arrays = feed_chunk(
            position,
            line.chips,
            prefix_tokens,
            hidden_chunks[position],
            back_chunks[position],
            prefix_gate,
            prefix_up,
            prefix_down,
            arrays,
        )
    inner, gate_grad, up_grad, all_rows, all_back = arrays
    action_rows_all, action_back_all = (
        jnp.concatenate([unfold(v[prefix_tokens:]) for pair in chunks for v in pair], axis=0)
        for chunks in (hidden_chunks, back_chunks)
    )
    action_inner, pull = jax.vjp(
        activate, multiply(action_rows_all, action_gate), multiply(action_rows_all, action_up)
    )
    action_inner = action_inner.astype(LOW)
    action_gate_grad, action_up_grad = (
        v.astype(LOW) for v in pull(multiply_right(action_back_all, action_down))
    )

    down_grad = multiply_left(inner, all_back).astype(LOW)
    action_feed = tuple(
        v.astype(LOW)
        for v in (
            multiply_left(action_rows_all, action_gate_grad),
            multiply_left(action_rows_all, action_up_grad),
            multiply_left(action_inner, action_back_all),
        )
    )
    gate_grad, up_grad, down_grad = lax.optimization_barrier((gate_grad, up_grad, down_grad))
    first_sums = lax.psum((down_grad, *action_feed), "dp")

    def halves(rows):
        return fold(rows.astype(LOW)).reshape(line.chips, 2, folded_pad, width)

    small = halves(
        multiply_right(action_gate_grad, action_gate) + multiply_right(action_up_grad, action_up)
    )
    part_of = [
        part_chunk(
            back_kernel,
            i,
            prefix_tokens,
            (gate_grad, up_grad),
            (prefix_gate, prefix_up),
            lambda tile: pl.BlockSpec((tile, gate_grad.shape[1]), lambda j: (j, 0)),
            small[i],
            width,
        )
        for i in range(line.chips)
    ]
    feed_back = unpack(line.scatter_chunks(part_of))

    gate_weight_grad = multiply_left(all_rows, gate_grad).astype(LOW)
    gate_weight_grad, first_done = lax.optimization_barrier((gate_weight_grad, first_sums[0]))
    gate_sum = lax.psum(gate_weight_grad, "dp")
    up_weight_grad = multiply_left(all_rows, up_grad).astype(LOW)
    up_weight_grad, gate_done = lax.optimization_barrier((up_weight_grad, gate_sum))
    up_sum = lax.psum(up_weight_grad, "dp")

    small = halves(multiply(action_inner, action_down))
    part_of = [
        part_chunk(
            down_kernel,
            i,
            prefix_tokens,
            (inner,),
            (prefix_down,),
            lambda tile: pl.BlockSpec((inner.shape[1], tile), lambda j: (0, j)),
            small[i],
            width,
        )
        for i in range(line.chips)
    ]
    sums = unpack(line.scatter_chunks(part_of))
    prefix_out, action_out = trimmed(
        (prefix_mid + sums[0]).astype(LOW), (action_mid + sums[1]).astype(LOW)
    )

    _, pull = jax.vjp(normalize, prefix_mid, prefix_gain)
    prefix_inner_grad, prefix_middle_part = pull(feed_back[0])
    _, pull = jax.vjp(normalize, action_mid, action_gain)
    action_inner_grad, action_middle_part = pull(feed_back[1])
    prefix_mid_grad = prefix_back.astype(FULL) + prefix_inner_grad
    action_mid_grad = action_back.astype(FULL) + action_inner_grad
    prefix_low = prefix_mid_grad.astype(LOW)
    action_low = action_mid_grad.astype(LOW)
    output_part = multiply_left(prefix_mixed, prefix_low).astype(LOW)
    output_owned = line.scatter_rows(output_part.reshape(shards, features // shards, width))
    mixed_grads = (
        multiply_right(prefix_low, prefix_o).astype(LOW).reshape(items, prefix_pad, features),
        multiply_right(action_low, action_o).astype(LOW).reshape(items, action_pad, features),
    )
    prefix_query_grad, action_query_grad, kv_grad = mix(True, grads=mixed_grads)
    step = prefix_pad + action_pad
    kv_grad = scatter_copies([kv_grad[:, k * step : (k + 1) * step] for k in range(copies)])
    kv_grad = kv_grad.astype(LOW)
    prefix_qkv_grad = jnp.concatenate([prefix_query_grad, kv_grad[:, :prefix_pad]], axis=2)
    action_qkv_grad = jnp.concatenate([action_query_grad, kv_grad[:, prefix_pad:]], axis=2)
    prefix_qkv_grad = prefix_qkv_grad.reshape(prefix_tokens, columns)
    action_qkv_grad = action_qkv_grad.reshape(action_tokens, columns)
    prefix_hidden_grad = multiply_right(prefix_qkv_grad, prefix_qkv)
    action_hidden_grad = multiply_right(action_qkv_grad, action_qkv)
    _, pull = jax.vjp(normalize, prefix_flat, prefix_gain_in)
    prefix_entry_grad, prefix_before_part = pull(prefix_hidden_grad)
    _, pull = jax.vjp(normalize, action_flat, action_gain_in)
    action_entry_grad, action_before_part = pull(action_hidden_grad)
    prefix_grad, action_grad = trimmed(
        prefix_mid_grad + prefix_entry_grad, action_mid_grad + action_entry_grad
    )

    gain_parts = jnp.concatenate(
        [
            part.reshape(shards, -1)
            for part in (
                prefix_before_part,
                prefix_middle_part,
                action_before_part,
                action_middle_part,
            )
        ],
        axis=1,
    )
    gain_rows = rounded(-(-cuts[4] // columns))
    gain_parts = jnp.pad(gain_parts, ((0, 0), (0, gain_rows * columns - cuts[4])))
    qkv_part = multiply_left(prefix_hidden, prefix_qkv_grad).astype(LOW)
    qkv_owned = line.scatter_rows(
        jnp.concatenate(
            [
                qkv_part.reshape(shards, width // shards, columns),
                gain_parts.astype(LOW).reshape(shards, gain_rows, columns),
            ],
            axis=1,
        )
    )
    tokens_all = jnp.concatenate([action_hidden, action_mixed, action_low, action_qkv_grad], axis=1)
    tokens_all = lax.all_gather(tokens_all, "fsdp", axis=0, tiled=True)
    edges = [0]
    for part in (action_width, features, action_width, columns):
        edges.append(edges[-1] + part)
    rows = action_query.shape[0]
    hidden_slice = lax.dynamic_slice_in_dim(tokens_all[:, : edges[1]], line.place * rows, rows, 1)
    action_qkv_owned = multiply_left(hidden_slice, tokens_all[:, edges[3] :])
    rows = action_output.shape[0]
    mixed_slice = lax.dynamic_slice_in_dim(
        tokens_all[:, edges[1] : edges[2]], line.place * rows, rows, 1
    )
    action_output_owned = multiply_left(mixed_slice, tokens_all[:, edges[2] : edges[3]])

    owned = tuple(
        v.astype(LOW) for v in (qkv_owned, output_owned, action_qkv_owned, action_output_owned)
    )
    owned, up_done = lax.optimization_barrier((owned, up_sum))
    qkv_owned, output_owned, action_qkv_owned, action_output_owned = (
        v.astype(FULL) for v in lax.psum(owned, "dp")
    )
    rows = prefix_query.shape[0]
    gain_owned = qkv_owned[rows:].reshape(-1)
    return (
        prefix_out,
        action_out,
        prefix_grad,
        action_grad,
        gain_owned[cuts[0] : cuts[1]],
        qkv_owned[:rows, :features],
        qkv_owned[:rows, features : features + head_size],
        qkv_owned[:rows, features + head_size :],
        output_owned,
        gain_owned[cuts[1] : cuts[2]],
        gate_done.astype(FULL),
        up_done.astype(FULL),
        first_done.astype(FULL),
        gain_owned[cuts[2] : cuts[3]],
        action_qkv_owned[:, :features],
        action_qkv_owned[:, features : features + head_size],
        action_qkv_owned[:, features + head_size :],
        action_output_owned,
        gain_owned[cuts[3] : cuts[4]],
        *(v.astype(FULL) for v in first_sums[1:]),
    )


def solution(mesh):
    tokens = P("fsdp", "dp", None)
    rows, columns, vector = P("fsdp", None), P(None, "fsdp"), P("fsdp")
    weights = (vector, rows, rows, rows, rows, vector, columns, columns, rows)
    return jax.shard_map(
        body,
        mesh=mesh,
        in_specs=(tokens, tokens, vector, *weights, *weights, tokens, tokens),
        out_specs=(tokens, tokens, tokens, tokens, *weights, *weights),
        check_vma=False,
    )
```

time: 2310 us -> 1610 us (0.70)
  waiting for transfers between devices: 1470 us -> 558 us
  Pallas kernels: 0 us -> 434 us
  matrix products: 468 us -> 186 us
  blocking collectives: 186 us -> 0 us
  starting transfers between devices: 2 us -> 121 us
  other arithmetic: 91.3 us -> 182 us
  local copies, waits for them, and re-layouts: 66.1 us -> 108 us
    reduce_scatter x12 -> x0, waiting for transfers between devices: 608 us -> none  [the longest x1 219 us: body(): lax.psum_scatter(feed_prefix[0], 'fsdp', scatter_dimension=0, tiled=True)]
    pallas_call x0 -> x15, Pallas kernels: none -> 434 us  [the longest x1 136 us: gather_shards(): pl.pallas_call(functools.partial(gather_kernel, shares), out_shape=[jax.S...]
    ppermute x0 -> x60, waiting for transfers between devices: none -> 308 us  [the longest x36 296 us: move(): return lax.ppermute(value, 'fsdp', pairs)]
    all_gather x8 -> x1, waiting for transfers between devices: 271 us -> 0.01 us  [body(): tokens_all = lax.all_gather(tokens_all, 'fsdp', axis=0, tiled=True)]
    psum x1 -> x4, waiting for transfers between devices: 494 us -> 250 us  [the longest x1 105 us: body(): lax.psum(owned, 'dp')]
    all_gather x12 -> x0, blocking collectives: 149 us -> none  [the longest x1 17.3 us: body(): lax.all_gather(action_back, 'fsdp', axis=0, tiled=True)]
    dot_general x14 -> x7, matrix products: 163 us -> 25.4 us  [multiply_right(): lax.dot_general(left, right, (((1,), (1,)), ((), ())), preferred_element_...]
    dot_general x20 -> x7, matrix products: 162 us -> 24.1 us  [multiply(): return jnp.dot(left, right, preferred_element_type=FULL)]
  transfers between devices with their start and end apart: 23 -> 65, of which waited for: 14 -> 23; matrix products, arithmetic and copies ran while one was open for 23% -> 22% of each run, Pallas kernels for 0% -> 15%
where the time goes in v1:
time: 1610 us
  waiting for transfers between devices  558 us (35%)
  Pallas kernels  434 us (27%)
  matrix products  186 us (12%)
  other arithmetic  182 us (11%)
  starting transfers between devices  121 us (8%)
  local copies, waits for them, and re-layouts  108 us (7%)
  between operations  17.7 us (1%)
    ppermute x36, waiting for transfers between devices, move(): return lax.ppermute(value, 'fsdp', pairs)  296 us
    dot_general x10, matrix products, multiply_left(): lax.dot_general(left, right, (((0,), (0,)), ((), ())), preferred_element_...  137 us
    pallas_call x1, Pallas kernels, gather_shards(): pl.pallas_call(functools.partial(gather_kernel, shares), out_shape=[jax.S...  136 us
    pallas_call x4, Pallas kernels, feed_chunk(): pl.pallas_call(functools.partial(feed_kernel, valid), out_shape=shapes, g...  132 us
    pallas_call x8, Pallas kernels, part_chunk(): pl.pallas_call(functools.partial(kernel, valid), out_shape=[jax.ShapeDtyp...  123 us
    ppermute x36, starting transfers between devices, move(): return lax.ppermute(value, 'fsdp', pairs)  109 us
    psum x1, waiting for transfers between devices, body(): lax.psum(owned, 'dp')  105 us
    psum x1, waiting for transfers between devices, body(): gate_sum = lax.psum(gate_weight_grad, 'dp')  77.5 us
  transfers between devices with their start and end apart: 65, of which 23 were waited for; matrix products, arithmetic and copies ran while one was open for 22% of the time, Pallas kernels for 15%

profile of v1, /device:TPU:0, one launch (start us, length us, event | category | flops | bytes accessed | tf_op | source)
XLA Modules:
  0.0 1607.8 jit_solution(1521478959083087085)
XLA Ops:
  18.3 136.0 %gather_shards.1 = (bf16[2048,2560]{1,0:T(8,128)(2,1)}, bf16[1024,2560]{1,0:T(8,128)(2,1)}, bf16[2048,2048]{1,0:T(8,128)(2,1)}, bf16[2048,1024]{1,0:T(8,128)(2,1)}, bf16[128,128]{1,0:T(8,128)(2,1)}) custom-call(bf16[256,2560]{1,0:T(8,128)(2,1)} %pad_maximum_fusion.3.refs_0_, bf16[128,2560]{1,0:T(8,128)(2,1)} %pad_maximum_fusion.4.refs_1_, ...), custom_call_target="tpu_custom_call" | custom-call | tf_op jit(solution)/shard_map/gather_shards/pallas_call | solution.py:374
  239.5 34.2 %collective-permute-done.5 = bf16[432,2048]{1,0:T(8,128)(2,1)S(1)} collective-permute-done((bf16[432,2048]{1,0:T(8,128)(2,1)S(1)}, bf16[432,2048]{1,0:T(8,128)(2,1)S(1)}, u32[]{:S(2)}, u32[]{:S(2)}) %collective-permute-start.5) | collective-permute-done | bytes 1769504 | tf_op jit(solution)/shard_map/ppermute | solution.py:65
  278.1 33.5 %collective-permute-done.13 = bf16[432,2048]{1,0:T(8,128)(2,1)S(1)} collective-permute-done((bf16[432,2048]{1,0:T(8,128)(2,1)}, bf16[432,2048]{1,0:T(8,128)(2,1)S(1)}, u32[]{:S(2)}, u32[]{:S(2)}) %collective-permute-start.13) | collective-permute-done | bytes 1769504 | tf_op jit(solution)/shard_map/ppermute | solution.py:65
  314.8 34.8 %collective-permute-done.6 = bf16[432,2048]{1,0:T(8,128)(2,1)} collective-permute-done((bf16[432,2048]{1,0:T(8,128)(2,1)S(1)}, bf16[432,2048]{1,0:T(8,128)(2,1)}, u32[]{:S(2)}, u32[]{:S(2)}) %collective-permute-start.6) | collective-permute-done | bytes 1769504 | tf_op jit(solution)/shard_map/ppermute | solution.py:65
  355.7 31.8 %collective-permute-done.14 = bf16[432,2048]{1,0:T(8,128)(2,1)} collective-permute-done((bf16[432,2048]{1,0:T(8,128)(2,1)S(1)}, bf16[432,2048]{1,0:T(8,128)(2,1)}, u32[]{:S(2)}, u32[]{:S(2)}) %collective-permute-start.14) | collective-permute-done | bytes 1769504 | tf_op jit(solution)/shard_map/ppermute | solution.py:65
  393.4 31.1 %collective-permute-done.7 = bf16[432,2048]{1,0:T(8,128)(2,1)} collective-permute-done((bf16[432,2048]{1,0:T(8,128)(2,1)}, bf16[432,2048]{1,0:T(8,128)(2,1)}, u32[]{:S(2)}, u32[]{:S(2)}) %collective-permute-start.7) | collective-permute-done | bytes 1769504 | tf_op jit(solution)/shard_map/ppermute | solution.py:65
  430.3 33.0 %feed_chunk.4 = (bf16[3328,2048]{1,0:T(8,128)(2,1)}, bf16[3328,2048]{1,0:T(8,128)(2,1)}, bf16[3328,2048]{1,0:T(8,128)(2,1)}, bf16[3328,2048]{1,0:T(8,128)(2,1)}, bf16[3328,2048]{1,0:T(8,128)(2,1)}) custom-call(bf16[432,2048]{1,0:T(8,128)(2,1)} %copy-done.72, bf16[432,2048]{1,0:T(8,128)(2,1)} %collective-permute-done.21.other_ref, ...), custom_call_target="tpu_custom_call" | custom-call | flops 20937965568 | bytes 52428800 | tf_op jit(solution)/shard_map/feed_chunk/pallas_call | solution.py:444
  488.8 32.8 %feed_chunk.5 = (bf16[3328,2048]{1,0:T(8,128)(2,1)}, bf16[3328,2048]{1,0:T(8,128)(2,1)}, bf16[3328,2048]{1,0:T(8,128)(2,1)}, bf16[3328,2048]{1,0:T(8,128)(2,1)}, bf16[3328,2048]{1,0:T(8,128)(2,1)}) custom-call(bf16[432,2048]{1,0:T(8,128)(2,1)} %get-tuple-element.183.mine_ref, ...), custom_call_target="tpu_custom_call", output_to_operand_aliasing={{0}: (7, {}), {1}: (8, {}), {2}: (9, {}), {3}: (10, {}), {4... | custom-call | flops 20937965568 | bytes 52428800 | tf_op jit(solution)/shard_map/feed_chunk/pallas_call | solution.py:444
  521.6 33.1 %feed_chunk.6 = (bf16[3328,2048]{1,0:T(8,128)(2,1)}, bf16[3328,2048]{1,0:T(8,128)(2,1)}, bf16[3328,2048]{1,0:T(8,128)(2,1)}, bf16[3328,2048]{1,0:T(8,128)(2,1)}, bf16[3328,2048]{1,0:T(8,128)(2,1)}) custom-call(bf16[432,2048]{1,0:T(8,128)(2,1)} %get-tuple-element.175.mine_ref, ...), custom_call_target="tpu_custom_call", output_to_operand_aliasing={{0}: (7, {}), {1}: (8, {}), {2}: (9, {}), {3}: (10, {}), {4... | custom-call | flops 20937965568 | bytes 52428800 | tf_op jit(solution)/shard_map/feed_chunk/pallas_call | solution.py:444
  554.7 32.8 %feed_chunk.7 = (bf16[3328,2048]{1,0:T(8,128)(2,1)}, bf16[3328,2048]{1,0:T(8,128)(2,1)}, bf16[3328,2048]{1,0:T(8,128)(2,1)}, bf16[3328,2048]{1,0:T(8,128)(2,1)}, bf16[3328,2048]{1,0:T(8,128)(2,1)}) custom-call(bf16[432,2048]{1,0:T(8,128)(2,1)} %get-tuple-element.176.mine_ref, ...), custom_call_target="tpu_custom_call", output_to_operand_aliasing={{0}: (7, {}), {1}: (8, {}), {2}: (9, {}), {3}: (10, {}), {4... | custom-call | flops 20937965568 | bytes 52428800 | tf_op jit(solution)/shard_map/feed_chunk/pallas_call | solution.py:444
  587.5 37.0 %convolution_convert_fusion.3 = bf16[2048,2048]{1,0:T(8,128)(2,1)} fusion(bf16[3328,2048]{1,0:T(8,128)(2,1)} %get-tuple-element.102.inner_ref, bf16[3328,2048]{1,0:T(8,128)(2,1)} %get-tuple-element.113), kind=kOutput, calls=%fused_computation.12 | convolution fusion | flops 27921481728 | bytes 35651584 | tf_op jit(solution)/shard_map/dot_general | solution.py:28
  631.8 20.2 %part_chunk.15 = (bf16[432,2048]{1,0:T(8,128)(2,1)S(1)}, bf16[432,2048]{1,0:T(8,128)(2,1)}) custom-call(bf16[3328,2048]{1,0:T(8,128)(2,1)} %get-tuple-element.114.gate_grad_ref, bf16[3328,2048]{1,0:T(8,128)(2,1)} %get-tuple-element.115.up_grad_ref, bf16[2048,2048]{1,0:T(8,128)(2,1)} %gate_ref.15, bf16[2048,2048]{1,0:T(8,128)(2,1)} %up_ref.15, ...), custom_call_target="tpu_custom_call" | custom-call | flops 13958643712 | bytes 27000832 | tf_op jit(solution)/shard_map/part_chunk/pallas_call | solution.py:485
  666.2 19.5 %part_chunk.14 = (bf16[432,2048]{1,0:T(8,128)(2,1)S(1)}, bf16[432,2048]{1,0:T(8,128)(2,1)S(1)}) custom-call(bf16[3328,2048]{1,0:T(8,128)(2,1)} %get-tuple-element.114.gate_grad_ref, bf16[3328,2048]{1,0:T(8,128)(2,1)} %get-tuple-element.115.up_grad_ref, bf16[2048,2048]{1,0:T(8,128)(2,1)} %gate_ref.15, bf16[2048,2048]{1,0:T(8,128)(2,1)} %up_ref.15, ...), custom_call_target="tpu_custom_call" | custom-call | flops 13958643712 | bytes 27000832 | tf_op jit(solution)/shard_map/part_chunk/pallas_call | solution.py:485
  717.3 19.6 %part_chunk.13 = (bf16[432,2048]{1,0:T(8,128)(2,1)S(1)}, bf16[432,2048]{1,0:T(8,128)(2,1)S(1)}) custom-call(bf16[3328,2048]{1,0:T(8,128)(2,1)} %get-tuple-element.114.gate_grad_ref, bf16[3328,2048]{1,0:T(8,128)(2,1)} %get-tuple-element.115.up_grad_ref, bf16[2048,2048]{1,0:T(8,128)(2,1)} %gate_ref.15, bf16[2048,2048]{1,0:T(8,128)(2,1)} %up_ref.15, ...), custom_call_target="tpu_custom_call" | custom-call | flops 13958643712 | bytes 27000832 | tf_op jit(solution)/shard_map/part_chunk/pallas_call | solution.py:485
  799.3 19.7 %part_chunk.12 = (bf16[432,2048]{1,0:T(8,128)(2,1)S(1)}, bf16[432,2048]{1,0:T(8,128)(2,1)S(1)}) custom-call(bf16[3328,2048]{1,0:T(8,128)(2,1)} %get-tuple-element.114.gate_grad_ref, bf16[3328,2048]{1,0:T(8,128)(2,1)} %get-tuple-element.115.up_grad_ref, bf16[2048,2048]{1,0:T(8,128)(2,1)} %gate_ref.15, bf16[2048,2048]{1,0:T(8,128)(2,1)} %up_ref.15, ...), custom_call_target="tpu_custom_call" | custom-call | flops 13958643712 | bytes 27000832 | tf_op jit(solution)/shard_map/part_chunk/pallas_call | solution.py:485
  909.4 25.3 %collective-permute-done.29 = bf16[432,2048]{1,0:T(8,128)(2,1)} collective-permute-done((bf16[432,2048]{1,0:T(8,128)(2,1)}, bf16[432,2048]{1,0:T(8,128)(2,1)}, u32[]{:S(2)}, u32[]{:S(2)}) %collective-permute-start.29) | collective-permute-done | bytes 1769504 | tf_op jit(solution)/shard_map/ppermute | solution.py:65
  952.8 27.5 %mix_back.1 = (bf16[2,208,2048]{2,1,0:T(8,128)(2,1)S(1)}, bf16[2,16,2048]{2,1,0:T(8,128)(2,1)S(1)}, f32[2,896,512]{2,1,0:T(8,128)}) custom-call(bf16[2,208,2560]{2,1,0:T(8,128)(2,1)} %bitcast.192, bf16[2,16,2560]{2,1,0:T(8,128)(2,1)S(1)} %bitcast.163, bf16[2,208,2048]{2,1,0:T(8,128)(2,1)} %bitcast.201, bf16[2,16,2048]{2,1,0:T(8,128)(2,1)S(1)} %bitcast.164, ...), custom_call_target="tpu_custom_call" | custom-call | flops 8220835840 | bytes 7340032 | tf_op jit(solution)/shard_map/mix_back/pallas_call | solution.py:572
  987.5 36.7 %convolution_convert_fusion.1 = bf16[2048,2048]{1,0:T(8,128)(2,1)} fusion(bf16[3328,2048]{1,0:T(8,128)(2,1)} %get-tuple-element.127, bf16[3328,2048]{1,0:T(8,128)(2,1)} %get-tuple-element.114.gate_grad_ref), kind=kOutput, calls=%fused_computation.10 | convolution fusion | flops 27921481728 | bytes 35651584 | tf_op jit(solution)/shard_map/dot_general | solution.py:28
  1045.7 28.7 %all-reduce.12.cloned.1.call-done = bf16[2048,2048]{1,0:T(8,128)(2,1)} async-done(((bf16[2048,2048]{1,0:T(8,128)(2,1)}), bf16[2048,2048]{1,0:T(8,128)(2,1)}) %all-reduce.12.cloned.1.call-update) | async-done | bytes 8388624 | tf_op jit(solution)/shard_map/psum | solution.py:766
  1136.3 37.3 %convolution_convert_fusion.2 = bf16[2048,2048]{1,0:T(8,128)(2,1)} fusion(bf16[3328,2048]{1,0:T(8,128)(2,1)} %get-tuple-element.127, bf16[3328,2048]{1,0:T(8,128)(2,1)} %get-tuple-element.115.up_grad_ref), kind=kOutput, calls=%fused_computation.11 | convolution fusion | flops 27921481728 | bytes 35651584 | tf_op jit(solution)/shard_map/dot_general | solution.py:28
  1173.6 77.5 %all-reduce.14.cloned.1.call-done = bf16[2048,2048]{1,0:T(8,128)(2,1)} async-done(((bf16[2048,2048]{1,0:T(8,128)(2,1)}), bf16[2048,2048]{1,0:T(8,128)(2,1)}) %all-reduce.14.cloned.1.call-update) | async-done | bytes 8388624 | tf_op jit(solution)/shard_map/psum | solution.py:791
  1289.5 22.1 %collective-permute-done.48 = bf16[272,2560]{1,0:T(8,128)(2,1)} collective-permute-done((bf16[272,2560]{1,0:T(8,128)(2,1)S(1)}, bf16[272,2560]{1,0:T(8,128)(2,1)}, u32[]{:S(2)}, u32[]{:S(2)}) %collective-permute-start.48) | collective-permute-done | bytes 1392672 | tf_op jit(solution)/shard_map/ppermute | solution.py:65
  1389.5 38.6 %all-reduce.16.cloned.1.call-done = bf16[2048,2048]{1,0:T(8,128)(2,1)} async-done(((bf16[2048,2048]{1,0:T(8,128)(2,1)}), bf16[2048,2048]{1,0:T(8,128)(2,1)}) %all-reduce.16.cloned.1.call-update) | async-done | bytes 8388624 | tf_op jit(solution)/shard_map/psum | solution.py:794
  1479.7 104.7 %all-reduce.18.cloned.1.call-done = (bf16[272,2560]{1,0:T(8,128)(2,1)}, bf16[256,2048]{1,0:T(8,128)(2,1)}, bf16[128,2560]{1,0:T(8,128)(2,1)}, bf16[256,1024]{1,0...) async-done(((bf16[272,2560]{1,0:T(8,128)(2,1)}, bf16[256,2048]{1,0:T(8,128)(2,1)}, bf16[128,2560]{1,0:T(8,128)(2,1)}, ...) | async-done | bytes 6766608 | tf_op jit(solution)/shard_map/psum | solution.py:890
  (619 shorter events, 642.8 us)
Async XLA Ops:
  8.1 1066.3 %all-reduce.12.cloned.1.call-start = ((), (), s32[]{:S(2)}) async-start(), calls=%async_computation.1 | async-start | bytes 16777216 | tf_op jit(solution)/shard_map/psum | solution.py:766
  236.3 75.3 %collective-permute-start.13 = (bf16[432,2048]{1,0:T(8,128)(2,1)}, bf16[432,2048]{1,0:T(8,128)(2,1)S(1)}, u32[]{:S(2)}, u32[]{:S(2)}) collective-permute-start(bf16[432,2048]{1,0:T(8,128)(2,1)} %collective-permute-done.12), channel_id=1, source_target_pairs={{2,0},{3,1},{4,2},{5,3},{10,8},{11,9},{12,10},{13,11},{18,16},{19,... | collective-permute-start | bytes 5308424 | tf_op jit(solution)/shard_map/ppermute | solution.py:65
  237.6 75.3 %collective-permute-start.11 = (bf16[432,2048]{1,0:T(8,128)(2,1)}, bf16[432,2048]{1,0:T(8,128)(2,1)}, u32[]{:S(2)}, u32[]{:S(2)}) collective-permute-start(bf16[432,2048]{1,0:T(8,128)(2,1)} %collective-permute-done.10), channel_id=1, source_target_pairs={{2,4},{3,5},{4,6},{5,7},{10,12},{11,13},{12,14},{13,15},{18,20},{1... | collective-permute-start | bytes 5308424 | tf_op jit(solution)/shard_map/ppermute | solution.py:65
  274.8 74.7 %collective-permute-start.6 = (bf16[432,2048]{1,0:T(8,128)(2,1)S(1)}, bf16[432,2048]{1,0:T(8,128)(2,1)}, u32[]{:S(2)}, u32[]{:S(2)}) collective-permute-start(bf16[432,2048]{1,0:T(8,128)(2,1)S(1)} %collective-permute-done.5), channel_id=1, source_target_pairs={{2,0},{3,1},{4,2},{5,3},{10,8},{11,9},{12,10},{13,11},{18,16},{19,... | collective-permute-start | bytes 5308424 | tf_op jit(solution)/shard_map/ppermute | solution.py:65
  276.2 74.7 %collective-permute-start.4 = (bf16[432,2048]{1,0:T(8,128)(2,1)S(1)}, bf16[432,2048]{1,0:T(8,128)(2,1)}, u32[]{:S(2)}, u32[]{:S(2)}) collective-permute-start(bf16[432,2048]{1,0:T(8,128)(2,1)S(1)} %collective-permute-done.3), channel_id=1, source_target_pairs={{2,4},{3,5},{4,6},{5,7},{10,12},{11,13},{12,14},{13,15},{18,20},{1... | collective-permute-start | bytes 5308424 | tf_op jit(solution)/shard_map/ppermute | solution.py:65
  278.1 76.1 %collective-permute-start.22 = (bf16[432,2048]{1,0:T(8,128)(2,1)}, bf16[432,2048]{1,0:T(8,128)(2,1)}, u32[]{:S(2)}, u32[]{:S(2)}) collective-permute-start(bf16[432,2048]{1,0:T(8,128)(2,1)} %pad_maximum_fusion.2.back_mine_ref), channel_id=1, source_target_pairs={{0,1},{1,0},{2,3},{3,2},{4,5},{5,4},{6,7},{7,6},{8,9},{9,8},{10,11... | collective-permute-start | bytes 5308424 | tf_op jit(solution)/shard_map/ppermute | solution.py:68
  311.6 75.9 %collective-permute-start.14 = (bf16[432,2048]{1,0:T(8,128)(2,1)S(1)}, bf16[432,2048]{1,0:T(8,128)(2,1)}, u32[]{:S(2)}, u32[]{:S(2)}) collective-permute-start(bf16[432,2048]{1,0:T(8,128)(2,1)S(1)} %collective-permute-done.13), channel_id=1, source_target_pairs={{2,0},{3,1},{10,8},{11,9},{18,16},{19,17},{26,24},{27,25}} | collective-permute-start | bytes 5308424 | tf_op jit(solution)/shard_map/ppermute | solution.py:65
  312.9 74.6 %collective-permute-start.15 = (bf16[432,2048]{1,0:T(8,128)(2,1)}, bf16[432,2048]{1,0:T(8,128)(2,1)}, u32[]{:S(2)}, u32[]{:S(2)}) collective-permute-start(bf16[432,2048]{1,0:T(8,128)(2,1)} %collective-permute-done.11), channel_id=1, source_target_pairs={{4,6},{5,7},{12,14},{13,15},{20,22},{21,23},{28,30},{29,31}} | collective-permute-start | bytes 5308424 | tf_op jit(solution)/shard_map/ppermute | solution.py:65
  349.6 75.0 %collective-permute-start.7 = (bf16[432,2048]{1,0:T(8,128)(2,1)}, bf16[432,2048]{1,0:T(8,128)(2,1)}, u32[]{:S(2)}, u32[]{:S(2)}) collective-permute-start(bf16[432,2048]{1,0:T(8,128)(2,1)} %collective-permute-done.6), channel_id=1, source_target_pairs={{2,0},{3,1},{10,8},{11,9},{18,16},{19,17},{26,24},{27,25}} | collective-permute-start | bytes 5308424 | tf_op jit(solution)/shard_map/ppermute | solution.py:65
  350.9 73.6 %collective-permute-start.8 = (bf16[432,2048]{1,0:T(8,128)(2,1)}, bf16[432,2048]{1,0:T(8,128)(2,1)}, u32[]{:S(2)}, u32[]{:S(2)}) collective-permute-start(bf16[432,2048]{1,0:T(8,128)(2,1)} %collective-permute-done.4), channel_id=1, source_target_pairs={{4,6},{5,7},{12,14},{13,15},{20,22},{21,23},{28,30},{29,31}} | collective-permute-start | bytes 5308424 | tf_op jit(solution)/shard_map/ppermute | solution.py:65
  354.2 76.1 %collective-permute-start.21 = (bf16[432,2048]{1,0:T(8,128)(2,1)}, bf16[432,2048]{1,0:T(8,128)(2,1)}, u32[]{:S(2)}, u32[]{:S(2)}) collective-permute-start(bf16[432,2048]{1,0:T(8,128)(2,1)} %copy-done.72), channel_id=1, source_target_pairs={{0,1},{1,0},{2,3},{3,2},{4,5},{5,4},{6,7},{7,6},{8,9},{9,8},{10,11... | collective-permute-start | bytes 5308424 | tf_op jit(solution)/shard_map/ppermute | solution.py:68
  392.9 82.9 %collective-permute-start.20 = (bf16[432,2048]{1,0:T(8,128)(2,1)}, bf16[432,2048]{1,0:T(8,128)(2,1)}, u32[]{:S(2)}, u32[]{:S(2)}) collective-permute-start(bf16[432,2048]{1,0:T(8,128)(2,1)} %get-tuple-element.182.back_mine_ref), channel_id=1, source_target_pairs={{0,1},{1,0},{2,3},{3,2},{4,5},{5,4},{6,7},{7,6},{8,9},{9,8},{10,11... | collective-permute-start | bytes 5308424 | tf_op jit(solution)/shard_map/ppermute | solution.py:68
  392.9 86.3 %collective-permute-start.18 = (bf16[432,2048]{1,0:T(8,128)(2,1)}, bf16[432,2048]{1,0:T(8,128)(2,1)}, u32[]{:S(2)}, u32[]{:S(2)}) collective-permute-start(bf16[432,2048]{1,0:T(8,128)(2,1)} %get-tuple-element.173.back_mine_ref), channel_id=1, source_target_pairs={{0,1},{1,0},{2,3},{3,2},{4,5},{5,4},{6,7},{7,6},{8,9},{9,8},{10,11... | collective-permute-start | bytes 5308424 | tf_op jit(solution)/shard_map/ppermute | solution.py:68
  475.8 78.9 %collective-permute-start.9 = (bf16[432,2048]{1,0:T(8,128)(2,1)}, bf16[432,2048]{1,0:T(8,128)(2,1)}, u32[]{:S(2)}, u32[]{:S(2)}) collective-permute-start(bf16[432,2048]{1,0:T(8,128)(2,1)} %get-tuple-element.176.mine_ref), channel_id=1, source_target_pairs={{0,1},{1,0},{2,3},{3,2},{4,5},{5,4},{6,7},{7,6},{8,9},{9,8},{10,11... | collective-permute-start | bytes 5308424 | tf_op jit(solution)/shard_map/ppermute | solution.py:68
  712.8 70.5 %collective-permute-start.27 = (bf16[432,2048]{1,0:T(8,128)(2,1)}, bf16[432,2048]{1,0:T(8,128)(2,1)}, u32[]{:S(2)}, u32[]{:S(2)}) collective-permute-start(bf16[432,2048]{1,0:T(8,128)(2,1)} %add_convert_fusion.11), channel_id=1, source_target_pairs={{0,2},{1,3},{8,10},{9,11},{16,18},{17,19},{24,26},{25,27}} | collective-permute-start | bytes 5308424 | tf_op jit(solution)/shard_map/ppermute | solution.py:65
  715.4 69.8 %collective-permute-start.30 = (bf16[432,2048]{1,0:T(8,128)(2,1)}, bf16[432,2048]{1,0:T(8,128)(2,1)}, u32[]{:S(2)}, u32[]{:S(2)}) collective-permute-start(bf16[432,2048]{1,0:T(8,128)(2,1)} %add_convert_fusion.11), channel_id=1, source_target_pairs={{6,4},{7,5},{14,12},{15,13},{22,20},{23,21},{30,28},{31,29}} | collective-permute-start | bytes 5308424 | tf_op jit(solution)/shard_map/ppermute | solution.py:65
  761.0 79.7 %collective-permute-start.24 = (bf16[432,2048]{1,0:T(8,128)(2,1)}, bf16[432,2048]{1,0:T(8,128)(2,1)}, u32[]{:S(2)}, u32[]{:S(2)}) collective-permute-start(bf16[432,2048]{1,0:T(8,128)(2,1)} %copy-done.24), channel_id=1, source_target_pairs={{0,1},{1,0},{2,3},{3,2},{4,5},{5,4},{6,7},{7,6},{8,9},{9,8},{10,11... | collective-permute-start | bytes 5308424 | tf_op jit(solution)/shard_map/ppermute | solution.py:68
  866.8 67.9 %collective-permute-start.29 = (bf16[432,2048]{1,0:T(8,128)(2,1)}, bf16[432,2048]{1,0:T(8,128)(2,1)}, u32[]{:S(2)}, u32[]{:S(2)}) collective-permute-start(bf16[432,2048]{1,0:T(8,128)(2,1)} %get-tuple-element.171), channel_id=1, source_target_pairs={{0,2},{1,3},{2,4},{3,5},{4,6},{5,7},{8,10},{9,11},{10,12},{11,13},... | collective-permute-start | bytes 5308424 | tf_op jit(solution)/shard_map/ppermute | solution.py:65
  883.1 368.0 %all-reduce.14.cloned.1.call-start = ((), (), s32[]{:S(2)}) async-start(), calls=%async_computation.2 | async-start | bytes 16777216 | tf_op jit(solution)/shard_map/psum | solution.py:791
  1074.4 267.6 %all-gather.2.cloned.1.call-start = ((), (), s32[]{:S(2)}) async-start(), calls=%async_computation | async-start | bytes 3833856 | tf_op jit(solution)/shard_map/all_gather | solution.py:872
  1102.6 325.4 %all-reduce.16.cloned.1.call-start = ((), (), s32[]{:S(2)}) async-start(), calls=%async_computation.3 | async-start | bytes 16777216 | tf_op jit(solution)/shard_map/psum | solution.py:794
  1118.8 134.0 %collective-permute-start.54 = (bf16[256,2048]{1,0:T(8,128)(2,1)}, bf16[256,2048]{1,0:T(8,128)(2,1)}, u32[]{:S(2)}, u32[]{:S(2)}) collective-permute-start(bf16[256,2048]{1,0:T(8,128)(2,1)} %get-tuple-element.167), channel_id=1, source_target_pairs={{0,2},{1,3},{8,10},{9,11},{16,18},{17,19},{24,26},{25,27}} | collective-permute-start | bytes 3145736 | tf_op jit(solution)/shard_map/ppermute | solution.py:65
  1133.8 128.1 %collective-permute-start.47 = (bf16[272,2560]{1,0:T(8,128)(2,1)S(1)}, bf16[272,2560]{1,0:T(8,128)(2,1)}, u32[]{:S(2)}, u32[]{:S(2)}) collective-permute-start(bf16[272,2560]{1,0:T(8,128)(2,1)S(1)} %get-tuple-element.159), channel_id=1, source_target_pairs={{0,2},{1,3},{8,10},{9,11},{16,18},{17,19},{24,26},{25,27}} | collective-permute-start | bytes 4177928 | tf_op jit(solution)/shard_map/ppermute | solution.py:65
  1251.1 333.3 %all-reduce.18.cloned.1.call-start = ((), (), s32[]{:S(2)}) async-start(), calls=%async_computation.4 | async-start | bytes 13533184 | tf_op jit(solution)/shard_map/psum | solution.py:890
  (186 other events, 4374.9 us)
Sparse Core Ops, SparseCore 0:
  883.2 191.0 all-reduce.11
  1078.3 172.7 all-reduce.13
  1255.2 172.7 all-reduce.15
  1435.0 149.4 all-reduce.17
Sparse Core Ops, SparseCore 1:
  1102.7 52.8 all-gather.1

commit v2 on v1

v2 whole, which is shorter than its diff:
```python
import functools
import math

import jax
import jax.numpy as jnp
from jax import lax
from jax.experimental import pallas as pl
from jax.experimental.pallas import tpu as pltpu
from jax.sharding import PartitionSpec as P

EPS = 1e-06
NEGATIVE = -1e30
LOW = jnp.bfloat16
FULL = jnp.float32
TILE = 16
MIB = 1 << 20
SMALL = pl.CostEstimate(flops=1, bytes_accessed=1, transcendentals=0)


def normalize(rows, gain):
    return rows * lax.rsqrt(jnp.mean(rows * rows, axis=-1, keepdims=True) + EPS) * gain


def multiply(left, right):
    return jnp.dot(left, right, preferred_element_type=FULL)


def multiply_left(left, right):
    return lax.dot_general(
        left, right, (((0,), (0,)), ((), ())), preferred_element_type=FULL
    )


def multiply_right(left, right):
    return lax.dot_general(
        left, right, (((1,), (1,)), ((), ())), preferred_element_type=FULL
    )


def activate(gate, upper):
    return jax.nn.gelu(gate, approximate=True) * upper


class Line:
    def __init__(self):
        self.size = lax.axis_size("fsdp")
        self.chips = self.size // 2
        self.place = lax.axis_index("fsdp")
        self.chip = self.place // 2
        self.core = self.place % 2

    def move(self, value, chips, step):
        pairs = [
            (2 * chip + core, 2 * (chip + step) + core) for chip in chips for core in range(2)
        ]
        return lax.ppermute(value, "fsdp", pairs)

    def pairs(self, identity, *values):
        mine, other = (weight_shares(core, *values) for core in (self.core, 1 - self.core))
        return add_pairs(identity, mine, other)


class Relay:
    def __init__(self, line, summed, index):
        self.line, self.summed, self.index = line, summed, index
        self.taken, self.arrived = 0, []

    def advance(self, part, parts=3):
        line, count = self.line, self.line.chips
        last = -(-(count - 1) * part // parts)
        while self.taken < last:
            self.taken += 1
            step, arrived = self.taken, self.arrived
            self.arrived = []
            for i, side in enumerate((1, -1)):
                target = self.index(jnp.clip(line.chip + side * (count - step), 0, count - 1))
                if arrived:
                    payload = add_block(self.summed, target, [arrived[i]], LOW)
                else:
                    payload = lax.dynamic_index_in_dim(self.summed, target, 0, keepdims=False)
                chips = range(0, step) if side == 1 else range(count - step, count)
                self.arrived.append(line.move(payload, chips, side))

    def after(self, values):
        self.arrived, values = lax.optimization_barrier((self.arrived, values))
        return values

    def finish(self):
        self.advance(1, 1)
        return add_block(self.summed, self.index(self.line.chip), self.arrived, FULL)


def add_kernel(index_ref, value_ref, *refs):
    total = value_ref[0].astype(FULL)
    for ref in refs[:-1]:
        total = total + ref[...].astype(FULL)
    refs[-1][...] = total.astype(refs[-1].dtype)


def add_block(values, index, others, kind):
    shape = values.shape[1:]
    block = pl.BlockSpec(shape, lambda i, index: (0, 0))
    return pl.pallas_call(
        add_kernel,
        out_shape=jax.ShapeDtypeStruct(shape, kind),
        grid_spec=pltpu.PrefetchScalarGridSpec(
            num_scalar_prefetch=1,
            grid=(1,),
            in_specs=[pl.BlockSpec((1, *shape), lambda i, index: (index[0], 0, 0))]
            + [block] * len(others),
            out_specs=block,
        ),
        compiler_params=pltpu.CompilerParams(vmem_limit_bytes=40 * MIB),
        cost_estimate=SMALL,
        name="add_block",
    )(jnp.reshape(index, (1,)).astype(jnp.int32), values, *others)


def pair_kernel(mine_ref, other_ref, out_ref, landed, send_sem, recv_sem):
    place, me = lax.axis_index("dp"), lax.axis_index("fsdp")
    partner = (place, me + 1 - 2 * (me % 2))
    mesh = pl.DeviceIdType.MESH
    turn, count = pl.program_id(0), landed.shape[0]

    def copy(at):
        return pltpu.make_async_remote_copy(
            src_ref=other_ref.at[at],
            dst_ref=landed.at[at],
            send_sem=send_sem.at[at],
            recv_sem=recv_sem.at[at],
            device_id=partner,
            device_id_type=mesh,
        )

    @pl.when(turn == 0)
    def _():
        barrier = pltpu.get_barrier_semaphore()
        pl.semaphore_signal(barrier, inc=1, device_id=partner, device_id_type=mesh)
        pl.semaphore_wait(barrier, 1)
        for at in range(count):
            copy(at).start()

    copy(turn).wait_recv()
    out_ref[0] = (mine_ref[0].astype(FULL) + landed[turn].astype(FULL)).astype(LOW)

    @pl.when(turn == count - 1)
    def _():
        for at in range(count):
            copy(at).wait_send()


def add_pairs(identity, mine, other):
    count, shape = mine.shape[0], mine.shape[1:]
    block = pl.BlockSpec((1, *shape), lambda i: (i, 0, 0))
    dma = pltpu.SemaphoreType.DMA
    return pl.pallas_call(
        pair_kernel,
        out_shape=jax.ShapeDtypeStruct(mine.shape, LOW),
        grid=(count,),
        in_specs=[block, pl.BlockSpec(memory_space=pl.ANY)],
        out_specs=block,
        scratch_shapes=[pltpu.VMEM(mine.shape, LOW), dma((count,)), dma((count,))],
        compiler_params=pltpu.CompilerParams(
            collective_id=identity, has_side_effects=True, vmem_limit_bytes=40 * MIB
        ),
        cost_estimate=SMALL,
        name="add_pairs",
    )(mine, other)


def rounded(count, unit=TILE):
    return -(-count // unit) * unit


def gather_kernel(shares, *refs):
    count = len(shares)
    shards, wholes = refs[:count], refs[count : 2 * count]
    local_sem, pair_send, pair_recv = refs[2 * count : 2 * count + 3]
    line_send, line_recv, copy_send, copy_recv, core_send, core_recv = refs[2 * count + 3 :]
    mesh = pl.DeviceIdType.MESH
    copies = lax.axis_size("dp")
    place = lax.axis_index("dp")
    size = lax.axis_size("fsdp")
    chips = size // 2
    me = lax.axis_index("fsdp")
    chip, core = me // 2, me % 2
    partner = 2 * chip + 1 - core
    has_left, has_right = chip > 0, chip < chips - 1

    barrier = pltpu.get_barrier_semaphore()
    pl.semaphore_signal(barrier, inc=1, device_id=(place, partner), device_id_type=mesh)
    for k in range(1, copies):
        peer = lax.rem(place + k, copies)
        pl.semaphore_signal(barrier, inc=1, device_id=(peer, me), device_id_type=mesh)

    @pl.when(has_left)
    def _():
        pl.semaphore_signal(barrier, inc=1, device_id=(place, me - 2), device_id_type=mesh)

    @pl.when(has_right)
    def _():
        pl.semaphore_signal(barrier, inc=1, device_id=(place, me + 2), device_id_type=mesh)

    neighbours = jnp.minimum(chip, 1) + jnp.minimum(chips - 1 - chip, 1)
    pl.semaphore_wait(barrier, copies + neighbours)

    def rows(a, owner, share):
        whole = shards[a].shape[0]
        part = whole // shares[a]
        return pl.ds(pl.multiple_of(owner * whole + share * part, TILE), part)

    def remote(source, target, send, recv, device):
        return pltpu.make_async_remote_copy(
            src_ref=source,
            dst_ref=target,
            send_sem=send,
            recv_sem=recv,
            device_id=device,
            device_id_type=mesh,
        )

    def my_share(a):
        return place if shares[a] > 1 else 0

    def line_copy(a, side, step):
        owner = me - 2 * step if side == 0 else me + 2 * step
        where = rows(a, owner, my_share(a))
        target = me + 2 if side == 0 else me - 2
        return remote(
            wholes[a].at[where],
            wholes[a].at[where],
            line_send.at[a, side, step],
            line_recv.at[a, side, step],
            (place, target),
        )

    def first_copy(a, side):
        part = shards[a].shape[0] // shares[a]
        target = me + 2 if side == 0 else me - 2
        return remote(
            shards[a].at[pl.ds(pl.multiple_of(my_share(a) * part, TILE), part)],
            wholes[a].at[rows(a, me, my_share(a))],
            line_send.at[a, side, 0],
            line_recv.at[a, side, 0],
            (place, target),
        )

    def owner_of(side, step):
        return me - 2 * step if side == 0 else me + 2 * step

    def peer_copy(a, side, step, k):
        where = rows(a, owner_of(side, step), place)
        return remote(
            wholes[a].at[where],
            wholes[a].at[where],
            copy_send.at[a, side, step, k],
            copy_recv.at[a, side, step, k],
            (lax.rem(place + k, copies), me),
        )

    def core_copy(a, side, step, k):
        share = lax.rem(place + copies - k, copies) if shares[a] > 1 else 0
        where = rows(a, owner_of(side, step), share)
        return remote(
            wholes[a].at[where],
            wholes[a].at[where],
            core_send.at[a, side, step, k],
            core_recv.at[a, side, step, k],
            (place, partner),
        )

    def pair_copy(a):
        return remote(
            shards[a],
            wholes[a].at[rows_all(a)],
            pair_send.at[a],
            pair_recv.at[a],
            (place, partner),
        )

    def rows_all(a):
        whole = shards[a].shape[0]
        return pl.ds(pl.multiple_of(me * whole, TILE), whole)

    def local_copy(a):
        return pltpu.make_async_copy(shards[a], wholes[a].at[rows_all(a)], local_sem.at[a])

    def sends(side):
        return has_right if side == 0 else has_left

    def has(side, step):
        return chip >= step if side == 0 else chip + step <= chips - 1

    for a in range(count):
        for side in range(2):

            @pl.when(sends(side))
            def _(a=a, side=side):
                first_copy(a, side).start()

    for a in range(count):
        pair_copy(a).start()
        local_copy(a).start()

    def peers(a):
        return range(1, copies) if shares[a] > 1 else range(0)

    def hand_over(a, side, step):
        for k in peers(a):
            peer_copy(a, side, step, k).wait_recv()
            core_copy(a, side, step, k).start()

    def advance(step, _):
        for a in range(count):
            for side in range(2):

                @pl.when(has(side, step))
                def _(a=a, side=side):
                    line_copy(a, side, step - 1).wait_recv()

                    @pl.when(sends(side))
                    def _():
                        line_copy(a, side, step).start()

                    for k in peers(a):
                        peer_copy(a, side, step, k).start()
                    core_copy(a, side, step, 0).start()

        for a in range(count):
            for side in range(2):

                @pl.when((step > 1) & has(side, step - 1))
                def _(a=a, side=side):
                    hand_over(a, side, step - 1)

        return 0

    lax.fori_loop(1, chips, advance, 0)
    for a in range(count):
        for side in range(2):

            @pl.when(has(side, chips - 1))
            def _(a=a, side=side):
                hand_over(a, side, chips - 1)

    def finish(step, _):
        for a in range(count):
            for side in range(2):

                @pl.when(has(side, step))
                def _(a=a, side=side):
                    @pl.when(sends(side))
                    def _():
                        line_copy(a, side, step).wait_send()

                    for k in peers(a):
                        peer_copy(a, side, step, k).wait_send()
                        core_copy(a, side, step, k).wait_send()
                        core_copy(a, side, step, k).wait_recv()
                    core_copy(a, side, step, 0).wait_send()
                    core_copy(a, side, step, 0).wait_recv()

        return 0

    lax.fori_loop(1, chips, finish, 0)
    for a in range(count):
        for side in range(2):

            @pl.when(sends(side))
            def _(a=a, side=side):
                first_copy(a, side).wait_send()

        pair_copy(a).wait_send()
        pair_copy(a).wait_recv()
        local_copy(a).wait()


def gather_shards(identity, *shards):
    copies, size = lax.axis_size("dp"), lax.axis_size("fsdp")
    chips = size // 2
    shares = [copies if shard.shape[0] % (TILE * copies) == 0 else 1 for shard in shards]
    count = len(shards)
    dma = pltpu.SemaphoreType.DMA
    anywhere = pl.BlockSpec(memory_space=pl.ANY)
    return pl.pallas_call(
        functools.partial(gather_kernel, shares),
        out_shape=[
            jax.ShapeDtypeStruct((size * shard.shape[0], *shard.shape[1:]), shard.dtype)
            for shard in shards
        ],
        in_specs=[anywhere] * count,
        out_specs=[anywhere] * count,
        scratch_shapes=[
            dma((count,)),
            dma((count,)),
            dma((count,)),
            dma((count, 2, chips)),
            dma((count, 2, chips)),
            dma((count, 2, chips, copies)),
            dma((count, 2, chips, copies)),
            dma((count, 2, chips, copies)),
            dma((count, 2, chips, copies)),
        ],
        compiler_params=pltpu.CompilerParams(collective_id=identity, has_side_effects=True),
        cost_estimate=SMALL,
        name="gather_shards",
    )(*shards)


def across(number, other):
    total, bit = 0, 1
    while bit < lax.axis_size("fsdp") // 2:
        total = total + bit * ((number // bit % 2 + other // bit % 2) % 2)
        bit *= 2
    return total


def greet(place, me, chip, chips):
    mesh = pl.DeviceIdType.MESH
    barrier = pltpu.get_barrier_semaphore()
    partner = 2 * chip + 1 - me % 2
    pl.semaphore_signal(barrier, inc=1, device_id=(place, partner), device_id_type=mesh)

    @pl.when(chip > 0)
    def _():
        pl.semaphore_signal(barrier, inc=1, device_id=(place, me - 2), device_id_type=mesh)

    @pl.when(chip < chips - 1)
    def _():
        pl.semaphore_signal(barrier, inc=1, device_id=(place, me + 2), device_id_type=mesh)

    neighbours = jnp.minimum(chip, 1) + jnp.minimum(chips - 1 - chip, 1)
    pl.semaphore_wait(barrier, 1 + neighbours)


def feed_kernel(
    valid,
    hidden_ref,
    backs_ref,
    gate_ref,
    up_ref,
    down_ref,
    inner_ref,
    gate_grad_ref,
    up_grad_ref,
    rows_ref,
    back_ref,
    small_ref,
    land,
    held,
    line_send,
    line_recv,
    core_send,
    core_recv,
    own_sem,
    back_sem,
    out_sem,
):
    mesh = pl.DeviceIdType.MESH
    place, me = lax.axis_index("dp"), lax.axis_index("fsdp")
    chips = lax.axis_size("fsdp") // 2
    chip, core = me // 2, me % 2
    block = hidden_ref.shape[0]
    position, tile = pl.program_id(0), pl.program_id(1)
    tiles = pl.num_programs(1)
    source = across(chip, position)
    owners = (2 * source + core, 2 * source + 1 - core)
    slot = lax.rem(position, 2)

    def sends(side):
        return chip < chips - 1 if side == 0 else chip > 0

    def has(side, step):
        return chip >= step if side == 0 else chip + step <= chips - 1

    def line_copy(side, step):
        owner = me - 2 * step if side == 0 else me + 2 * step
        target = me + 2 if side == 0 else me - 2
        return pltpu.make_async_remote_copy(
            src_ref=land.at[owner],
            dst_ref=land.at[owner],
            send_sem=line_send.at[side, step],
            recv_sem=line_recv.at[side, step],
            device_id=(place, target),
            device_id_type=mesh,
        )

    def line_arrival(side, step):
        owner = me - 2 * step if side == 0 else me + 2 * step
        return pltpu.make_async_remote_copy(
            src_ref=land.at[owner],
            dst_ref=land.at[owner],
            send_sem=line_send.at[side, step - 1],
            recv_sem=line_recv.at[side, step - 1],
            device_id=(place, me + 2 if side == 0 else me - 2),
            device_id_type=mesh,
        )

    def core_copy(owner_chip):
        owner = 2 * owner_chip + core
        return pltpu.make_async_remote_copy(
            src_ref=land.at[owner],
            dst_ref=land.at[owner],
            send_sem=core_send.at[owner_chip],
            recv_sem=core_recv.at[owner_chip],
            device_id=(place, 2 * chip + 1 - core),
            device_id_type=mesh,
        )

    def back_copies(at):
        origin = across(chip, at)
        to = lax.rem(at, 2)
        return [
            pltpu.make_async_copy(
                backs_ref.at[pl.ds(pl.multiple_of(owner * block, TILE), block)],
                held.at[to, half],
                back_sem.at[to, half],
            )
            for half, owner in enumerate((2 * origin + core, 2 * origin + 1 - core))
        ]

    def out_copies():
        copies = []
        for half in range(2):
            where = pl.ds(pl.multiple_of((2 * position + half) * valid, TILE), valid)
            rows, back = land.at[owners[half]], held.at[slot, half]
            for source_ref, target, small in ((rows, rows_ref, 0), (back, back_ref, 1)):
                copies.append((source_ref.at[pl.ds(0, valid)], target.at[where]))
                copies.append(
                    (
                        source_ref.at[pl.ds(valid, block - valid)],
                        small_ref.at[small, position, half],
                    )
                )
        return [
            pltpu.make_async_copy(source_ref, target, out_sem.at[i])
            for i, (source_ref, target) in enumerate(copies)
        ]

    @pl.when((position == 0) & (tile == 0))
    def _():
        for copy in back_copies(0):
            copy.start()
        own = pltpu.make_async_copy(hidden_ref, land.at[me], own_sem)
        own.start()
        greet(place, me, chip, chips)
        own.wait()
        for side in range(2):

            @pl.when(sends(side))
            def _(side=side):
                line_copy(side, 0).start()

        core_copy(chip).start()

    @pl.when(tile == 0)
    def _():
        for side in range(2):

            @pl.when((position > 0) & has(side, position))
            def _(side=side):
                line_arrival(side, position).wait_recv()

                @pl.when(sends(side))
                def _():
                    line_copy(side, position).start()

                core_copy(chip - position if side == 0 else chip + position).start()

        core_copy(source).wait_recv()
        for copy in back_copies(position):
            copy.wait()
        for copy in out_copies():
            copy.start()

        @pl.when(position < chips - 1)
        def _():
            for copy in back_copies(position + 1):
                copy.start()

    root = math.sqrt(2.0 / math.pi)
    for half in range(2):
        where = slice(half * valid, (half + 1) * valid)
        rows = land[owners[half], :valid]
        back = held[slot, half, :valid]
        gate = multiply(rows, gate_ref[...])
        upper = multiply(rows, up_ref[...])
        inner_grad = multiply_right(back, down_ref[...])
        square = gate * gate
        bent = jnp.tanh(root * gate * (1.0 + 0.044715 * square))
        half_up = 0.5 + 0.5 * bent
        active = gate * half_up
        slope = half_up + (0.5 * root) * gate * (1.0 - bent * bent) * (1.0 + 0.134145 * square)
        inner_ref[where] = (active * upper).astype(LOW)
        gate_grad_ref[where] = (inner_grad * upper * slope).astype(LOW)
        up_grad_ref[where] = (inner_grad * active).astype(LOW)

    @pl.when(tile == tiles - 1)
    def _():
        for copy in out_copies():
            copy.wait()

    @pl.when((tile == tiles - 1) & (position == chips - 1))
    def _():
        for side in range(2):

            @pl.when(sends(side))
            def _(side=side):
                line_copy(side, 0).wait_send()

        for owner in range(chips):
            core_copy(owner).wait_send()

        def finish(step, _):
            for side in range(2):

                @pl.when(sends(side) & has(side, step))
                def _(side=side):
                    line_copy(side, step).wait_send()

            return 0

        lax.fori_loop(1, chips, finish, 0)


def feed_all(valid, hidden, backs, gate, up, down):
    block, width = hidden.shape
    size = lax.axis_size("fsdp")
    chips = size // 2
    units = gate.shape[1]
    tile = math.gcd(units, 512)
    column = pl.BlockSpec((width, tile), lambda p, j: (0, j))
    anywhere = pl.BlockSpec(memory_space=pl.ANY)
    total = chips * 2 * valid
    dma = pltpu.SemaphoreType.DMA
    return pl.pallas_call(
        functools.partial(feed_kernel, valid),
        out_shape=[jax.ShapeDtypeStruct((total, units), LOW)] * 3
        + [jax.ShapeDtypeStruct((total, width), LOW)] * 2
        + [jax.ShapeDtypeStruct((2, chips, 2, block - valid, width), LOW)],
        grid=(chips, units // tile),
        in_specs=[anywhere, anywhere, column, column]
        + [pl.BlockSpec((tile, width), lambda p, j: (j, 0))],
        out_specs=[pl.BlockSpec((2 * valid, tile), lambda p, j: (p, j))] * 3 + [anywhere] * 3,
        scratch_shapes=[
            pltpu.VMEM((size, block, width), LOW),
            pltpu.VMEM((2, 2, block, width), LOW),
            dma((2, chips)),
            dma((2, chips)),
            dma((chips,)),
            dma((chips,)),
            dma,
            dma((2, 2)),
            dma((8,)),
        ],
        compiler_params=pltpu.CompilerParams(
            collective_id=1, has_side_effects=True, vmem_limit_bytes=58 * MIB
        ),
        cost_estimate=SMALL,
        name="feed_all",
    )(hidden, backs, gate, up, down)


def collect_kernel(valid, transposed, count, width, *refs):
    grads, weights = refs[:count], refs[count : 2 * count]
    small_ref, total_ref = refs[2 * count : 2 * count + 2]
    mine, other, pair, arrive = refs[2 * count + 2 : 2 * count + 6]
    line_send, line_recv, core_send, core_recv = refs[2 * count + 6 :]
    mesh = pl.DeviceIdType.MESH
    place, me = lax.axis_index("dp"), lax.axis_index("fsdp")
    chips = lax.axis_size("fsdp") // 2
    chip, core = me // 2, me % 2
    turn, tile = pl.program_id(0), pl.program_id(1)
    tiles = pl.num_programs(1)
    span = small_ref.shape[-1]
    target = across(chip, chips - 1 - turn)
    slot = lax.rem(turn, 2)
    columns = pl.ds(pl.multiple_of(tile * span, 128), span)

    def core_copy(at_turn, at_tile):
        where = pl.ds(pl.multiple_of(at_tile * span, 128), span)
        owner = across(chip, chips - 1 - at_turn)
        return pltpu.make_async_remote_copy(
            src_ref=other.at[lax.rem(at_turn, 2), :, where],
            dst_ref=pair.at[owner, :, where],
            send_sem=core_send.at[lax.rem(at_turn, 2), at_tile],
            recv_sem=core_recv.at[owner, at_tile],
            device_id=(place, 2 * chip + 1 - core),
            device_id_type=mesh,
        )

    def valid_at(side, step):
        return chip <= step - 1 if side == 0 else chip >= chips - step

    def fed(side):
        return chip > 0 if side == 0 else chip < chips - 1

    def owner_at(side, step):
        return chip + chips - step if side == 0 else chip - chips + step

    def line_copy(side, step):
        return pltpu.make_async_remote_copy(
            src_ref=mine.at[owner_at(side, step)],
            dst_ref=arrive.at[side, step - 1],
            send_sem=line_send.at[side, step - 1],
            recv_sem=line_recv.at[side, step - 1],
            device_id=(place, me + 2 if side == 0 else me - 2),
            device_id_type=mesh,
        )

    def line_arrival(side, step):
        return pltpu.make_async_remote_copy(
            src_ref=mine.at[chip],
            dst_ref=arrive.at[side, step - 1],
            send_sem=line_send.at[side, step - 1],
            recv_sem=line_recv.at[side, step - 1],
            device_id=(place, me + 2 if side == 0 else me - 2),
            device_id_type=mesh,
        )

    @pl.when((turn == 0) & (tile == 0))
    def _():
        greet(place, me, chip, chips)

    @pl.when((turn > 0) & (tile == 0))
    def _():
        done = across(chip, chips - turn)

        def take(at_tile, _):
            core_copy(turn - 1, at_tile).wait_recv()
            return 0

        lax.fori_loop(0, tiles, take, 0)
        mine[done] = (mine[done].astype(FULL) + pair[done].astype(FULL)).astype(LOW)
        for side in range(2):

            @pl.when(valid_at(side, turn))
            def _(side=side):
                owner = owner_at(side, turn)

                @pl.when((turn > 1) & fed(side))
                def _():
                    line_arrival(side, turn - 1).wait_recv()
                    mine[owner] = (
                        mine[owner].astype(FULL) + arrive[side, turn - 2].astype(FULL)
                    ).astype(LOW)

                line_copy(side, turn).start()

    @pl.when(turn > 1)
    def _():
        core_copy(turn - 2, tile).wait_send()

    for half in range(2):
        where = slice(half * valid, (half + 1) * valid)
        part = None
        for grad, weight in zip(grads, weights):
            product = (multiply_right if transposed else multiply)(grad[where], weight[...])
            part = product if part is None else part + product
        if half == 0:
            mine[target, :valid, columns] = part.astype(LOW)
            mine[target, valid:, columns] = small_ref[0, 0]
        else:
            other[slot, :valid, columns] = part.astype(LOW)
            other[slot, valid:, columns] = small_ref[0, 1]
    core_copy(turn, tile).start()

    @pl.when((turn == chips - 1) & (tile == tiles - 1))
    def _():
        def take(at_tile, _):
            core_copy(turn, at_tile).wait_recv()
            core_copy(turn, at_tile).wait_send()

            @pl.when(turn > 0)
            def _():
                core_copy(turn - 1, at_tile).wait_send()

            return 0

        lax.fori_loop(0, tiles, take, 0)
        total_ref[...] = mine[chip].astype(FULL) + pair[chip].astype(FULL)
        for side in range(2):

            @pl.when(fed(side))
            def _(side=side):
                line_arrival(side, chips - 1).wait_recv()
                total_ref[...] += arrive[side, chips - 2].astype(FULL)

        def finish(step, _):
            for side in range(2):

                @pl.when(valid_at(side, step))
                def _(side=side):
                    line_copy(side, step).wait_send()

            return 0

        lax.fori_loop(1, chips, finish, 0)


def collect(identity, valid, transposed, grads, weights, small, width):
    chips = lax.axis_size("fsdp") // 2
    units = grads[0].shape[1]
    extra = small.shape[2]
    block = valid + extra
    tile = math.gcd(width, 256)
    count = len(grads)
    rows = pl.BlockSpec((2 * valid, units), lambda t, j: (chips - 1 - t, 0))
    if transposed:
        weight = pl.BlockSpec((tile, units), lambda t, j: (j, 0))
    else:
        weight = pl.BlockSpec((units, tile), lambda t, j: (0, j))
    dma = pltpu.SemaphoreType.DMA
    return pl.pallas_call(
        functools.partial(collect_kernel, valid, transposed, count, width),
        out_shape=jax.ShapeDtypeStruct((block, width), FULL),
        grid=(chips, width // tile),
        in_specs=[rows] * count
        + [weight] * count
        + [pl.BlockSpec((1, 2, extra, tile), lambda t, j: (chips - 1 - t, 0, 0, j))],
        out_specs=pl.BlockSpec((block, width), lambda t, j: (0, 0)),
        scratch_shapes=[
            pltpu.VMEM((chips, block, width), LOW),
            pltpu.VMEM((2, block, width), LOW),
            pltpu.VMEM((chips, block, width), LOW),
            pltpu.VMEM((2, chips - 1, block, width), LOW),
            dma((2, chips - 1)),
            dma((2, chips - 1)),
            dma((2, width // tile)),
            dma((chips, width // tile)),
        ],
        compiler_params=pltpu.CompilerParams(
            collective_id=identity, has_side_effects=True, vmem_limit_bytes=62 * MIB
        ),
        cost_estimate=SMALL,
        name="collect",
    )(*grads, *weights, small)


def part_kernel(valid, inner_ref, down_ref, small_ref, mine_ref, other_ref):
    for half, out in enumerate((mine_ref, other_ref)):
        where = slice(half * valid, (half + 1) * valid)
        out[0, :valid] = multiply(inner_ref[where], down_ref[...]).astype(LOW)
        out[0, valid:] = small_ref[0, half]


def part_chunks(valid, inner, down, small):
    chips, _, extra, width = small.shape
    units = inner.shape[1]
    tile = math.gcd(width, 512)
    out = pl.BlockSpec((1, valid + extra, tile), lambda p, j: (p, 0, j))
    return pl.pallas_call(
        functools.partial(part_kernel, valid),
        out_shape=[jax.ShapeDtypeStruct((chips, valid + extra, width), LOW)] * 2,
        grid=(chips, width // tile),
        in_specs=[
            pl.BlockSpec((2 * valid, units), lambda p, j: (p, 0)),
            pl.BlockSpec((units, tile), lambda p, j: (0, j)),
            pl.BlockSpec((1, 2, extra, tile), lambda p, j: (p, 0, 0, j)),
        ],
        out_specs=[out] * 2,
        compiler_params=pltpu.CompilerParams(vmem_limit_bytes=48 * MIB),
        cost_estimate=SMALL,
        name="part_chunks",
    )(inner, down, small)


def norm_back(rows, gain, grad):
    factor = lax.rsqrt(jnp.mean(rows * rows, axis=-1, keepdims=True) + EPS)
    scaled = gain * grad
    inner = jnp.mean(rows * scaled, axis=-1, keepdims=True)
    rows_grad = factor * scaled - (factor * factor * factor * inner) * rows
    return rows_grad, jnp.sum(grad * rows * factor, axis=0, keepdims=True)


def middle_kernel(grad_ref, rows_ref, back_ref, gain_ref, weight_ref, total_ref, low_ref, mixed_ref, part_ref):
    @pl.when(pl.program_id(0) == 0)
    def _():
        rows_grad, part_ref[...] = norm_back(rows_ref[...], gain_ref[...], grad_ref[...])
        total = back_ref[...].astype(FULL) + rows_grad
        total_ref[...] = total
        low_ref[...] = total.astype(LOW)

    mixed_ref[...] = multiply_right(low_ref[...], weight_ref[...]).astype(LOW)


def middle_back(grad, rows, back, gain, weight):
    count, width = rows.shape
    features = weight.shape[0]
    tile = math.gcd(features, 512)
    whole = pl.BlockSpec((count, width), lambda j: (0, 0))
    return pl.pallas_call(
        middle_kernel,
        out_shape=[
            jax.ShapeDtypeStruct((count, width), FULL),
            jax.ShapeDtypeStruct((count, width), LOW),
            jax.ShapeDtypeStruct((count, features), LOW),
            jax.ShapeDtypeStruct((1, width), FULL),
        ],
        grid=(features // tile,),
        in_specs=[whole, whole, whole, pl.BlockSpec((1, width), lambda j: (0, 0))]
        + [pl.BlockSpec((tile, width), lambda j: (j, 0))],
        out_specs=[whole, whole, pl.BlockSpec((count, tile), lambda j: (0, j))]
        + [pl.BlockSpec((1, width), lambda j: (0, 0))],
        compiler_params=pltpu.CompilerParams(vmem_limit_bytes=56 * MIB),
        cost_estimate=SMALL,
        name="middle_back",
    )(grad, rows, back, gain.reshape(1, width), weight)


def entry_kernel(query_ref, kv_ref, rows_ref, total_ref, gain_ref, weight_ref, out_ref, part_ref, held):
    tile = weight_ref.shape[0]
    where = pl.ds(pl.multiple_of(pl.program_id(0) * tile, 128), tile)
    features = query_ref.shape[1]
    held[:, where] = multiply_right(query_ref[...], weight_ref[:, :features]) + multiply_right(
        kv_ref[...], weight_ref[:, features:]
    )

    @pl.when(pl.program_id(0) == pl.num_programs(0) - 1)
    def _():
        rows_grad, part_ref[...] = norm_back(rows_ref[...], gain_ref[...], held[...])
        out_ref[...] = total_ref[...] + rows_grad


def entry_back(query_grad, kv_grad, rows, total, gain, weight):
    count, width = rows.shape
    tile = math.gcd(width, 512)
    fixed = lambda j: (0, 0)
    whole = pl.BlockSpec((count, width), fixed)
    return pl.pallas_call(
        entry_kernel,
        out_shape=[
            jax.ShapeDtypeStruct((count, width), FULL),
            jax.ShapeDtypeStruct((1, width), FULL),
        ],
        grid=(width // tile,),
        in_specs=[
            pl.BlockSpec(query_grad.shape, fixed),
            pl.BlockSpec(kv_grad.shape, fixed),
            whole,
            whole,
            pl.BlockSpec((1, width), fixed),
            pl.BlockSpec((tile, weight.shape[1]), lambda j: (j, 0)),
        ],
        out_specs=[whole, pl.BlockSpec((1, width), fixed)],
        scratch_shapes=[pltpu.VMEM((count, width), FULL)],
        compiler_params=pltpu.CompilerParams(vmem_limit_bytes=56 * MIB),
        cost_estimate=SMALL,
        name="entry_back",
    )(query_grad, kv_grad, rows, total, gain.reshape(1, width), weight)


def sum_kernel(split, *refs):
    count = len(split)
    values, totals = refs[:count], refs[count : 2 * count]
    arrived, whole = refs[2 * count : 3 * count], refs[3 * count : 4 * count]
    part_send, part_recv, whole_send, whole_recv = refs[4 * count :]
    mesh = pl.DeviceIdType.MESH
    copies = lax.axis_size("dp")
    place, me = lax.axis_index("dp"), lax.axis_index("fsdp")
    barrier = pltpu.get_barrier_semaphore()
    for k in range(1, copies):
        peer = lax.rem(place + k, copies)
        pl.semaphore_signal(barrier, inc=1, device_id=(peer, me), device_id_type=mesh)
    pl.semaphore_wait(barrier, copies - 1)

    def rows(a, owner):
        part = values[a].shape[0] // copies
        return pl.ds(pl.multiple_of(owner * part, TILE), part)

    def part_copy(a, k):
        peer = lax.rem(place + k, copies)
        return pltpu.make_async_remote_copy(
            src_ref=values[a].at[rows(a, peer)] if split[a] else values[a],
            dst_ref=arrived[a].at[k - 1] if split[a] else arrived[a].at[place],
            send_sem=part_send.at[a, k],
            recv_sem=part_recv.at[a, k],
            device_id=(peer, me),
            device_id_type=mesh,
        )

    def whole_copy(a, k):
        return pltpu.make_async_remote_copy(
            src_ref=whole[a].at[rows(a, place)],
            dst_ref=whole[a].at[rows(a, place)],
            send_sem=whole_send.at[a, k],
            recv_sem=whole_recv.at[a, k],
            device_id=(lax.rem(place + k, copies), me),
            device_id_type=mesh,
        )

    for a in range(count):
        for k in range(1, copies):
            part_copy(a, k).start()
    for a in range(count):
        if not split[a]:
            arrived[a][place] = values[a][...]
        for k in range(1, copies):
            part_copy(a, k).wait_recv()
        if split[a]:
            total = values[a][rows(a, place)].astype(FULL)
            for k in range(1, copies):
                total = total + arrived[a][k - 1].astype(FULL)
            whole[a][rows(a, place)] = total.astype(LOW)
            for k in range(1, copies):
                whole_copy(a, k).start()
        else:
            total = arrived[a][0].astype(FULL)
            for k in range(1, copies):
                total = total + arrived[a][k].astype(FULL)
            totals[a][...] = total
    for a in range(count):
        for k in range(1, copies):
            part_copy(a, k).wait_send()
            if split[a]:
                whole_copy(a, k).wait_send()
                whole_copy(a, k).wait_recv()
        if split[a]:
            totals[a][...] = whole[a][...].astype(FULL)


def sum_copies(identity, values):
    copies = lax.axis_size("dp")
    split = [value.shape[0] % (TILE * copies) == 0 for value in values]
    count = len(values)
    dma = pltpu.SemaphoreType.DMA
    arrived, whole = [], []
    for value, parts in zip(values, split):
        rows, columns = value.shape
        arrived.append((copies - 1, rows // copies, columns) if parts else (copies, rows, columns))
        whole.append((rows, columns) if parts else (TILE, 128))
    inside = pl.BlockSpec(memory_space=pltpu.VMEM)
    return pl.pallas_call(
        functools.partial(sum_kernel, split),
        out_shape=[jax.ShapeDtypeStruct(value.shape, FULL) for value in values],
        in_specs=[inside] * count,
        out_specs=[inside] * count,
        scratch_shapes=[pltpu.VMEM(shape, LOW) for shape in arrived + whole]
        + [dma((count, copies))] * 4,
        compiler_params=pltpu.CompilerParams(
            collective_id=identity, has_side_effects=True, vmem_limit_bytes=48 * MIB
        ),
        cost_estimate=SMALL,
        name="sum_copies",
    )(*values)


def widen_kernel(*refs):
    count = len(refs) - 1
    for k, ref in enumerate(refs[:-1]):

        @pl.when(pl.program_id(0) == k)
        def _(ref=ref):
            refs[-1][...] = ref[...].astype(FULL)


def widen(*values):
    count, (rows, columns) = len(values), values[0].shape
    tile = math.gcd(rows, 256)
    return pl.pallas_call(
        widen_kernel,
        out_shape=jax.ShapeDtypeStruct((count * rows, columns), FULL),
        grid=(count, rows // tile),
        in_specs=[pl.BlockSpec((tile, columns), lambda k, i: (i, 0))] * count,
        out_specs=pl.BlockSpec((tile, columns), lambda k, i: (k * (rows // tile) + i, 0)),
        compiler_params=pltpu.CompilerParams(vmem_limit_bytes=32 * MIB),
        cost_estimate=SMALL,
        name="widen",
    )(*values)


def share_kernel(per, core_ref, left_ref, right_ref, action_left_ref, action_right_ref, *refs):
    out_ref = refs[-1]
    rows = left_ref.shape[1]
    out_ref[0, :rows] = multiply_left(left_ref[...], right_ref[...]).astype(LOW)
    product = multiply_left(action_left_ref[...], action_right_ref[...])
    count = product.shape[0] // per
    small = product[:count]
    which = lax.rem(2 * pl.program_id(0) + core_ref[0], per)
    for i in range(1, per):
        small = jnp.where(which == i, product[i * count : (i + 1) * count], small)
    small = small.astype(LOW)
    fold = out_ref.shape[2] // small.shape[1]
    extra = small.shape[0] // fold
    for i in range(fold):
        columns = slice(i * small.shape[1], (i + 1) * small.shape[1])
        out_ref[0, rows : rows + extra, columns] = small[i * extra : (i + 1) * extra]
    if len(refs) > 1:
        out_ref[0, rows + extra :] = refs[0][0]


def weight_shares(core, left, right, action_left, action_right, gains=None):
    size = lax.axis_size("fsdp")
    chips = size // 2
    count, rows = left.shape[0], left.shape[1] // size
    action_count, action_rows = action_left.shape[0], action_left.shape[1] // size
    width, action_width = right.shape[1], action_right.shape[1]
    total = rows + action_rows * action_width // width
    per = max(1, 128 // action_rows)
    extra = []
    if gains is not None:
        total += gains.shape[1]
        extra = [pl.BlockSpec((1, *gains.shape[1:]), lambda c, core: (2 * c + core[0], 0, 0))]
    return pl.pallas_call(
        functools.partial(share_kernel, per),
        out_shape=jax.ShapeDtypeStruct((chips, total, width), LOW),
        grid_spec=pltpu.PrefetchScalarGridSpec(
            num_scalar_prefetch=1,
            grid=(chips,),
            in_specs=[
                pl.BlockSpec((count, rows), lambda c, core: (0, 2 * c + core[0])),
                pl.BlockSpec((count, width), lambda c, core: (0, 0)),
                pl.BlockSpec(
                    (action_count, per * action_rows), lambda c, core: (0, (2 * c + core[0]) // per)
                ),
                pl.BlockSpec((action_count, action_width), lambda c, core: (0, 0)),
            ]
            + extra,
            out_specs=pl.BlockSpec((1, total, width), lambda c, core: (c, 0, 0)),
        ),
        compiler_params=pltpu.CompilerParams(vmem_limit_bytes=48 * MIB),
        cost_estimate=SMALL,
        name="weight_shares",
    )(
        jnp.reshape(core, (1,)).astype(jnp.int32),
        left,
        right,
        action_left,
        action_right,
        *([] if gains is None else [gains]),
    )


def stacked(refs, columns=slice(None)):
    return jnp.concatenate([ref[0, :, columns] for ref in refs], axis=0)


def softmax_of(queries, keys, bias, scale):
    scores = multiply_right(queries, keys) * scale + bias
    raised = jnp.exp(scores - jnp.max(scores, axis=-1, keepdims=True))
    return raised / jnp.sum(raised, axis=-1, keepdims=True)


def greet_copies():
    copies = lax.axis_size("dp")
    place, me = lax.axis_index("dp"), lax.axis_index("fsdp")
    barrier = pltpu.get_barrier_semaphore()
    for k in range(1, copies):
        pl.semaphore_signal(
            barrier,
            inc=1,
            device_id=(lax.rem(place + k, copies), me),
            device_id_type=pl.DeviceIdType.MESH,
        )
    pl.semaphore_wait(barrier, copies - 1)


def mix_kernel(
    scale,
    features,
    prefix_ref,
    action_ref,
    prefix_all_ref,
    action_all_ref,
    bias_ref,
    prefix_out,
    action_out,
    kv_out,
    held,
    send_sem,
    recv_sem,
    out_sem,
):
    copies = lax.axis_size("dp")
    place, me = lax.axis_index("dp"), lax.axis_index("fsdp")
    item, head = pl.program_id(0), pl.program_id(1)
    items, rows = prefix_all_ref.shape[0], prefix_ref.shape[1]

    def copy(at, k):
        return pltpu.make_async_remote_copy(
            src_ref=held.at[0, at],
            dst_ref=held.at[k, at],
            send_sem=send_sem.at[at, k],
            recv_sem=recv_sem.at[at, k],
            device_id=(lax.rem(place + k, copies), me),
            device_id_type=pl.DeviceIdType.MESH,
        )

    @pl.when((item == 0) & (head == 0))
    def _():
        for at in range(items):
            held[0, at, :rows] = prefix_all_ref[at, :, features:]
            held[0, at, rows:] = action_all_ref[at, :, features:]
        greet_copies()
        for at in range(items):
            for k in range(1, copies):
                copy(at, k).start()

    @pl.when(head == 0)
    def _():
        for k in range(1, copies):
            copy(item, k).wait_recv()

    queries = stacked((prefix_ref, action_ref))
    kv = jnp.concatenate([held[k, item] for k in range(copies)], axis=0)
    head_size = kv.shape[1] // 2
    probs = softmax_of(queries, kv[:, :head_size], bias_ref[0], scale).astype(LOW)
    mixed = multiply(probs, kv[:, head_size:]).astype(LOW)
    prefix_out[0] = mixed[:rows]
    action_out[0] = mixed[rows:]

    @pl.when((item == items - 1) & (head == pl.num_programs(1) - 1))
    def _():
        whole = pltpu.make_async_copy(held, kv_out, out_sem)
        whole.start()
        for at in range(items):
            for k in range(1, copies):
                copy(at, k).wait_send()
        whole.wait()


def mix_back_kernel(
    scale,
    prefix_ref,
    action_ref,
    prefix_grad_ref,
    action_grad_ref,
    bias_ref,
    kv_ref,
    prefix_out,
    action_out,
    kv_out,
    total,
    own,
    sent,
    arrived,
    send_sem,
    recv_sem,
):
    copies = lax.axis_size("dp")
    place, me = lax.axis_index("dp"), lax.axis_index("fsdp")
    item, head = pl.program_id(0), pl.program_id(1)
    items, heads = pl.num_programs(0), pl.num_programs(1)
    rows = prefix_ref.shape[1]
    step = rows + action_ref.shape[1]

    def copy(at, k):
        return pltpu.make_async_remote_copy(
            src_ref=sent.at[at, k - 1],
            dst_ref=arrived.at[at, k - 1],
            send_sem=send_sem.at[at, k],
            recv_sem=recv_sem.at[at, k],
            device_id=(lax.rem(place + copies - k, copies), me),
            device_id_type=pl.DeviceIdType.MESH,
        )

    @pl.when((item == 0) & (head == 0))
    def _():
        greet_copies()

    @pl.when(head == 0)
    def _():
        total[...] = jnp.zeros_like(total)

    queries = stacked((prefix_ref, action_ref))
    grads = stacked((prefix_grad_ref, action_grad_ref))
    kv = jnp.concatenate([kv_ref[k, 0] for k in range(copies)], axis=0)
    head_size = kv.shape[1] // 2
    keys, values = kv[:, :head_size], kv[:, head_size:]
    probs = softmax_of(queries, keys, bias_ref[0], scale)
    probs_grad = multiply_right(grads, values)
    delta = jnp.sum(probs * probs_grad, axis=-1, keepdims=True)
    score_grad = (probs * (probs_grad - delta)).astype(LOW)
    query_grad = (multiply(score_grad, keys) * scale).astype(LOW)
    prefix_out[0] = query_grad[:rows]
    action_out[0] = query_grad[rows:]
    total[:, :head_size] += multiply_left(score_grad, queries) * scale
    total[:, head_size:] += multiply_left(probs.astype(LOW), grads)

    @pl.when(head == heads - 1)
    def _():
        own[item] = total[:step]
        for k in range(1, copies):
            sent[item, k - 1] = total[k * step : (k + 1) * step].astype(LOW)
            copy(item, k).start()

    @pl.when((item == items - 1) & (head == heads - 1))
    def _():
        for at in range(kv_out.shape[0]):
            for k in range(1, copies):
                copy(at, k).wait_recv()
                copy(at, k).wait_send()
            summed = own[at]
            for k in range(1, copies):
                summed = summed + arrived[at, k - 1].astype(FULL)
            kv_out[at] = summed.astype(LOW)


def mix_call(scale, heads, prefix, action, bias, grads=None, kv=None):
    copies = lax.axis_size("dp")
    items, prefix_rows, columns = prefix.shape
    action_rows = action.shape[1]
    rows, length = prefix_rows + action_rows, bias.shape[2]
    head_size = columns // (heads + 2)
    features = heads * head_size
    per_head = [
        pl.BlockSpec((1, prefix_rows, head_size), lambda i, h: (i, 0, h)),
        pl.BlockSpec((1, action_rows, head_size), lambda i, h: (i, 0, h)),
    ]
    bias_spec = pl.BlockSpec((1, rows, length), lambda i, h: (i, 0, 0))
    shapes = [
        jax.ShapeDtypeStruct((items, prefix_rows, features), LOW),
        jax.ShapeDtypeStruct((items, action_rows, features), LOW),
    ]
    dma = pltpu.SemaphoreType.DMA
    sems = [dma((items, copies)), dma((items, copies))]
    block = (rows, 2 * head_size)
    if grads is None:
        return pl.pallas_call(
            functools.partial(mix_kernel, scale, features),
            out_shape=shapes + [jax.ShapeDtypeStruct((copies, items, *block), LOW)],
            grid=(items, heads),
            in_specs=per_head
            + [
                pl.BlockSpec(prefix.shape, lambda i, h: (0, 0, 0)),
                pl.BlockSpec(action.shape, lambda i, h: (0, 0, 0)),
                bias_spec,
            ],
            out_specs=per_head + [pl.BlockSpec(memory_space=pl.ANY)],
            scratch_shapes=[pltpu.VMEM((copies, items, *block), LOW), *sems, dma],
            compiler_params=pltpu.CompilerParams(
                collective_id=7, has_side_effects=True, vmem_limit_bytes=48 * MIB
            ),
            cost_estimate=SMALL,
            name="mix",
        )(prefix, action, prefix, action, bias)
    return pl.pallas_call(
        functools.partial(mix_back_kernel, scale),
        out_shape=shapes + [jax.ShapeDtypeStruct((items, *block), LOW)],
        grid=(items, heads),
        in_specs=per_head * 2
        + [bias_spec, pl.BlockSpec((copies, 1, *block), lambda i, h: (0, i, 0, 0))],
        out_specs=per_head + [pl.BlockSpec((items, *block), lambda i, h: (0, 0, 0))],
        scratch_shapes=[
            pltpu.VMEM((length, 2 * head_size), FULL),
            pltpu.VMEM((items, *block), FULL),
            pltpu.VMEM((items, copies - 1, *block), LOW),
            pltpu.VMEM((items, copies - 1, *block), LOW),
            *sems,
        ],
        compiler_params=pltpu.CompilerParams(
            collective_id=8, has_side_effects=True, vmem_limit_bytes=48 * MIB
        ),
        cost_estimate=SMALL,
        name="mix_back",
    )(prefix, action, *grads, bias, kv)


def body(
    prefix_in,
    action_in,
    valid_count,
    prefix_before,
    prefix_query,
    prefix_key,
    prefix_value,
    prefix_output,
    prefix_middle,
    prefix_gate,
    prefix_up,
    prefix_down,
    action_before,
    action_query,
    action_key,
    action_value,
    action_output,
    action_middle,
    action_gate,
    action_up,
    action_down,
    prefix_cotangent,
    action_cotangent,
):
    line = Line()
    shards = line.size
    copies = lax.axis_size("dp")
    items, prefix_rows, width = prefix_in.shape
    action_rows = action_in.shape[1]
    action_width = action_in.shape[2]
    head_size = prefix_key.shape[1]
    features = prefix_query.shape[1]
    heads = features // head_size
    columns = features + 2 * head_size
    prefix_length = prefix_rows * copies
    scale = head_size ** (-0.5)
    place = lax.axis_index("dp")
    prefix_pad, action_pad = rounded(prefix_rows), rounded(action_rows)
    prefix_tokens, action_tokens = items * prefix_pad, items * action_pad
    folded = action_tokens * action_width // width
    folded_pad = rounded(folded)

    def padded(prefix, action):
        prefix = jnp.pad(prefix, ((0, 0), (0, prefix_pad - prefix_rows), (0, 0)))
        action = jnp.pad(action, ((0, 0), (0, action_pad - action_rows), (0, 0)))
        return prefix.reshape(prefix_tokens, width), action.reshape(action_tokens, action_width)

    def trimmed(prefix, action):
        prefix = prefix.reshape(items, prefix_pad, width)[:, :prefix_rows]
        return prefix, action.reshape(items, action_pad, action_width)[:, :action_rows]

    def fold(action):
        rows = action.reshape(-1, folded, width)
        return jnp.pad(rows, ((0, 0), (0, folded_pad - folded), (0, 0)))

    def unfold(rows):
        return rows[:folded].reshape(action_tokens, action_width)

    def pack(prefix, action):
        return jnp.concatenate([prefix, fold(action)[0]], axis=0)

    def unpack(packed):
        return packed[:prefix_tokens], unfold(packed[prefix_tokens:])

    share, action_share = prefix_before.shape[0], action_before.shape[0]
    cuts = [0, share, 2 * share, 2 * share + action_share, 2 * share + 2 * action_share]
    gain_rows = rounded(-(-cuts[4] // 128))
    gains = jnp.concatenate([prefix_before, prefix_middle, action_before, action_middle])
    gains = jnp.pad(gains, (0, gain_rows * 128 - cuts[4])).reshape(gain_rows, 128)
    prefix_qkv, action_qkv, gains = gather_shards(
        0,
        jnp.concatenate([prefix_query, prefix_key, prefix_value], axis=1),
        jnp.concatenate([action_query, action_key, action_value], axis=1),
        gains,
    )
    gains = gains.reshape(shards, gain_rows * 128).astype(FULL)
    prefix_gain_in, prefix_gain, action_gain_in, action_gain = (
        gains[:, cuts[i] : cuts[i + 1]].reshape(-1) for i in range(4)
    )

    live = (place * action_rows + jnp.arange(action_rows))[None, :] < valid_count[:, None]
    prefix_back, action_back = padded(
        prefix_cotangent,
        jnp.where(live[:, :, None], action_cotangent, jnp.zeros_like(action_cotangent)),
    )
    backs = lax.all_gather(pack(prefix_back, action_back), "fsdp", axis=0, tiled=True)

    prefix_flat, action_flat = padded(prefix_in.astype(FULL), action_in.astype(FULL))
    prefix_hidden = normalize(prefix_flat, prefix_gain_in).astype(LOW)
    action_hidden = normalize(action_flat, action_gain_in).astype(LOW)
    prefix_all = multiply(prefix_hidden, prefix_qkv).astype(LOW)
    prefix_all = prefix_all.reshape(items, prefix_pad, columns)
    action_all = multiply(action_hidden, action_qkv).astype(LOW)
    action_all = action_all.reshape(items, action_pad, columns)
    far = copies * (prefix_rows + action_rows)

    def places(owner):
        prefix = jnp.arange(prefix_pad)
        action = jnp.arange(action_pad)
        return jnp.concatenate(
            [
                jnp.where(prefix < prefix_rows, owner * prefix_rows + prefix, far),
                jnp.where(
                    action < action_rows, prefix_length + owner * action_rows + action, far
                ),
            ]
        )

    query_place = places(place)
    key_place = jnp.concatenate([places((place + copies - k) % copies) for k in range(copies)])
    later = (query_place[:, None] >= prefix_length) & (key_place[None, :] <= query_place[:, None])
    allowed = (key_place[None, None, :] < prefix_length) | later[None] & (
        key_place[None, None, :] < prefix_length + valid_count[:, None, None]
    )
    bias = jnp.where(allowed, 0.0, NEGATIVE).astype(FULL)
    prefix_mixed, action_mixed, kv = mix_call(scale, heads, prefix_all, action_all, bias)
    backs, prefix_output, action_output, _ = lax.optimization_barrier(
        (backs, prefix_output, action_output, prefix_mixed)
    )
    prefix_o, action_o = gather_shards(4, prefix_output, action_output)

    prefix_mixed = prefix_mixed.reshape(prefix_tokens, features)
    action_mixed = action_mixed.reshape(action_tokens, features)
    prefix_mid = prefix_flat + multiply(prefix_mixed, prefix_o)
    action_mid = action_flat + multiply(action_mixed, action_o)

    hidden = pack(
        normalize(prefix_mid, prefix_gain).astype(LOW),
        normalize(action_mid, action_gain).astype(LOW),
    )
    inner, gate_grad, up_grad, all_rows, all_back, small = feed_all(
        prefix_tokens, hidden, backs, prefix_gate, prefix_up, prefix_down
    )
    action_rows_all, action_back_all = (
        small[i, :, :, :folded].reshape(shards * action_tokens, action_width) for i in range(2)
    )
    action_inner, pull = jax.vjp(
        activate, multiply(action_rows_all, action_gate), multiply(action_rows_all, action_up)
    )
    action_inner = action_inner.astype(LOW)
    action_gate_grad, action_up_grad = (
        v.astype(LOW) for v in pull(multiply_right(action_back_all, action_down))
    )

    down_grad = multiply_left(inner, all_back).astype(LOW)
    action_feed = tuple(
        v.astype(LOW)
        for v in (
            multiply_left(action_rows_all, action_gate_grad),
            multiply_left(action_rows_all, action_up_grad),
            multiply_left(action_inner, action_back_all),
        )
    )
    gate_weight_grad = multiply_left(all_rows, gate_grad).astype(LOW)
    gate_grad, up_grad, down_grad, gate_weight_grad = lax.optimization_barrier(
        (gate_grad, up_grad, down_grad, gate_weight_grad)
    )
    def halves(rows):
        return fold(rows.astype(LOW)).reshape(line.chips, 2, folded_pad, width)

    up_weight_grad = multiply_left(all_rows, up_grad).astype(LOW)
    gate_grad, up_grad, down_grad, gate_weight_grad, up_weight_grad, action_feed = (
        lax.optimization_barrier(
            (gate_grad, up_grad, down_grad, gate_weight_grad, up_weight_grad, action_feed)
        )
    )
    feed_sums = lax.psum((down_grad, gate_weight_grad, up_weight_grad, *action_feed), "dp")
    small = halves(
        multiply_right(action_gate_grad, action_gate) + multiply_right(action_up_grad, action_up)
    )
    feed_back = collect(
        2, prefix_tokens, True, (gate_grad, up_grad), (prefix_gate, prefix_up), small, width
    )
    feed_back, inner = lax.optimization_barrier((unpack(feed_back), inner))

    prefix_mid_grad, prefix_low, prefix_mixed_grad, prefix_middle_part = middle_back(
        feed_back[0], prefix_mid, prefix_back, prefix_gain, prefix_o
    )
    action_mid_grad, action_low, action_mixed_grad, action_middle_part = middle_back(
        feed_back[1], action_mid, action_back, action_gain, action_o
    )
    sent = line.pairs(9, prefix_mixed, prefix_low, action_mixed, action_low)
    output_sums = Relay(line, sent, lambda chip: chip)
    output_sums.advance(1)
    parts = part_chunks(
        prefix_tokens,
        lax.optimization_barrier((inner, sent))[0],
        prefix_down,
        halves(multiply(action_inner, action_down)),
    )
    sent = add_pairs(11, *parts)
    sent, mixed_grads = lax.optimization_barrier((sent, (prefix_mixed_grad, action_mixed_grad)))
    prefix_mixed_grad, action_mixed_grad = mixed_grads
    out_sums = Relay(line, sent, lambda chip: line.chip ^ chip)
    out_sums.advance(1)
    prefix_mixed_grad = output_sums.after(prefix_mixed_grad)
    output_sums.advance(2)
    mixed_grads = (
        prefix_mixed_grad.reshape(items, prefix_pad, features),
        action_mixed_grad.reshape(items, action_pad, features),
    )
    prefix_query_grad, action_query_grad, kv_grad = mix_call(
        scale, heads, prefix_all, action_all, bias, mixed_grads, kv
    )
    kv_grad = output_sums.after(out_sums.after(kv_grad))
    out_sums.advance(2)
    output_sums.advance(3)
    prefix_qkv_grad = jnp.concatenate([prefix_query_grad, kv_grad[:, :prefix_pad]], axis=2)
    action_qkv_grad = jnp.concatenate([action_query_grad, kv_grad[:, prefix_pad:]], axis=2)
    prefix_qkv_grad = prefix_qkv_grad.reshape(prefix_tokens, columns)
    action_qkv_grad = action_qkv_grad.reshape(action_tokens, columns)
    prefix_grad, prefix_before_part = entry_back(
        prefix_query_grad.reshape(prefix_tokens, features),
        kv_grad[:, :prefix_pad].reshape(prefix_tokens, 2 * head_size),
        prefix_flat,
        prefix_mid_grad,
        prefix_gain_in,
        prefix_qkv,
    )
    action_grad, action_before_part = entry_back(
        action_query_grad.reshape(action_tokens, features),
        kv_grad[:, prefix_pad:].reshape(action_tokens, 2 * head_size),
        action_flat,
        action_mid_grad,
        action_gain_in,
        action_qkv,
    )
    prefix_grad, action_grad = trimmed(prefix_grad, action_grad)

    gain_parts = jnp.concatenate(
        [
            part.reshape(shards, -1)
            for part in (
                prefix_before_part,
                prefix_middle_part,
                action_before_part,
                action_middle_part,
            )
        ],
        axis=1,
    )
    gain_rows = rounded(-(-cuts[4] // columns))
    gain_parts = jnp.pad(gain_parts, ((0, 0), (0, gain_rows * columns - cuts[4])))
    gain_parts = gain_parts.astype(LOW).reshape(shards, gain_rows, columns)
    sent = line.pairs(
        10, prefix_hidden, prefix_qkv_grad, action_hidden, action_qkv_grad, gain_parts
    )
    qkv_sums = Relay(line, out_sums.after(sent), lambda chip: chip)
    out_sums.advance(3)
    qkv_sums.advance(1)
    output_owned = output_sums.finish()
    qkv_sums.arrived, output_owned = out_sums.after((qkv_sums.arrived, output_owned))
    qkv_sums.advance(2)
    rows, output_rows = prefix_query.shape[0], prefix_output.shape[0]
    folded_rows = output_owned[output_rows:]
    folded_rows = jnp.concatenate(
        [folded_rows[:, i : i + action_width] for i in range(0, width, action_width)], axis=0
    )
    output_owned, action_output_owned = sum_copies(
        6, [output_owned[:output_rows].astype(LOW), folded_rows.astype(LOW)]
    )
    feed_sums, output_owned = qkv_sums.after((feed_sums, output_owned))
    qkv_sums.advance(3)
    sums = unpack(out_sums.finish())
    prefix_out, action_out = trimmed(
        (prefix_mid + sums[0]).astype(LOW), (action_mid + sums[1]).astype(LOW)
    )
    qkv_owned = qkv_sums.finish()
    gain_start = rows + action_query.shape[0]
    qkv_owned, action_qkv_owned, gain_owned = sum_copies(
        12,
        [
            qkv_owned[:rows].astype(LOW),
            qkv_owned[rows:gain_start].astype(LOW),
            qkv_owned[gain_start:].reshape(TILE * copies, -1).astype(LOW),
        ],
    )
    gain_owned = gain_owned.reshape(-1)
    return (
        prefix_out,
        action_out,
        prefix_grad,
        action_grad,
        gain_owned[cuts[0] : cuts[1]],
        qkv_owned[:rows, :features],
        qkv_owned[:rows, features : features + head_size],
        qkv_owned[:rows, features + head_size :],
        output_owned,
        gain_owned[cuts[1] : cuts[2]],
        widen(feed_sums[1]),
        widen(feed_sums[2]),
        widen(feed_sums[0]),
        gain_owned[cuts[2] : cuts[3]],
        action_qkv_owned[:, :features],
        action_qkv_owned[:, features : features + head_size],
        action_qkv_owned[:, features + head_size :],
        action_output_owned,
        gain_owned[cuts[3] : cuts[4]],
        *(widen(v) for v in feed_sums[3:]),
    )


def solution(mesh):
    tokens = P("fsdp", "dp", None)
    rows, columns, vector = P("fsdp", None), P(None, "fsdp"), P("fsdp")
    weights = (vector, rows, rows, rows, rows, vector, columns, columns, rows)
    return jax.shard_map(
        body,
        mesh=mesh,
        in_specs=(tokens, tokens, vector, *weights, *weights, tokens, tokens),
        out_specs=(tokens, tokens, tokens, tokens, *weights, *weights),
        check_vma=False,
    )
```

time: 1610 us -> 1280 us (0.80)
  waiting for transfers between devices: 558 us -> 71.2 us
  Pallas kernels: 434 us -> 846 us
  other arithmetic: 182 us -> 19.4 us
  matrix products: 186 us -> 144 us
  starting transfers between devices: 121 us -> 79.7 us
    pallas_call x14 -> x39, Pallas kernels: 298 us -> 672 us  [the longest x1 152 us: feed_all(): pl.pallas_call(functools.partial(feed_kernel, valid), out_shape=[jax.Shap...]
    psum x4 -> x1, waiting for transfers between devices: 250 us -> 0.01 us  [body(): lax.psum((down_grad, gate_weight_grad, up_weight_grad, *action_feed), 'dp')]
    ppermute x36 -> x18, waiting for transfers between devices: 296 us -> 71.2 us  [move(): return lax.ppermute(value, 'fsdp', pairs)]
    convert_element_type x26 -> x3, other arithmetic: 123 us -> 0.85 us  [the longest x1 0.75 us: body(): (prefix_mid + sums[0]).astype(LOW)]
    pallas_call x1 -> x2, Pallas kernels: 136 us -> 174 us  [gather_shards(): pl.pallas_call(functools.partial(gather_kernel, shares), out_shape=[jax.S...]
    ppermute x36 -> x18, starting transfers between devices: 109 us -> 79.7 us  [move(): return lax.ppermute(value, 'fsdp', pairs)]
    dot_general x10 -> x6, matrix products: 137 us -> 112 us  [multiply_left(): lax.dot_general(left, right, (((0,), (0,)), ((), ())), preferred_element_...]
    dot_general x7 -> x3, matrix products: 25.4 us -> 2.63 us  [multiply_right(): lax.dot_general(left, right, (((1,), (1,)), ((), ())), preferred_element_...]
  transfers between devices with their start and end apart: 65 -> 20, of which waited for: 23 -> 1; matrix products, arithmetic and copies ran while one was open for 22% -> 5% of each run, Pallas kernels for 15% -> 45%
where the time goes in v2:
time: 1280 us; the launch traced here: 1270 us
  Pallas kernels  846 us (66%)
  matrix products  144 us (11%)
  local copies, waits for them, and re-layouts  97 us (8%)
  starting transfers between devices  79.7 us (6%)
  waiting for transfers between devices  71.2 us (6%)
  other arithmetic  19.4 us (2%)
  between operations  15.9 us (1%)
    pallas_call x2, Pallas kernels, gather_shards(): pl.pallas_call(functools.partial(gather_kernel, shares), out_shape=[jax.S...  174 us
    pallas_call x1, Pallas kernels, feed_all(): pl.pallas_call(functools.partial(feed_kernel, valid), out_shape=[jax.Shap...  152 us
    pallas_call x1, Pallas kernels, collect(): pl.pallas_call(functools.partial(collect_kernel, valid, transposed, count...  146 us
    dot_general x6, matrix products, multiply_left(): lax.dot_general(left, right, (((0,), (0,)), ((), ())), preferred_element_...  112 us
    pallas_call x2, Pallas kernels, sum_copies(): pl.pallas_call(functools.partial(sum_kernel, split), out_shape=[jax.Shape...  81.9 us
    ppermute x18, starting transfers between devices, move(): return lax.ppermute(value, 'fsdp', pairs)  79.7 us
    unnamed x196, local copies, waits for them, and re-layouts  71.4 us
    ppermute x18, waiting for transfers between devices, move(): return lax.ppermute(value, 'fsdp', pairs)  71.2 us
  transfers between devices with their start and end apart: 20, of which 1 were waited for; matrix products, arithmetic and copies ran while one was open for 5% of the time, Pallas kernels for 45%

profile of v2, /device:TPU:0, one launch (start us, length us, event | category | flops | bytes accessed | tf_op | source)
XLA Modules:
  0.0 1273.1 jit_solution(11084623813589503188)
XLA Ops:
  17.2 108.5 %gather_shards.2 = (bf16[2048,2560]{1,0:T(8,128)(2,1)}, bf16[1024,2560]{1,0:T(8,128)(2,1)}, bf16[128,128]{1,0:T(8,128)(2,1)}) custom-call(bf16[256,2560]{1,0:T(8,128)(2,1)} %pad_maximum_fusion.3.refs_0_, bf16[128,2560]{1,0:T(8,128)(2,1)} %pad_maximum_fusion.4.refs_1_, bf16[16,128]{1,0:T(8,128)(2,1)} %fusion.23.refs_2_), custom_call_target="tpu_custom_call" | custom-call | flops 1 | bytes 1 | tf_op jit(solution)/shard_map/gather_shards/pallas_call | solution.py:385
  143.9 10.5 convolution_convert_fusion.3
  154.3 34.4 %mix.1 = (bf16[2,208,2048]{2,1,0:T(8,128)(2,1)S(1)}, bf16[2,16,2048]{2,1,0:T(8,128)(2,1)S(1)}, bf16[4,2,224,512]{3,2,1,0:T(8,128)(2,1)S(1)}) custom-call(bf16[2,208,2560]{2,1,0:T(8,128)(2,1)} %bitcast.142, bf16[2,16,2560]{2,1,0:T(8,128)(2,1)S(1)} %bitcast.129, bf16[2,208,2560]{2,1,0:T(8,128)(2,1)} %bitcast.143, bf16[2,16,2560]{2,1,0:T(8,128)(2,1)S(1)} %bitcast.130, ...), custom_call_target="tpu_custom_call" | custom-call | flops 1 | bytes 1 | tf_op jit(solution)/shard_map/mix/pallas_call | solution.py:1319
  191.2 65.0 %gather_shards.3 = (bf16[2048,2048]{1,0:T(8,128)(2,1)}, bf16[2048,1024]{1,0:T(8,128)(2,1)}) custom-call(bf16[256,2048]{1,0:T(8,128)(2,1)} %refs_0_, bf16[256,1024]{1,0:T(8,128)(2,1)} %refs_1_), custom_call_target="tpu_custom_call" | custom-call | flops 1 | bytes 1 | tf_op jit(solution)/shard_map/gather_shards/pallas_call | solution.py:385
  259.5 8.8 multiply_reduce_fusion
  271.4 152.3 %feed_all.1 = (bf16[3328,2048]{1,0:T(8,128)(2,1)}, bf16[3328,2048]{1,0:T(8,128)(2,1)}, bf16[3328,2048]{1,0:T(8,128)(2,1)}, bf16[3328,2048]{1,0:T(8,128)(2,1)}, b...) custom-call(bf16[432,2048]{1,0:T(8,128)(2,1)} %pad_maximum_fusion.2.hidden_ref, ...), custom_call_target="tpu_custom_call" | custom-call | flops 1 | bytes 1 | tf_op jit(solution)/shard_map/feed_all/pallas_call | solution.py:636
  423.7 36.8 %convolution_convert_fusion.2 = bf16[2048,2048]{1,0:T(8,128)(2,1)} fusion(bf16[3328,2048]{1,0:T(8,128)(2,1)} %get-tuple-element.133.inner_ref, bf16[3328,2048]{1,0:T(8,128)(2,1)} %get-tuple-element.119), kind=kOutput, calls=%fused_computation.2 | convolution fusion | flops 27921481728 | bytes 35651584 | tf_op jit(solution)/shard_map/dot_general | solution.py:29
  460.5 34.2 %convolution_convert_fusion.1 = bf16[2048,2048]{1,0:T(8,128)(2,1)} fusion(bf16[3328,2048]{1,0:T(8,128)(2,1)} %get-tuple-element.120, bf16[3328,2048]{1,0:T(8,128)(2,1)S(1)} %copy-done.55), kind=kOutput, calls=%fused_computation.1 | convolution fusion | flops 27921481728 | bytes 35651584 | tf_op jit(solution)/shard_map/dot_general | solution.py:29
  494.7 36.7 %convolution_convert_fusion = bf16[2048,2048]{1,0:T(8,128)(2,1)} fusion(bf16[3328,2048]{1,0:T(8,128)(2,1)} %get-tuple-element.120, bf16[3328,2048]{1,0:T(8,128)(2,1)} %get-tuple-element.127.refs_1_), kind=kOutput, calls=%fused_computation | convolution fusion | flops 27921481728 | bytes 35651584 | tf_op jit(solution)/shard_map/dot_general | solution.py:29
  543.6 145.7 %collect.1 = f32[432,2048]{1,0:T(8,128)} custom-call(bf16[3328,2048]{1,0:T(8,128)(2,1)} %get-tuple-element.126.refs_0_, bf16[3328,2048]{1,0:T(8,128)(2,1)} %get-tuple-element.127.refs_1_, bf16[2048,2048]{1,0:T(8,128)(2,1)} %refs_2_.1, bf16[2048,2048]{1,0:T(8,128)(2,1)} %refs_3_.1, bf16[4,2,16,2048]{3,2,1,0:T(8,128)(2,1)} %reshape.428.refs_4_), custom_call_target="tpu_custom_call" | custom-call | flops 1 | bytes 1 | tf_op jit(solution)/shard_map/collect/pallas_call | solution.py:814
  694.3 13.3 %middle_back.2 = (f32[416,2048]{1,0:T(8,128)}, bf16[416,2048]{1,0:T(8,128)(2,1)}, bf16[416,2048]{1,0:T(8,128)(2,1)}, f32[1,2048]{1,0:T(1,128)}) custom-call(f32[416,2048]{1,0:T(8,128)} %slice.113.grad_ref, f32[416,2048]{1,0:T(8,128)} %copy-done.51, bf16[416,2048]{1,0:T(8,128)(2,1)} %bitcast.146, f32[1,2048]{1,0:T(1,128)} %bitcast.159, ...), custom_call_target="tpu_custom_call" | custom-call | flops 1 | bytes 1 | tf_op jit(solution)/shard_map/middle_back/pallas_call | solution.py:892
  727.0 10.8 add_pairs.3.value_ref
  748.1 38.6 %part_chunks.1 = (bf16[4,432,2048]{2,1,0:T(8,128)(2,1)}, bf16[4,432,2048]{2,1,0:T(8,128)(2,1)}) custom-call(bf16[3328,2048]{1,0:T(8,128)(2,1)} %get-tuple-element.133.inner_ref, bf16[2048,2048]{1,0:T(8,128)(2,1)} %down_ref.3, bf16[4,2,16,2048]{3,2,1,0:T(8,128)(2,1)S(1)} %reshape.433.small_ref), custom_call_target="tpu_custom_call" | custom-call | flops 1 | bytes 1 | tf_op jit(solution)/shard_map/part_chunks/pallas_call | solution.py:852
  789.7 12.0 add_pairs.4.value_ref
  826.7 55.8 %mix_back.1 = (bf16[2,208,2048]{2,1,0:T(8,128)(2,1)S(1)}, bf16[2,16,2048]{2,1,0:T(8,128)(2,1)S(1)}, bf16[2,224,512]{2,1,0:T(8,128)(2,1)S(1)}) custom-call(bf16[2,208,2560]{2,1,0:T(8,128)(2,1)} %bitcast.144, bf16[2,16,2560]{2,1,0:T(8,128)(2,1)S(1)} %bitcast.131, bf16[2,208,2048]{2,1,0:T(8,128)(2,1)S(1)} %bitcast.132, bf16[2,16,2048]{2,1,0:T(8,128)(2,1)S(1)} %bitcast.139, ...), custom_call_target="tpu_custom_call" | custom-call | flops 1 | bytes 1 | tf_op jit(solution)/shard_map/mix_back/pallas_call | solution.py:1337
  896.0 14.7 %entry_back.2 = (f32[416,2048]{1,0:T(8,128)}, f32[1,2048]{1,0:T(1,128)}) custom-call(bf16[416,2048]{1,0:T(8,128)(2,1)} %bitcast.126, bf16[416,512]{1,0:T(8,128)(2,1)} %bitcast.148, f32[416,2048]{1,0:T(8,128)} %bitcast.141, f32[416,2048]{1,0:T(8,128)} %get-tuple-element.152.total_ref, f32[1,2048]{1,0:T(1,128)} %bitcast.158, ...), custom_call_target="tpu_custom_call" | custom-call | flops 1 | bytes 1 | tf_op jit(solution)/shard_map/entry_back/pallas_call | solution.py:930
  936.3 15.2 %add_pairs.5.value_ref = bf16[4,400,2560]{2,1,0:T(8,128)(2,1)S(1)} custom-call(bf16[4,400,2560]{2,1,0:T(8,128)(2,1)} %weight_shares.6.mine_ref, bf16[4,400,2560]{2,1,0:T(8,128)(2,1)} %weight_shares.7.other_ref), custom_call_target="tpu_custom_call" | custom-call | flops 1 | bytes 1 | tf_op jit(solution)/shard_map/add_pairs/pallas_call | solution.py:156
  975.7 71.1 %collective-permute-done.13.refs_1_ = bf16[384,2048]{1,0:T(8,128)(2,1)S(1)} collective-permute-done((bf16[384,2048]{1,0:T(8,128)(2,1)S(1)}, bf16[384,2048]{1,0:T(8,128)(2,1)S(1)}, u32[]{:S(2)}, u32[]{:S(2)}) %collective-permute-start.13) | collective-permute-done | bytes 1572896 | tf_op jit(solution)/shard_map/ppermute | solution.py:56
  1067.0 36.4 %sum_copies.2 = (f32[256,2048]{1,0:T(8,128)S(1)}, f32[256,1024]{1,0:T(8,128)S(1)}) custom-call(bf16[256,2048]{1,0:T(8,128)(2,1)S(1)} %slice.149.refs_0_, bf16[256,1024]{1,0:T(8,128)(2,1)S(1)} %pad_maximum_fusion.5.refs_1_), custom_call_target="tpu_custom_call" | custom-call | flops 1 | bytes 1 | tf_op jit(solution)/shard_map/sum_copies/pallas_call | solution.py:1033
  1113.8 42.4 %collective-permute-start.16 = (bf16[400,2560]{1,0:T(8,128)(2,1)}, bf16[400,2560]{1,0:T(8,128)(2,1)}, u32[]{:S(2)}, u32[]{:S(2)}) collective-permute-start(bf16[400,2560]{1,0:T(8,128)(2,1)} %add_block.27), channel_id=1, source_target_pairs={{0,2},{1,3},{2,4},{3,5},{4,6},{5,7},{8,10},{9,11},{10,12},{11,13},... | collective-permute-start | bytes 6144008 | tf_op jit(solution)/shard_map/ppermute | solution.py:56
  1177.8 7.1 widen.6
  1188.2 7.1 widen.7
  1195.3 6.5 widen.8
  1210.8 45.5 %sum_copies.3 = (f32[256,2560]{1,0:T(8,128)S(1)}, f32[128,2560]{1,0:T(8,128)S(1)}, f32[64,640]{1,0:T(8,128)S(1)}) custom-call(bf16[256,2560]{1,0:T(8,128)(2,1)S(1)} %slice.152.refs_0_, bf16[128,2560]{1,0:T(8,128)(2,1)S(1)} %slice.153.refs_1_, bf16[64,640]{1,0:T(8,128)(2,1)S(1)} %convert_element_type.106.refs_2_), custom_call_target="tpu_custom_call" | custom-call | flops 1 | bytes 1 | tf_op jit(solution)/shard_map/sum_copies/pallas_call | solution.py:1033
  (362 shorter events, 247.9 us)
Async XLA Ops:
  7.2 528.0 %copy-start = (bf16[1024,512]{1,0:T(8,128)(2,1)S(1)}, bf16[1024,512]{1,0:T(8,128)(2,1)}, u32[]{:S(2)}) copy-start(bf16[1024,512]{1,0:T(8,128)(2,1)} %param.42) | copy-start | bytes 3145732
  7.2 184.0 %all-gather.2.cloned.1.call-start = ((), (), s32[]{:S(2)}) async-start(), calls=%async_computation | async-start | bytes 15925248 | tf_op jit(solution)/shard_map/all_gather | solution.py:1445
  14.0 1093.0 %all-reduce.9.cloned.1.call-start = ((), (), s32[]{:S(2)}) async-start(), calls=%async_computation.1 | async-start | bytes 56623104 | tf_op jit(solution)/shard_map/psum | solution.py:1526
  137.7 118.5 %copy-start.61 = (f32[2,16,1024]{2,1,0:T(8,128)}, f32[2,16,1024]{2,1,0:T(8,128)S(1)}, u32[]{:S(2)}) copy-start(f32[2,16,1024]{2,1,0:T(8,128)S(1)} %copy.77) | copy-start | bytes 393220
  191.2 68.2 %copy-start.36 = (bf16[2,16,2048]{2,1,0:T(8,128)(2,1)}, bf16[2,16,2048]{2,1,0:T(8,128)(2,1)S(1)}, u32[]{:S(2)}) copy-start(bf16[2,16,2048]{2,1,0:T(8,128)(2,1)S(1)} %get-tuple-element.113) | copy-start | bytes 393220
  741.4 67.9 %collective-permute-start.2 = (bf16[384,2048]{1,0:T(8,128)(2,1)}, bf16[384,2048]{1,0:T(8,128)(2,1)}, u32[]{:S(2)}, u32[]{:S(2)}) collective-permute-start(bf16[384,2048]{1,0:T(8,128)(2,1)} %get-tuple-element.203), channel_id=1, source_target_pairs={{0,2},{1,3},{8,10},{9,11},{16,18},{17,19},{24,26},{25,27}} | collective-permute-start | bytes 4718600 | tf_op jit(solution)/shard_map/ppermute | solution.py:56
  745.6 63.7 %collective-permute-start.3 = (bf16[384,2048]{1,0:T(8,128)(2,1)}, bf16[384,2048]{1,0:T(8,128)(2,1)}, u32[]{:S(2)}, u32[]{:S(2)}) collective-permute-start(bf16[384,2048]{1,0:T(8,128)(2,1)} %get-tuple-element.202), channel_id=1, source_target_pairs={{6,4},{7,5},{14,12},{15,13},{22,20},{23,21},{30,28},{31,29}} | collective-permute-start | bytes 4718600 | tf_op jit(solution)/shard_map/ppermute | solution.py:56
  805.7 76.8 %collective-permute-start = (bf16[432,2048]{1,0:T(8,128)(2,1)}, bf16[432,2048]{1,0:T(8,128)(2,1)}, u32[]{:S(2)}, u32[]{:S(2)}) collective-permute-start(bf16[432,2048]{1,0:T(8,128)(2,1)} %get-tuple-element.201), channel_id=1, source_target_pairs={{0,2},{1,3},{8,10},{9,11},{16,18},{17,19},{24,26},{25,27}} | collective-permute-start | bytes 5308424 | tf_op jit(solution)/shard_map/ppermute | solution.py:56
  808.6 74.0 %collective-permute-start.1 = (bf16[432,2048]{1,0:T(8,128)(2,1)}, bf16[432,2048]{1,0:T(8,128)(2,1)S(1)}, u32[]{:S(2)}, u32[]{:S(2)}) collective-permute-start(bf16[432,2048]{1,0:T(8,128)(2,1)} %get-tuple-element.200), channel_id=1, source_target_pairs={{6,4},{7,5},{14,12},{15,13},{22,20},{23,21},{30,28},{31,29}} | collective-permute-start | bytes 5308424 | tf_op jit(solution)/shard_map/ppermute | solution.py:56
  815.4 74.8 %collective-permute-start.6 = (bf16[384,2048]{1,0:T(8,128)(2,1)}, bf16[384,2048]{1,0:T(8,128)(2,1)}, u32[]{:S(2)}, u32[]{:S(2)}) collective-permute-start(bf16[384,2048]{1,0:T(8,128)(2,1)} %add_block.17), channel_id=1, source_target_pairs={{0,2},{1,3},{2,4},{3,5},{8,10},{9,11},{10,12},{11,13},{16,18},{17,... | collective-permute-start | bytes 4718600 | tf_op jit(solution)/shard_map/ppermute | solution.py:56
  820.9 69.4 %collective-permute-start.7 = (bf16[384,2048]{1,0:T(8,128)(2,1)}, bf16[384,2048]{1,0:T(8,128)(2,1)}, u32[]{:S(2)}, u32[]{:S(2)}) collective-permute-start(bf16[384,2048]{1,0:T(8,128)(2,1)} %add_block.18), channel_id=1, source_target_pairs={{4,2},{5,3},{6,4},{7,5},{12,10},{13,11},{14,12},{15,13},{20,18},{2... | collective-permute-start | bytes 4718600 | tf_op jit(solution)/shard_map/ppermute | solution.py:56
  886.4 65.1 %collective-permute-start.4 = (bf16[432,2048]{1,0:T(8,128)(2,1)}, bf16[432,2048]{1,0:T(8,128)(2,1)S(1)}, u32[]{:S(2)}, u32[]{:S(2)}) collective-permute-start(bf16[432,2048]{1,0:T(8,128)(2,1)} %add_block.15), channel_id=1, source_target_pairs={{0,2},{1,3},{2,4},{3,5},{8,10},{9,11},{10,12},{11,13},{16,18},{17,... | collective-permute-start | bytes 5308424 | tf_op jit(solution)/shard_map/ppermute | solution.py:56
  889.4 62.1 %collective-permute-start.5 = (bf16[432,2048]{1,0:T(8,128)(2,1)}, bf16[432,2048]{1,0:T(8,128)(2,1)S(1)}, u32[]{:S(2)}, u32[]{:S(2)}) collective-permute-start(bf16[432,2048]{1,0:T(8,128)(2,1)} %add_block.16), channel_id=1, source_target_pairs={{4,2},{5,3},{6,4},{7,5},{12,10},{13,11},{14,12},{15,13},{20,18},{2... | collective-permute-start | bytes 5308424 | tf_op jit(solution)/shard_map/ppermute | solution.py:56
  918.4 55.9 %collective-permute-start.12 = (bf16[384,2048]{1,0:T(8,128)(2,1)}, bf16[384,2048]{1,0:T(8,128)(2,1)}, u32[]{:S(2)}, u32[]{:S(2)}) collective-permute-start(bf16[384,2048]{1,0:T(8,128)(2,1)} %add_block.21), channel_id=1, source_target_pairs={{0,2},{1,3},{2,4},{3,5},{4,6},{5,7},{8,10},{9,11},{10,12},{11,13},... | collective-permute-start | bytes 4718600 | tf_op jit(solution)/shard_map/ppermute | solution.py:56
  956.0 99.5 %collective-permute-start.10 = (bf16[400,2560]{1,0:T(8,128)(2,1)}, bf16[400,2560]{1,0:T(8,128)(2,1)}, u32[]{:S(2)}, u32[]{:S(2)}) collective-permute-start(bf16[400,2560]{1,0:T(8,128)(2,1)} %get-tuple-element.199), channel_id=1, source_target_pairs={{0,2},{1,3},{8,10},{9,11},{16,18},{17,19},{24,26},{25,27}} | collective-permute-start | bytes 6144008 | tf_op jit(solution)/shard_map/ppermute | solution.py:56
  960.8 94.6 %collective-permute-start.11 = (bf16[400,2560]{1,0:T(8,128)(2,1)}, bf16[400,2560]{1,0:T(8,128)(2,1)}, u32[]{:S(2)}, u32[]{:S(2)}) collective-permute-start(bf16[400,2560]{1,0:T(8,128)(2,1)} %get-tuple-element.198), channel_id=1, source_target_pairs={{6,4},{7,5},{14,12},{15,13},{22,20},{23,21},{30,28},{31,29}} | collective-permute-start | bytes 6144008 | tf_op jit(solution)/shard_map/ppermute | solution.py:56
  967.7 86.6 %collective-permute-start.8 = (bf16[432,2048]{1,0:T(8,128)(2,1)}, bf16[432,2048]{1,0:T(8,128)(2,1)S(1)}, u32[]{:S(2)}, u32[]{:S(2)}) collective-permute-start(bf16[432,2048]{1,0:T(8,128)(2,1)} %add_block.19), channel_id=1, source_target_pairs={{0,2},{1,3},{2,4},{3,5},{4,6},{5,7},{8,10},{9,11},{10,12},{11,13},... | collective-permute-start | bytes 5308424 | tf_op jit(solution)/shard_map/ppermute | solution.py:56
  970.8 84.7 %collective-permute-start.9 = (bf16[432,2048]{1,0:T(8,128)(2,1)}, bf16[432,2048]{1,0:T(8,128)(2,1)}, u32[]{:S(2)}, u32[]{:S(2)}) collective-permute-start(bf16[432,2048]{1,0:T(8,128)(2,1)} %add_block.20), channel_id=1, source_target_pairs={{2,0},{3,1},{4,2},{5,3},{6,4},{7,5},{10,8},{11,9},{12,10},{13,11},... | collective-permute-start | bytes 5308424 | tf_op jit(solution)/shard_map/ppermute | solution.py:56
  972.2 83.3 %slice-start = ((s8[8192000]{0:T(1024)(128)(4,1)}), s8[4194304]{0:T(1024)(128)(4,1)S(1)}, s32[]{:S(2)}) async-start(s8[8192000]{0:T(1024)(128)(4,1)} %bitcast.113), calls=%async_computation.2 | async-start | bytes 8388608
  974.3 72.6 %collective-permute-start.13 = (bf16[384,2048]{1,0:T(8,128)(2,1)S(1)}, bf16[384,2048]{1,0:T(8,128)(2,1)S(1)}, u32[]{:S(2)}, u32[]{:S(2)}) collective-permute-start(bf16[384,2048]{1,0:T(8,128)(2,1)S(1)} %add_block.22), channel_id=1, source_target_pairs={{2,0},{3,1},{4,2},{5,3},{6,4},{7,5},{10,8},{11,9},{12,10},{13,11},... | collective-permute-start | bytes 4718600 | tf_op jit(solution)/shard_map/ppermute | solution.py:56
  1058.9 46.8 %collective-permute-start.14 = (bf16[400,2560]{1,0:T(8,128)(2,1)}, bf16[400,2560]{1,0:T(8,128)(2,1)}, u32[]{:S(2)}, u32[]{:S(2)}) collective-permute-start(bf16[400,2560]{1,0:T(8,128)(2,1)} %add_block.25), channel_id=1, source_target_pairs={{0,2},{1,3},{2,4},{3,5},{8,10},{9,11},{10,12},{11,13},{16,18},{17,... | collective-permute-start | bytes 6144008 | tf_op jit(solution)/shard_map/ppermute | solution.py:56
  1065.8 39.9 %collective-permute-start.15 = (bf16[400,2560]{1,0:T(8,128)(2,1)}, bf16[400,2560]{1,0:T(8,128)(2,1)S(1)}, u32[]{:S(2)}, u32[]{:S(2)}) collective-permute-start(bf16[400,2560]{1,0:T(8,128)(2,1)} %add_block.26), channel_id=1, source_target_pairs={{4,2},{5,3},{6,4},{7,5},{12,10},{13,11},{14,12},{15,13},{20,18},{2... | collective-permute-start | bytes 6144008 | tf_op jit(solution)/shard_map/ppermute | solution.py:56
  1113.8 93.1 %collective-permute-start.16 = (bf16[400,2560]{1,0:T(8,128)(2,1)}, bf16[400,2560]{1,0:T(8,128)(2,1)}, u32[]{:S(2)}, u32[]{:S(2)}) collective-permute-start(bf16[400,2560]{1,0:T(8,128)(2,1)} %add_block.27), channel_id=1, source_target_pairs={{0,2},{1,3},{2,4},{3,5},{4,6},{5,7},{8,10},{9,11},{10,12},{11,13},... | collective-permute-start | bytes 6144008 | tf_op jit(solution)/shard_map/ppermute | solution.py:56
  1158.1 48.8 %collective-permute-start.17 = (bf16[400,2560]{1,0:T(8,128)(2,1)}, bf16[400,2560]{1,0:T(8,128)(2,1)}, u32[]{:S(2)}, u32[]{:S(2)}) collective-permute-start(bf16[400,2560]{1,0:T(8,128)(2,1)} %add_block.28), channel_id=1, source_target_pairs={{2,0},{3,1},{4,2},{5,3},{6,4},{7,5},{10,8},{11,9},{12,10},{13,11},... | collective-permute-start | bytes 6144008 | tf_op jit(solution)/shard_map/ppermute | solution.py:56
  (88 other events, 617.2 us)
Sparse Core Ops, SparseCore 0:
  14.1 156.8 all-gather.1
  540.5 518.8 all-reduce.8

commit v3 on v2

--- a/solution.py
+++ b/solution.py
@@ -172,235 +172,250 @@
     return -(-count // unit) * unit
 
 
-def gather_kernel(shares, *refs):
-    count = len(shares)
-    shards, wholes = refs[:count], refs[count : 2 * count]
-    local_sem, pair_send, pair_recv = refs[2 * count : 2 * count + 3]
-    line_send, line_recv, copy_send, copy_recv, core_send, core_recv = refs[2 * count + 3 :]
-    mesh = pl.DeviceIdType.MESH
-    copies = lax.axis_size("dp")
-    place = lax.axis_index("dp")
-    size = lax.axis_size("fsdp")
-    chips = size // 2
-    me = lax.axis_index("fsdp")
-    chip, core = me // 2, me % 2
-    partner = 2 * chip + 1 - core
-    has_left, has_right = chip > 0, chip < chips - 1
-
-    barrier = pltpu.get_barrier_semaphore()
-    pl.semaphore_signal(barrier, inc=1, device_id=(place, partner), device_id_type=mesh)
-    for k in range(1, copies):
-        peer = lax.rem(place + k, copies)
-        pl.semaphore_signal(barrier, inc=1, device_id=(peer, me), device_id_type=mesh)
-
-    @pl.when(has_left)
-    def _():
-        pl.semaphore_signal(barrier, inc=1, device_id=(place, me - 2), device_id_type=mesh)
-
-    @pl.when(has_right)
-    def _():
-        pl.semaphore_signal(barrier, inc=1, device_id=(place, me + 2), device_id_type=mesh)
-
-    neighbours = jnp.minimum(chip, 1) + jnp.minimum(chips - 1 - chip, 1)
-    pl.semaphore_wait(barrier, copies + neighbours)
-
-    def rows(a, owner, share):
-        whole = shards[a].shape[0]
-        part = whole // shares[a]
+class Gather:
+    def __init__(self, shares, shards, wholes, sems):
+        self.shares, self.shards, self.wholes = shares, shards, wholes
+        self.local_sem, self.pair_send, self.pair_recv = sems[:3]
+        self.line_send, self.line_recv, self.copy_send, self.copy_recv = sems[3:7]
+        self.core_send, self.core_recv = sems[7:]
+        self.copies, self.place = lax.axis_size("dp"), lax.axis_index("dp")
+        self.chips, self.me = lax.axis_size("fsdp") // 2, lax.axis_index("fsdp")
+        self.chip, self.core = self.me // 2, self.me % 2
+        self.partner = 2 * self.chip + 1 - self.core
+
+    @staticmethod
+    def scratch(count):
+        dma = pltpu.SemaphoreType.DMA
+        copies, chips = lax.axis_size("dp"), lax.axis_size("fsdp") // 2
+        return (
+            [dma((count,))] * 3 + [dma((count, 2, chips))] * 2 + [dma((count, 2, chips, copies))] * 4
+        )
+
+    def greet(self):
+        mesh = pl.DeviceIdType.MESH
+        place, me, chip = self.place, self.me, self.chip
+        barrier = pltpu.get_barrier_semaphore()
+        pl.semaphore_signal(barrier, inc=1, device_id=(place, self.partner), device_id_type=mesh)
+        for k in range(1, self.copies):
+            peer = lax.rem(place + k, self.copies)
+            pl.semaphore_signal(barrier, inc=1, device_id=(peer, me), device_id_type=mesh)
+
+        @pl.when(chip > 0)
+        def _():
+            pl.semaphore_signal(barrier, inc=1, device_id=(place, me - 2), device_id_type=mesh)
+
+        @pl.when(chip < self.chips - 1)
+        def _():
+            pl.semaphore_signal(barrier, inc=1, device_id=(place, me + 2), device_id_type=mesh)
+
+        neighbours = jnp.minimum(chip, 1) + jnp.minimum(self.chips - 1 - chip, 1)
+        pl.semaphore_wait(barrier, self.copies + neighbours)
+
+    def rows(self, a, owner, share):
+        whole = self.shards[a].shape[0]
+        part = whole // self.shares[a]
         return pl.ds(pl.multiple_of(owner * whole + share * part, TILE), part)
 
-    def remote(source, target, send, recv, device):
+    def remote(self, source, target, send, recv, device):
         return pltpu.make_async_remote_copy(
             src_ref=source,
             dst_ref=target,
             send_sem=send,
             recv_sem=recv,
             device_id=device,
-            device_id_type=mesh,
-        )
-
-    def my_share(a):
-        return place if shares[a] > 1 else 0
-
-    def line_copy(a, side, step):
-        owner = me - 2 * step if side == 0 else me + 2 * step
-        where = rows(a, owner, my_share(a))
-        target = me + 2 if side == 0 else me - 2
-        return remote(
-            wholes[a].at[where],
-            wholes[a].at[where],
-            line_send.at[a, side, step],
-            line_recv.at[a, side, step],
-            (place, target),
-        )
-
-    def first_copy(a, side):
-        part = shards[a].shape[0] // shares[a]
-        target = me + 2 if side == 0 else me - 2
-        return remote(
-            shards[a].at[pl.ds(pl.multiple_of(my_share(a) * part, TILE), part)],
-            wholes[a].at[rows(a, me, my_share(a))],
-            line_send.at[a, side, 0],
-            line_recv.at[a, side, 0],
-            (place, target),
-        )
-
-    def owner_of(side, step):
-        return me - 2 * step if side == 0 else me + 2 * step
-
-    def peer_copy(a, side, step, k):
-        where = rows(a, owner_of(side, step), place)
-        return remote(
-            wholes[a].at[where],
-            wholes[a].at[where],
-            copy_send.at[a, side, step, k],
-            copy_recv.at[a, side, step, k],
-            (lax.rem(place + k, copies), me),
-        )
-
-    def core_copy(a, side, step, k):
-        share = lax.rem(place + copies - k, copies) if shares[a] > 1 else 0
-        where = rows(a, owner_of(side, step), share)
-        return remote(
-            wholes[a].at[where],
-            wholes[a].at[where],
-            core_send.at[a, side, step, k],
-            core_recv.at[a, side, step, k],
-            (place, partner),
-        )
-
-    def pair_copy(a):
-        return remote(
-            shards[a],
-            wholes[a].at[rows_all(a)],
-            pair_send.at[a],
-            pair_recv.at[a],
-            (place, partner),
-        )
-
-    def rows_all(a):
-        whole = shards[a].shape[0]
-        return pl.ds(pl.multiple_of(me * whole, TILE), whole)
-
-    def local_copy(a):
-        return pltpu.make_async_copy(shards[a], wholes[a].at[rows_all(a)], local_sem.at[a])
-
-    def sends(side):
-        return has_right if side == 0 else has_left
-
-    def has(side, step):
-        return chip >= step if side == 0 else chip + step <= chips - 1
-
-    for a in range(count):
-        for side in range(2):
-
-            @pl.when(sends(side))
-            def _(a=a, side=side):
-                first_copy(a, side).start()
-
-    for a in range(count):
-        pair_copy(a).start()
-        local_copy(a).start()
-
-    def peers(a):
-        return range(1, copies) if shares[a] > 1 else range(0)
-
-    def hand_over(a, side, step):
-        for k in peers(a):
-            peer_copy(a, side, step, k).wait_recv()
-            core_copy(a, side, step, k).start()
+            device_id_type=pl.DeviceIdType.MESH,
+        )
+
+    def my_share(self, a):
+        return self.place if self.shares[a] > 1 else 0
+
+    def peers(self, a):
+        return range(1, self.copies) if self.shares[a] > 1 else range(0)
+
+    def owner_of(self, side, step):
+        return self.me - 2 * step if side == 0 else self.me + 2 * step
+
+    def sends(self, side):
+        return self.chip < self.chips - 1 if side == 0 else self.chip > 0
+
+    def has(self, side, step):
+        return self.chip >= step if side == 0 else self.chip + step <= self.chips - 1
+
+    def line_copy(self, a, side, step):
+        where = self.rows(a, self.owner_of(side, step), self.my_share(a))
+        target = self.me + 2 if side == 0 else self.me - 2
+        return self.remote(
+            self.wholes[a].at[where],
+            self.wholes[a].at[where],
+            self.line_send.at[a, side, step],
+            self.line_recv.at[a, side, step],
+            (self.place, target),
+        )
+
+    def first_copy(self, a, side):
+        part = self.shards[a].shape[0] // self.shares[a]
+        target = self.me + 2 if side == 0 else self.me - 2
+        return self.remote(
+            self.shards[a].at[pl.ds(pl.multiple_of(self.my_share(a) * part, TILE), part)],
+            self.wholes[a].at[self.rows(a, self.me, self.my_share(a))],
+            self.line_send.at[a, side, 0],
+            self.line_recv.at[a, side, 0],
+            (self.place, target),
+        )
+
+    def peer_copy(self, a, side, step, k):
+        where = self.rows(a, self.owner_of(side, step), self.place)
+        return self.remote(
+            self.wholes[a].at[where],
+            self.wholes[a].at[where],
+            self.copy_send.at[a, side, step, k],
+            self.copy_recv.at[a, side, step, k],
+            (lax.rem(self.place + k, self.copies), self.me),
+        )
+
+    def core_copy(self, a, side, step, k):
+        share = lax.rem(self.place + self.copies - k, self.copies) if self.shares[a] > 1 else 0
+        where = self.rows(a, self.owner_of(side, step), share)
+        return self.remote(
+            self.wholes[a].at[where],
+            self.wholes[a].at[where],
+            self.core_send.at[a, side, step, k],
+            self.core_recv.at[a, side, step, k],
+            (self.place, self.partner),
+        )
+
+    def rows_all(self, a):
+        whole = self.shards[a].shape[0]
+        return pl.ds(pl.multiple_of(self.me * whole, TILE), whole)
+
+    def pair_copy(self, a):
+        return self.remote(
+            self.shards[a],
+            self.wholes[a].at[self.rows_all(a)],
+            self.pair_send.at[a],
+            self.pair_recv.at[a],
+            (self.place, self.partner),
+        )
+
+    def local_copy(self, a):
+        return pltpu.make_async_copy(
+            self.shards[a], self.wholes[a].at[self.rows_all(a)], self.local_sem.at[a]
+        )
+
+    def start(self):
+        for a in range(len(self.shards)):
+            for side in range(2):
+
+                @pl.when(self.sends(side))
+                def _(a=a, side=side):
+                    self.first_copy(a, side).start()
+
+        for a in range(len(self.shards)):
+            self.pair_copy(a).start()
+            self.local_copy(a).start()
+
+    def hand_over(self, a, side, step):
+        for k in self.peers(a):
+            self.peer_copy(a, side, step, k).wait_recv()
+            self.core_copy(a, side, step, k).start()
+
+    def advance(self, step):
+        for a in range(len(self.shards)):
+            for side in range(2):
+
+                @pl.when(self.has(side, step))
+                def _(a=a, side=side):
+                    self.line_copy(a, side, step - 1).wait_recv()
+
+                    @pl.when(self.sends(side))
+                    def _():
+                        self.line_copy(a, side, step).start()
+
+                    for k in self.peers(a):
+                        self.peer_copy(a, side, step, k).start()
+                    self.core_copy(a, side, step, 0).start()
+
+        for a in range(len(self.shards)):
+            for side in range(2):
+
+                @pl.when((step > 1) & self.has(side, step - 1))
+                def _(a=a, side=side):
+                    self.hand_over(a, side, step - 1)
+
+    def finish(self):
+        last = self.chips - 1
+        for a in range(len(self.shards)):
+            for side in range(2):
+
+                @pl.when(self.has(side, last))
+                def _(a=a, side=side):
+                    self.hand_over(a, side, last)
+
+        def settle(step, _):
+            for a in range(len(self.shards)):
+                for side in range(2):
+
+                    @pl.when(self.has(side, step))
+                    def _(a=a, side=side):
+                        @pl.when(self.sends(side))
+                        def _():
+                            self.line_copy(a, side, step).wait_send()
+
+                        for k in self.peers(a):
+                            self.peer_copy(a, side, step, k).wait_send()
+                            self.core_copy(a, side, step, k).wait_send()
+                            self.core_copy(a, side, step, k).wait_recv()
+                        self.core_copy(a, side, step, 0).wait_send()
+                        self.core_copy(a, side, step, 0).wait_recv()
+
+            return 0
+
+        lax.fori_loop(1, self.chips, settle, 0)
+        for a in range(len(self.shards)):
+            for side in range(2):
+
+                @pl.when(self.sends(side))
+                def _(a=a, side=side):
+                    self.first_copy(a, side).wait_send()
+
+            self.pair_copy(a).wait_send()
+            self.pair_copy(a).wait_recv()
+            self.local_copy(a).wait()
+
+
+def shares_of(shards):
+    copies = lax.axis_size("dp")
+    return [copies if shard.shape[0] % (TILE * copies) == 0 else 1 for shard in shards]
+
+
+def whole_shapes(shards):
+    size = lax.axis_size("fsdp")
+    return [jax.ShapeDtypeStruct((size * s.shape[0], *s.shape[1:]), s.dtype) for s in shards]
+
+
+def gather_kernel(shares, *refs):
+    count = len(shares)
+    gather = Gather(shares, refs[:count], refs[count : 2 * count], refs[2 * count :])
+    gather.greet()
+    gather.start()
 
     def advance(step, _):
-        for a in range(count):
-            for side in range(2):
-
-                @pl.when(has(side, step))
-                def _(a=a, side=side):
-                    line_copy(a, side, step - 1).wait_recv()
-
-                    @pl.when(sends(side))
-                    def _():
-                        line_copy(a, side, step).start()
-
-                    for k in peers(a):
-                        peer_copy(a, side, step, k).start()
-                    core_copy(a, side, step, 0).start()
-
-        for a in range(count):
-            for side in range(2):
-
-                @pl.when((step > 1) & has(side, step - 1))
-                def _(a=a, side=side):
-                    hand_over(a, side, step - 1)
-
+        gather.advance(step)
         return 0
 
-    lax.fori_loop(1, chips, advance, 0)
-    for a in range(count):
-        for side in range(2):
-
-            @pl.when(has(side, chips - 1))
-            def _(a=a, side=side):
-                hand_over(a, side, chips - 1)
-
-    def finish(step, _):
-        for a in range(count):
-            for side in range(2):
-
-                @pl.when(has(side, step))
-                def _(a=a, side=side):
-                    @pl.when(sends(side))
-                    def _():
-                        line_copy(a, side, step).wait_send()
-
-                    for k in peers(a):
-                        peer_copy(a, side, step, k).wait_send()
-                        core_copy(a, side, step, k).wait_send()
-                        core_copy(a, side, step, k).wait_recv()
-                    core_copy(a, side, step, 0).wait_send()
-                    core_copy(a, side, step, 0).wait_recv()
-
-        return 0
-
-    lax.fori_loop(1, chips, finish, 0)
-    for a in range(count):
-        for side in range(2):
-
-            @pl.when(sends(side))
-            def _(a=a, side=side):
-                first_copy(a, side).wait_send()
-
-        pair_copy(a).wait_send()
-        pair_copy(a).wait_recv()
-        local_copy(a).wait()
+    lax.fori_loop(1, gather.chips, advance, 0)
+    gather.finish()
 
 
 def gather_shards(identity, *shards):
-    copies, size = lax.axis_size("dp"), lax.axis_size("fsdp")
-    chips = size // 2
-    shares = [copies if shard.shape[0] % (TILE * copies) == 0 else 1 for shard in shards]
     count = len(shards)
-    dma = pltpu.SemaphoreType.DMA
     anywhere = pl.BlockSpec(memory_space=pl.ANY)
     return pl.pallas_call(
-        functools.partial(gather_kernel, shares),
-        out_shape=[
-            jax.ShapeDtypeStruct((size * shard.shape[0], *shard.shape[1:]), shard.dtype)
-            for shard in shards
-        ],
+        functools.partial(gather_kernel, shares_of(shards)),
+        out_shape=whole_shapes(shards),
         in_specs=[anywhere] * count,
         out_specs=[anywhere] * count,
-        scratch_shapes=[
-            dma((count,)),
-            dma((count,)),
-            dma((count,)),
-            dma((count, 2, chips)),
-            dma((count, 2, chips)),
-            dma((count, 2, chips, copies)),
-            dma((count, 2, chips, copies)),
-            dma((count, 2, chips, copies)),
-            dma((count, 2, chips, copies)),
-        ],
+        scratch_shapes=Gather.scratch(count),
         compiler_params=pltpu.CompilerParams(collective_id=identity, has_side_effects=True),
         cost_estimate=SMALL,
         name="gather_shards",
@@ -950,99 +965,220 @@
     )(query_grad, kv_grad, rows, total, gain.reshape(1, width), weight)
 
 
-def sum_kernel(split, *refs):
+class CopySum:
+    def __init__(self, split, values, totals, arrived, whole, sems):
+        self.split, self.values, self.totals = split, values, totals
+        self.arrived, self.whole = arrived, whole
+        self.part_send, self.part_recv, self.whole_send, self.whole_recv = sems
+        self.copies = lax.axis_size("dp")
+        self.place, self.me = lax.axis_index("dp"), lax.axis_index("fsdp")
+
+    @staticmethod
+    def split_of(shapes):
+        return [shape[0] % (TILE * lax.axis_size("dp")) == 0 for shape in shapes]
+
+    @staticmethod
+    def scratch(shapes):
+        copies = lax.axis_size("dp")
+        arrived, whole = [], []
+        for (rows, columns), parts in zip(shapes, CopySum.split_of(shapes)):
+            arrived.append((copies - 1, rows // copies, columns) if parts else (copies, rows, columns))
+            whole.append((rows, columns) if parts else (TILE, 128))
+        return [pltpu.VMEM(shape, LOW) for shape in arrived + whole]
+
+    def rows(self, a, owner):
+        part = self.values[a].shape[0] // self.copies
+        return pl.ds(pl.multiple_of(owner * part, TILE), part)
+
+    def part_copy(self, a, k):
+        peer = lax.rem(self.place + k, self.copies)
+        value, arrived = self.values[a], self.arrived[a]
+        return pltpu.make_async_remote_copy(
+            src_ref=value.at[self.rows(a, peer)] if self.split[a] else value,
+            dst_ref=arrived.at[k - 1] if self.split[a] else arrived.at[self.place],
+            send_sem=self.part_send.at[a, k],
+            recv_sem=self.part_recv.at[a, k],
+            device_id=(peer, self.me),
+            device_id_type=pl.DeviceIdType.MESH,
+        )
+
+    def whole_copy(self, a, k):
+        where = self.rows(a, self.place)
+        return pltpu.make_async_remote_copy(
+            src_ref=self.whole[a].at[where],
+            dst_ref=self.whole[a].at[where],
+            send_sem=self.whole_send.at[a, k],
+            recv_sem=self.whole_recv.at[a, k],
+            device_id=(lax.rem(self.place + k, self.copies), self.me),
+            device_id_type=pl.DeviceIdType.MESH,
+        )
+
+    def send(self, a):
+        for k in range(1, self.copies):
+            self.part_copy(a, k).start()
+
+    def reduce(self, a):
+        value, arrived = self.values[a], self.arrived[a]
+        if not self.split[a]:
+            arrived[self.place] = value[...]
+        for k in range(1, self.copies):
+            self.part_copy(a, k).wait_recv()
+        if self.split[a]:
+            total = value[self.rows(a, self.place)].astype(FULL)
+            for k in range(1, self.copies):
+                total = total + arrived[k - 1].astype(FULL)
+            self.whole[a][self.rows(a, self.place)] = total.astype(LOW)
+            for k in range(1, self.copies):
+                self.whole_copy(a, k).start()
+        else:
+            total = arrived[0].astype(FULL)
+            for k in range(1, self.copies):
+                total = total + arrived[k].astype(FULL)
+            self.totals[a][...] = total
+
+    def finish(self, a):
+        for k in range(1, self.copies):
+            self.part_copy(a, k).wait_send()
+            if self.split[a]:
+                self.whole_copy(a, k).wait_send()
+                self.whole_copy(a, k).wait_recv()
+        if self.split[a]:
+            self.totals[a][...] = self.whole[a][...].astype(FULL)
+
+
+def tail_kernel(split, *refs):
     count = len(split)
-    values, totals = refs[:count], refs[count : 2 * count]
-    arrived, whole = refs[2 * count : 3 * count], refs[3 * count : 4 * count]
-    part_send, part_recv, whole_send, whole_recv = refs[4 * count :]
+    given = count - 3
+    inputs, refs = refs[:given], refs[given:]
+    summed_ref, left_ref, right_ref = refs[:3]
+    totals, all_ref, refs = refs[3 : 3 + count], refs[3 + count], refs[4 + count :]
+    arrived, whole, refs = refs[:count], refs[count : 2 * count], refs[2 * count :]
+    held, arrive, total, action, weights, gains, right_all = refs[:7]
+    load_sem, right_sem, line_send, line_recv = refs[7:11]
+    sums = CopySum(split, (*inputs, action, weights, gains), totals, arrived, whole, refs[11:15])
+    gather = Gather([1], [right_ref], [all_ref], refs[15:])
     mesh = pl.DeviceIdType.MESH
+    place, me = lax.axis_index("dp"), lax.axis_index("fsdp")
+    chips = lax.axis_size("fsdp") // 2
+    chip = me // 2
+
+    load = pltpu.make_async_copy(summed_ref, held, load_sem)
+    load.start()
+    gather.greet()
+    gather.start()
+    load.wait()
+
+    def valid_at(side, step):
+        return chip <= step - 1 if side == 0 else chip >= chips - step
+
+    def fed(side):
+        return chip > 0 if side == 0 else chip < chips - 1
+
+    def line_copy(side, step, owner):
+        return pltpu.make_async_remote_copy(
+            src_ref=held.at[owner],
+            dst_ref=arrive.at[side, step - 1],
+            send_sem=line_send.at[side, step - 1],
+            recv_sem=line_recv.at[side, step - 1],
+            device_id=(place, me + 2 if side == 0 else me - 2),
+            device_id_type=mesh,
+        )
+
+    for step in range(1, chips):
+        for side in range(2):
+
+            @pl.when(valid_at(side, step))
+            def _(step=step, side=side):
+                owner = chip + chips - step if side == 0 else chip - chips + step
+                if step > 1:
+
+                    @pl.when(fed(side))
+                    def _():
+                        line_copy(side, step - 1, chip).wait_recv()
+                        held[owner] = (
+                            held[owner].astype(FULL) + arrive[side, step - 2].astype(FULL)
+                        ).astype(LOW)
+
+                line_copy(side, step, owner).start()
+
+        gather.advance(step)
+        if step == 1:
+            for a in range(given):
+                sums.send(a)
+        if step == min(2, chips - 1):
+            for a in range(given):
+                sums.reduce(a)
+    gather.finish()
+    fetch = pltpu.make_async_copy(all_ref, right_all, right_sem)
+    fetch.start()
+    fetch.wait()
+    action[...] = multiply_left(left_ref[...], right_all[...]).astype(LOW)
+    sums.send(given)
+    total[...] = held[chip].astype(FULL)
+    for side in range(2):
+
+        @pl.when(fed(side))
+        def _(side=side):
+            line_copy(side, chips - 1, chip).wait_recv()
+            total[...] += arrive[side, chips - 2].astype(FULL)
+
+    rows = weights.shape[0]
+    weights[...] = total[:rows].astype(LOW)
+    gains[...] = total[rows:].astype(LOW)
+    for a in range(given + 1, count):
+        sums.send(a)
+    for a in range(given):
+        sums.finish(a)
+    for a in range(given, count):
+        sums.reduce(a)
+    for step in range(1, chips):
+        for side in range(2):
+
+            @pl.when(valid_at(side, step))
+            def _(step=step, side=side):
+                line_copy(side, step, chip).wait_send()
+
+    for a in range(given, count):
+        sums.finish(a)
+
+
+def tail_sums(values, summed, rows, left, right):
+    chips, block = summed.shape[0], summed.shape[1:]
+    own = [(left.shape[1], right.shape[1]), (rows, block[1]), (block[0] - rows, block[1])]
+    shapes = [value.shape for value in values] + own
+    count = len(shapes)
+    dma = pltpu.SemaphoreType.DMA
     copies = lax.axis_size("dp")
-    place, me = lax.axis_index("dp"), lax.axis_index("fsdp")
-    barrier = pltpu.get_barrier_semaphore()
-    for k in range(1, copies):
-        peer = lax.rem(place + k, copies)
-        pl.semaphore_signal(barrier, inc=1, device_id=(peer, me), device_id_type=mesh)
-    pl.semaphore_wait(barrier, copies - 1)
-
-    def rows(a, owner):
-        part = values[a].shape[0] // copies
-        return pl.ds(pl.multiple_of(owner * part, TILE), part)
-
-    def part_copy(a, k):
-        peer = lax.rem(place + k, copies)
-        return pltpu.make_async_remote_copy(
-            src_ref=values[a].at[rows(a, peer)] if split[a] else values[a],
-            dst_ref=arrived[a].at[k - 1] if split[a] else arrived[a].at[place],
-            send_sem=part_send.at[a, k],
-            recv_sem=part_recv.at[a, k],
-            device_id=(peer, me),
-            device_id_type=mesh,
-        )
-
-    def whole_copy(a, k):
-        return pltpu.make_async_remote_copy(
-            src_ref=whole[a].at[rows(a, place)],
-            dst_ref=whole[a].at[rows(a, place)],
-            send_sem=whole_send.at[a, k],
-            recv_sem=whole_recv.at[a, k],
-            device_id=(lax.rem(place + k, copies), me),
-            device_id_type=mesh,
-        )
-
-    for a in range(count):
-        for k in range(1, copies):
-            part_copy(a, k).start()
-    for a in range(count):
-        if not split[a]:
-            arrived[a][place] = values[a][...]
-        for k in range(1, copies):
-            part_copy(a, k).wait_recv()
-        if split[a]:
-            total = values[a][rows(a, place)].astype(FULL)
-            for k in range(1, copies):
-                total = total + arrived[a][k - 1].astype(FULL)
-            whole[a][rows(a, place)] = total.astype(LOW)
-            for k in range(1, copies):
-                whole_copy(a, k).start()
-        else:
-            total = arrived[a][0].astype(FULL)
-            for k in range(1, copies):
-                total = total + arrived[a][k].astype(FULL)
-            totals[a][...] = total
-    for a in range(count):
-        for k in range(1, copies):
-            part_copy(a, k).wait_send()
-            if split[a]:
-                whole_copy(a, k).wait_send()
-                whole_copy(a, k).wait_recv()
-        if split[a]:
-            totals[a][...] = whole[a][...].astype(FULL)
-
-
-def sum_copies(identity, values):
-    copies = lax.axis_size("dp")
-    split = [value.shape[0] % (TILE * copies) == 0 for value in values]
-    count = len(values)
-    dma = pltpu.SemaphoreType.DMA
-    arrived, whole = [], []
-    for value, parts in zip(values, split):
-        rows, columns = value.shape
-        arrived.append((copies - 1, rows // copies, columns) if parts else (copies, rows, columns))
-        whole.append((rows, columns) if parts else (TILE, 128))
     inside = pl.BlockSpec(memory_space=pltpu.VMEM)
-    return pl.pallas_call(
-        functools.partial(sum_kernel, split),
-        out_shape=[jax.ShapeDtypeStruct(value.shape, FULL) for value in values],
-        in_specs=[inside] * count,
-        out_specs=[inside] * count,
-        scratch_shapes=[pltpu.VMEM(shape, LOW) for shape in arrived + whole]
-        + [dma((count, copies))] * 4,
+    anywhere = pl.BlockSpec(memory_space=pl.ANY)
+    outs = pl.pallas_call(
+        functools.partial(tail_kernel, CopySum.split_of(shapes)),
+        out_shape=[jax.ShapeDtypeStruct(shape, FULL) for shape in shapes] + whole_shapes([right]),
+        in_specs=[inside] * len(values) + [anywhere, inside, anywhere],
+        out_specs=[inside] * count + [anywhere],
+        scratch_shapes=CopySum.scratch(shapes)
+        + [
+            pltpu.VMEM((chips, *block), LOW),
+            pltpu.VMEM((2, chips - 1, *block), LOW),
+            pltpu.VMEM(block, FULL),
+            *(pltpu.VMEM(shape, LOW) for shape in own),
+            pltpu.VMEM((2 * chips * right.shape[0], right.shape[1]), LOW),
+            dma,
+            dma,
+            dma((2, chips - 1)),
+            dma((2, chips - 1)),
+        ]
+        + [dma((count, copies))] * 4
+        + Gather.scratch(1),
         compiler_params=pltpu.CompilerParams(
-            collective_id=identity, has_side_effects=True, vmem_limit_bytes=48 * MIB
+            collective_id=6, has_side_effects=True, vmem_limit_bytes=58 * MIB
         ),
-        cost_estimate=SMALL,
-        name="sum_copies",
-    )(*values)
+        cost_estimate=pl.CostEstimate(
+            flops=30_000_000_000, bytes_accessed=1, transcendentals=0
+        ),
+        name="tail_sums",
+    )(*values, summed, left, right)
+    return outs[:count]
 
 
 def widen_kernel(*refs):
@@ -1069,40 +1205,23 @@
     )(*values)
 
 
-def share_kernel(per, core_ref, left_ref, right_ref, action_left_ref, action_right_ref, *refs):
-    out_ref = refs[-1]
+def share_kernel(core_ref, left_ref, right_ref, *refs):
     rows = left_ref.shape[1]
-    out_ref[0, :rows] = multiply_left(left_ref[...], right_ref[...]).astype(LOW)
-    product = multiply_left(action_left_ref[...], action_right_ref[...])
-    count = product.shape[0] // per
-    small = product[:count]
-    which = lax.rem(2 * pl.program_id(0) + core_ref[0], per)
-    for i in range(1, per):
-        small = jnp.where(which == i, product[i * count : (i + 1) * count], small)
-    small = small.astype(LOW)
-    fold = out_ref.shape[2] // small.shape[1]
-    extra = small.shape[0] // fold
-    for i in range(fold):
-        columns = slice(i * small.shape[1], (i + 1) * small.shape[1])
-        out_ref[0, rows : rows + extra, columns] = small[i * extra : (i + 1) * extra]
+    refs[-1][0, :rows] = multiply_left(left_ref[...], right_ref[...]).astype(LOW)
     if len(refs) > 1:
-        out_ref[0, rows + extra :] = refs[0][0]
-
-
-def weight_shares(core, left, right, action_left, action_right, gains=None):
+        refs[-1][0, rows:] = refs[0][0]
+
+
+def weight_shares(core, left, right, gains=None):
     size = lax.axis_size("fsdp")
     chips = size // 2
     count, rows = left.shape[0], left.shape[1] // size
-    action_count, action_rows = action_left.shape[0], action_left.shape[1] // size
-    width, action_width = right.shape[1], action_right.shape[1]
-    total = rows + action_rows * action_width // width
-    per = max(1, 128 // action_rows)
-    extra = []
+    width, total, extra = right.shape[1], rows, []
     if gains is not None:
         total += gains.shape[1]
         extra = [pl.BlockSpec((1, *gains.shape[1:]), lambda c, core: (2 * c + core[0], 0, 0))]
     return pl.pallas_call(
-        functools.partial(share_kernel, per),
+        share_kernel,
         out_shape=jax.ShapeDtypeStruct((chips, total, width), LOW),
         grid_spec=pltpu.PrefetchScalarGridSpec(
             num_scalar_prefetch=1,
@@ -1110,10 +1229,6 @@
             in_specs=[
                 pl.BlockSpec((count, rows), lambda c, core: (0, 2 * c + core[0])),
                 pl.BlockSpec((count, width), lambda c, core: (0, 0)),
-                pl.BlockSpec(
-                    (action_count, per * action_rows), lambda c, core: (0, (2 * c + core[0]) // per)
-                ),
-                pl.BlockSpec((action_count, action_width), lambda c, core: (0, 0)),
             ]
             + extra,
             out_specs=pl.BlockSpec((1, total, width), lambda c, core: (c, 0, 0)),
@@ -1125,8 +1240,6 @@
         jnp.reshape(core, (1,)).astype(jnp.int32),
         left,
         right,
-        action_left,
-        action_right,
         *([] if gains is None else [gains]),
     )
 
@@ -1141,40 +1254,20 @@
     return raised / jnp.sum(raised, axis=-1, keepdims=True)
 
 
-def greet_copies():
-    copies = lax.axis_size("dp")
-    place, me = lax.axis_index("dp"), lax.axis_index("fsdp")
-    barrier = pltpu.get_barrier_semaphore()
-    for k in range(1, copies):
-        pl.semaphore_signal(
-            barrier,
-            inc=1,
-            device_id=(lax.rem(place + k, copies), me),
-            device_id_type=pl.DeviceIdType.MESH,
-        )
-    pl.semaphore_wait(barrier, copies - 1)
-
-
-def mix_kernel(
-    scale,
-    features,
-    prefix_ref,
-    action_ref,
-    prefix_all_ref,
-    action_all_ref,
-    bias_ref,
-    prefix_out,
-    action_out,
-    kv_out,
-    held,
-    send_sem,
-    recv_sem,
-    out_sem,
-):
+def mix_kernel(scale, features, shares, *refs):
+    count = len(shares)
+    prefix_ref, action_ref, prefix_all_ref, action_all_ref, bias_ref = refs[:5]
+    shards, refs = refs[5 : 5 + count], refs[5 + count :]
+    prefix_out, action_out, kv_out = refs[:3]
+    wholes, refs = refs[3 : 3 + count], refs[3 + count :]
+    held, send_sem, recv_sem, out_sem = refs[:4]
+    gather = Gather(shares, shards, wholes, refs[4:])
     copies = lax.axis_size("dp")
     place, me = lax.axis_index("dp"), lax.axis_index("fsdp")
     item, head = pl.program_id(0), pl.program_id(1)
     items, rows = prefix_all_ref.shape[0], prefix_ref.shape[1]
+    heads = pl.num_programs(1)
+    turn = item * heads + head
 
     def copy(at, k):
         return pltpu.make_async_remote_copy(
@@ -1191,15 +1284,22 @@
         for at in range(items):
             held[0, at, :rows] = prefix_all_ref[at, :, features:]
             held[0, at, rows:] = action_all_ref[at, :, features:]
-        greet_copies()
+        gather.greet()
         for at in range(items):
             for k in range(1, copies):
                 copy(at, k).start()
+        gather.start()
 
     @pl.when(head == 0)
     def _():
         for k in range(1, copies):
             copy(item, k).wait_recv()
+
+    every = 2 if gather.chips <= items * features // kv_out.shape[3] else 1
+
+    @pl.when((turn > 0) & (lax.rem(turn, every) == 0) & (turn < every * gather.chips))
+    def _():
+        gather.advance(turn // every)
 
     queries = stacked((prefix_ref, action_ref))
     kv = jnp.concatenate([held[k, item] for k in range(copies)], axis=0)
@@ -1217,32 +1317,24 @@
             for k in range(1, copies):
                 copy(at, k).wait_send()
         whole.wait()
-
-
-def mix_back_kernel(
-    scale,
-    prefix_ref,
-    action_ref,
-    prefix_grad_ref,
-    action_grad_ref,
-    bias_ref,
-    kv_ref,
-    prefix_out,
-    action_out,
-    kv_out,
-    total,
-    own,
-    sent,
-    arrived,
-    send_sem,
-    recv_sem,
-):
+        gather.finish()
+
+
+def mix_back_kernel(scale, shares, *refs):
+    count = len(shares)
+    prefix_ref, action_ref, prefix_grad_ref, action_grad_ref, bias_ref, kv_ref = refs[:6]
+    shards, refs = refs[6 : 6 + count], refs[6 + count :]
+    prefix_out, action_out, kv_out = refs[:3]
+    wholes, refs = refs[3 : 3 + count], refs[3 + count :]
+    total, own, sent, arrived, send_sem, recv_sem = refs[:6]
+    gather = Gather(shares, shards, wholes, refs[6:])
     copies = lax.axis_size("dp")
     place, me = lax.axis_index("dp"), lax.axis_index("fsdp")
     item, head = pl.program_id(0), pl.program_id(1)
     items, heads = pl.num_programs(0), pl.num_programs(1)
     rows = prefix_ref.shape[1]
     step = rows + action_ref.shape[1]
+    turn = item * heads + head
 
     def copy(at, k):
         return pltpu.make_async_remote_copy(
@@ -1254,9 +1346,14 @@
             device_id_type=pl.DeviceIdType.MESH,
         )
 
-    @pl.when((item == 0) & (head == 0))
-    def _():
-        greet_copies()
+    @pl.when(turn == 0)
+    def _():
+        gather.greet()
+        gather.start()
+
+    @pl.when((turn > 0) & (turn < gather.chips))
+    def _():
+        gather.advance(turn)
 
     @pl.when(head == 0)
     def _():
@@ -1294,9 +1391,10 @@
             for k in range(1, copies):
                 summed = summed + arrived[at, k - 1].astype(FULL)
             kv_out[at] = summed.astype(LOW)
-
-
-def mix_call(scale, heads, prefix, action, bias, grads=None, kv=None):
+        gather.finish()
+
+
+def mix_call(scale, heads, prefix, action, bias, grads=None, kv=None, shards=()):
     copies = lax.axis_size("dp")
     items, prefix_rows, columns = prefix.shape
     action_rows = action.shape[1]
@@ -1317,43 +1415,51 @@
     block = (rows, 2 * head_size)
     if grads is None:
         return pl.pallas_call(
-            functools.partial(mix_kernel, scale, features),
-            out_shape=shapes + [jax.ShapeDtypeStruct((copies, items, *block), LOW)],
+            functools.partial(mix_kernel, scale, features, shares_of(shards)),
+            out_shape=shapes
+            + [jax.ShapeDtypeStruct((copies, items, *block), LOW)]
+            + whole_shapes(shards),
             grid=(items, heads),
             in_specs=per_head
             + [
                 pl.BlockSpec(prefix.shape, lambda i, h: (0, 0, 0)),
                 pl.BlockSpec(action.shape, lambda i, h: (0, 0, 0)),
                 bias_spec,
-            ],
-            out_specs=per_head + [pl.BlockSpec(memory_space=pl.ANY)],
-            scratch_shapes=[pltpu.VMEM((copies, items, *block), LOW), *sems, dma],
+            ]
+            + [pl.BlockSpec(memory_space=pl.ANY)] * len(shards),
+            out_specs=per_head + [pl.BlockSpec(memory_space=pl.ANY)] * (1 + len(shards)),
+            scratch_shapes=[pltpu.VMEM((copies, items, *block), LOW), *sems, dma]
+            + Gather.scratch(len(shards)),
             compiler_params=pltpu.CompilerParams(
                 collective_id=7, has_side_effects=True, vmem_limit_bytes=48 * MIB
             ),
             cost_estimate=SMALL,
             name="mix",
-        )(prefix, action, prefix, action, bias)
+        )(prefix, action, prefix, action, bias, *shards)
     return pl.pallas_call(
-        functools.partial(mix_back_kernel, scale),
-        out_shape=shapes + [jax.ShapeDtypeStruct((items, *block), LOW)],
+        functools.partial(mix_back_kernel, scale, shares_of(shards)),
+        out_shape=shapes + [jax.ShapeDtypeStruct((items, *block), LOW)] + whole_shapes(shards),
         grid=(items, heads),
         in_specs=per_head * 2
-        + [bias_spec, pl.BlockSpec((copies, 1, *block), lambda i, h: (0, i, 0, 0))],
-        out_specs=per_head + [pl.BlockSpec((items, *block), lambda i, h: (0, 0, 0))],
+        + [bias_spec, pl.BlockSpec((copies, 1, *block), lambda i, h: (0, i, 0, 0))]
+        + [pl.BlockSpec(memory_space=pl.ANY)] * len(shards),
+        out_specs=per_head
+        + [pl.BlockSpec((items, *block), lambda i, h: (0, 0, 0))]
+        + [pl.BlockSpec(memory_space=pl.ANY)] * len(shards),
         scratch_shapes=[
             pltpu.VMEM((length, 2 * head_size), FULL),
             pltpu.VMEM((items, *block), FULL),
             pltpu.VMEM((items, copies - 1, *block), LOW),
             pltpu.VMEM((items, copies - 1, *block), LOW),
             *sems,
+            *Gather.scratch(len(shards)),
         ],
         compiler_params=pltpu.CompilerParams(
             collective_id=8, has_side_effects=True, vmem_limit_bytes=48 * MIB
         ),
         cost_estimate=SMALL,
         name="mix_back",
-    )(prefix, action, *grads, bias, kv)
+    )(prefix, action, *grads, bias, kv, *shards)
 
 
 def body(
@@ -1472,14 +1578,12 @@
         key_place[None, None, :] < prefix_length + valid_count[:, None, None]
     )
     bias = jnp.where(allowed, 0.0, NEGATIVE).astype(FULL)
-    prefix_mixed, action_mixed, kv = mix_call(scale, heads, prefix_all, action_all, bias)
-    backs, prefix_output, action_output, _ = lax.optimization_barrier(
-        (backs, prefix_output, action_output, prefix_mixed)
-    )
-    prefix_o, action_o = gather_shards(4, prefix_output, action_output)
-
+    prefix_mixed, action_mixed, kv, prefix_o, action_o = mix_call(
+        scale, heads, prefix_all, action_all, bias, shards=(prefix_output, action_output)
+    )
+    backs, prefix_mixed = lax.optimization_barrier((backs, prefix_mixed))
+    action_mixed = action_mixed.reshape(action_tokens, features)
     prefix_mixed = prefix_mixed.reshape(prefix_tokens, features)
-    action_mixed = action_mixed.reshape(action_tokens, features)
     prefix_mid = prefix_flat + multiply(prefix_mixed, prefix_o)
     action_mid = action_flat + multiply(action_mixed, action_o)
 
@@ -1524,46 +1628,43 @@
         )
     )
     feed_sums = lax.psum((down_grad, gate_weight_grad, up_weight_grad, *action_feed), "dp")
+    parts = part_chunks(
+        prefix_tokens,
+        lax.optimization_barrier((inner, up_weight_grad))[0],
+        prefix_down,
+        halves(multiply(action_inner, action_down)),
+    )
+    sent, gate_grad = lax.optimization_barrier((add_pairs(11, *parts), gate_grad))
+    out_sums = Relay(line, sent, lambda chip: line.chip ^ chip)
+    out_sums.advance(1)
     small = halves(
         multiply_right(action_gate_grad, action_gate) + multiply_right(action_up_grad, action_up)
     )
     feed_back = collect(
         2, prefix_tokens, True, (gate_grad, up_grad), (prefix_gate, prefix_up), small, width
     )
-    feed_back, inner = lax.optimization_barrier((unpack(feed_back), inner))
+    feed_back = out_sums.after(feed_back)
+    out_sums.advance(2)
 
     prefix_mid_grad, prefix_low, prefix_mixed_grad, prefix_middle_part = middle_back(
-        feed_back[0], prefix_mid, prefix_back, prefix_gain, prefix_o
+        feed_back, prefix_mid, prefix_back, prefix_gain, prefix_o
     )
     action_mid_grad, action_low, action_mixed_grad, action_middle_part = middle_back(
-        feed_back[1], action_mid, action_back, action_gain, action_o
-    )
-    sent = line.pairs(9, prefix_mixed, prefix_low, action_mixed, action_low)
+        unfold(feed_back[prefix_tokens:]), action_mid, action_back, action_gain, action_o
+    )
+    sent = line.pairs(9, prefix_mixed, prefix_low)
     output_sums = Relay(line, sent, lambda chip: chip)
     output_sums.advance(1)
-    parts = part_chunks(
-        prefix_tokens,
-        lax.optimization_barrier((inner, sent))[0],
-        prefix_down,
-        halves(multiply(action_inner, action_down)),
-    )
-    sent = add_pairs(11, *parts)
-    sent, mixed_grads = lax.optimization_barrier((sent, (prefix_mixed_grad, action_mixed_grad)))
-    prefix_mixed_grad, action_mixed_grad = mixed_grads
-    out_sums = Relay(line, sent, lambda chip: line.chip ^ chip)
-    out_sums.advance(1)
-    prefix_mixed_grad = output_sums.after(prefix_mixed_grad)
-    output_sums.advance(2)
     mixed_grads = (
         prefix_mixed_grad.reshape(items, prefix_pad, features),
         action_mixed_grad.reshape(items, action_pad, features),
     )
-    prefix_query_grad, action_query_grad, kv_grad = mix_call(
-        scale, heads, prefix_all, action_all, bias, mixed_grads, kv
+    tokens_all = jnp.concatenate([action_hidden, action_mixed, action_low], axis=1)
+    prefix_query_grad, action_query_grad, kv_grad, tokens_all = mix_call(
+        scale, heads, prefix_all, action_all, bias, mixed_grads, kv, (tokens_all,)
     )
     kv_grad = output_sums.after(out_sums.after(kv_grad))
-    out_sums.advance(2)
-    output_sums.advance(3)
+    output_sums.advance(2)
     prefix_qkv_grad = jnp.concatenate([prefix_query_grad, kv_grad[:, :prefix_pad]], axis=2)
     action_qkv_grad = jnp.concatenate([action_query_grad, kv_grad[:, prefix_pad:]], axis=2)
     prefix_qkv_grad = prefix_qkv_grad.reshape(prefix_tokens, columns)
@@ -1601,38 +1702,35 @@
     gain_rows = rounded(-(-cuts[4] // columns))
     gain_parts = jnp.pad(gain_parts, ((0, 0), (0, gain_rows * columns - cuts[4])))
     gain_parts = gain_parts.astype(LOW).reshape(shards, gain_rows, columns)
-    sent = line.pairs(
-        10, prefix_hidden, prefix_qkv_grad, action_hidden, action_qkv_grad, gain_parts
-    )
-    qkv_sums = Relay(line, out_sums.after(sent), lambda chip: chip)
+    gain_parts = output_sums.after(gain_parts)
+    output_sums.advance(3)
+    sent = line.pairs(10, prefix_hidden, prefix_qkv_grad, gain_parts)
+    edges = [0]
+    for part in (action_width, features, action_width):
+        edges.append(edges[-1] + part)
+    hidden_all, mixed_all, low_all = (
+        tokens_all[:, start:stop] for start, stop in zip(edges, edges[1:])
+    )
+    rows = action_query.shape[0]
+    hidden_slice = lax.dynamic_slice_in_dim(hidden_all, line.place * rows, rows, 1)
+    rows = action_output.shape[0]
+    action_output_owned = multiply_left(
+        lax.dynamic_slice_in_dim(mixed_all, line.place * rows, rows, 1), low_all
+    )
+    output_owned, action_output_owned, action_qkv_owned, qkv_owned, gain_owned = tail_sums(
+        [output_sums.finish().astype(LOW), action_output_owned.astype(LOW)],
+        sent,
+        prefix_query.shape[0],
+        hidden_slice,
+        action_qkv_grad,
+    )
+    feed_sums, output_owned, sent = lax.optimization_barrier((feed_sums, output_owned, sent))
     out_sums.advance(3)
-    qkv_sums.advance(1)
-    output_owned = output_sums.finish()
-    qkv_sums.arrived, output_owned = out_sums.after((qkv_sums.arrived, output_owned))
-    qkv_sums.advance(2)
-    rows, output_rows = prefix_query.shape[0], prefix_output.shape[0]
-    folded_rows = output_owned[output_rows:]
-    folded_rows = jnp.concatenate(
-        [folded_rows[:, i : i + action_width] for i in range(0, width, action_width)], axis=0
-    )
-    output_owned, action_output_owned = sum_copies(
-        6, [output_owned[:output_rows].astype(LOW), folded_rows.astype(LOW)]
-    )
-    feed_sums, output_owned = qkv_sums.after((feed_sums, output_owned))
-    qkv_sums.advance(3)
+    out_sums.arrived, output_owned = lax.optimization_barrier((out_sums.arrived, output_owned))
+    feed_sums = [widen(value) for value in feed_sums]
     sums = unpack(out_sums.finish())
     prefix_out, action_out = trimmed(
         (prefix_mid + sums[0]).astype(LOW), (action_mid + sums[1]).astype(LOW)
-    )
-    qkv_owned = qkv_sums.finish()
-    gain_start = rows + action_query.shape[0]
-    qkv_owned, action_qkv_owned, gain_owned = sum_copies(
-        12,
-        [
-            qkv_owned[:rows].astype(LOW),
-            qkv_owned[rows:gain_start].astype(LOW),
-            qkv_owned[gain_start:].reshape(TILE * copies, -1).astype(LOW),
-        ],
     )
     gain_owned = gain_owned.reshape(-1)
     return (
@@ -1646,16 +1744,16 @@
         qkv_owned[:rows, features + head_size :],
         output_owned,
         gain_owned[cuts[1] : cuts[2]],
-        widen(feed_sums[1]),
-        widen(feed_sums[2]),
-        widen(feed_sums[0]),
+        feed_sums[1],
+        feed_sums[2],
+        feed_sums[0],
         gain_owned[cuts[2] : cuts[3]],
         action_qkv_owned[:, :features],
         action_qkv_owned[:, features : features + head_size],
         action_qkv_owned[:, features + head_size :],
         action_output_owned,
         gain_owned[cuts[3] : cuts[4]],
-        *(widen(v) for v in feed_sums[3:]),
+        *feed_sums[3:],
     )
 
 

time: 1280 us -> 1220 us (0.953)
  waiting for transfers between devices: 71.2 us -> 0.09 us
  starting transfers between devices: 79.7 us -> 36.3 us
  Pallas kernels: 846 us -> 886 us
    ppermute x18 -> x12, waiting for transfers between devices: 71.2 us -> 0.03 us  [move(): return lax.ppermute(value, 'fsdp', pairs)]
    pallas_call x10 -> x8, Pallas kernels: 368 us -> 416 us  [the longest x1 145 us: tail_sums(): pl.pallas_call(functools.partial(tail_kernel, CopySum.split_of(shapes)),...]
    ppermute x18 -> x12, starting transfers between devices: 79.7 us -> 36.2 us  [move(): return lax.ppermute(value, 'fsdp', pairs)]
    pallas_call x15 -> x10, Pallas kernels: 39.7 us -> 22.6 us  [add_block(): pl.pallas_call(add_kernel, out_shape=jax.ShapeDtypeStruct(shape, kind), g...]
    dot_general x6 -> x7, matrix products: 112 us -> 123 us  [multiply_left(): lax.dot_general(left, right, (((0,), (0,)), ((), ())), preferred_element_...]
    unnamed x196 -> x198, local copies, waits for them, and re-layouts: 71.4 us -> 65.3 us
  transfers between devices with their start and end apart: 20 -> 14, of which waited for: 1 -> 0; matrix products, arithmetic and copies ran while one was open for 5% -> 6% of each run, Pallas kernels for 45% -> 58%
where the time goes in v3:
time: 1220 us; the launch traced here: 1210 us
  Pallas kernels  886 us (73%)
  matrix products  154 us (13%)
  local copies, waits for them, and re-layouts  94.7 us (8%)
  starting transfers between devices  36.3 us (3%)
  other arithmetic  20.2 us (2%)
  between operations  15.4 us (1%)
    pallas_call x1, Pallas kernels, feed_all(): pl.pallas_call(functools.partial(feed_kernel, valid), out_shape=[jax.Shap...  158 us
    pallas_call x1, Pallas kernels, collect(): pl.pallas_call(functools.partial(collect_kernel, valid, transposed, count...  155 us
    pallas_call x1, Pallas kernels, tail_sums(): pl.pallas_call(functools.partial(tail_kernel, CopySum.split_of(shapes)),...  145 us
    dot_general x7, matrix products, multiply_left(): lax.dot_general(left, right, (((0,), (0,)), ((), ())), preferred_element_...  123 us
    pallas_call x1, Pallas kernels, gather_shards(): pl.pallas_call(functools.partial(gather_kernel, shares_of(shards)), out_s...  105 us
    pallas_call x1, Pallas kernels, mix_call(): pl.pallas_call(functools.partial(mix_kernel, scale, features, shares_of(s...  82.6 us
    unnamed x198, local copies, waits for them, and re-layouts  65.3 us
    pallas_call x1, Pallas kernels, mix_call(): pl.pallas_call(functools.partial(mix_back_kernel, scale, shares_of(shards...  63.9 us
  transfers between devices with their start and end apart: 14, of which 0 were waited for; matrix products, arithmetic and copies ran while one was open for 6% of the time, Pallas kernels for 58%

profile of v3, /device:TPU:0, one launch (start us, length us, event | category | flops | bytes accessed | tf_op | source)
XLA Modules:
  0.0 1207.5 jit_solution(9749684307090740727)
XLA Ops:
  16.7 105.4 %gather_shards.1 = (bf16[2048,2560]{1,0:T(8,128)(2,1)}, bf16[1024,2560]{1,0:T(8,128)(2,1)}, bf16[128,128]{1,0:T(8,128)(2,1)}) custom-call(bf16[256,2560]{1,0:T(8,128)(2,1)} %pad_maximum_fusion.3.refs_0_, bf16[128,2560]{1,0:T(8,128)(2,1)} %pad_maximum_fusion.4.refs_1_, bf16[16,128]{1,0:T(8,128)(2,1)} %fusion.25.refs_2_), custom_call_target="tpu_custom_call" | custom-call | flops 1 | bytes 1 | tf_op jit(solution)/shard_map/gather_shards/pallas_call | solution.py:413
  140.3 10.4 convolution_convert_fusion.3
  150.8 82.6 %mix.1 = (bf16[2,208,2048]{2,1,0:T(8,128)(2,1)S(1)}, bf16[2,16,2048]{2,1,0:T(8,128)(2,1)S(1)}, bf16[4,2,224,512]{3,2,1,0:T(8,128)(2,1)}, bf16[2048,2048]{1,0:T(8,128)(2,1)}, bf16[2048,1024]{1,0:T(8,128)(2,1)}) custom-call(bf16[2,208,2560]{2,1,0:T(8,128)(2,1)} %bitcast.131, bf16[2,16,2560]{2,1,0:T(8,128)(2,1)S(1)} %bitcast.121, ...), custom_call_target="tpu_custom_call" | custom-call | flops 1 | bytes 1 | tf_op jit(solution)/shard_map/mix/pallas_call | solution.py:1417
  239.2 8.6 multiply_reduce_fusion
  251.3 158.4 %feed_all.1 = (bf16[3328,2048]{1,0:T(8,128)(2,1)}, bf16[3328,2048]{1,0:T(8,128)(2,1)}, bf16[3328,2048]{1,0:T(8,128)(2,1)}, bf16[3328,2048]{1,0:T(8,128)(2,1)}, b...) custom-call(bf16[432,2048]{1,0:T(8,128)(2,1)} %pad_maximum_fusion.2.hidden_ref, ...), custom_call_target="tpu_custom_call" | custom-call | flops 1 | bytes 1 | tf_op jit(solution)/shard_map/feed_all/pallas_call | solution.py:651
  409.7 46.1 %convolution_convert_fusion.2 = bf16[2048,2048]{1,0:T(8,128)(2,1)} fusion(bf16[3328,2048]{1,0:T(8,128)(2,1)} %get-tuple-element.118.inner_ref, bf16[3328,2048]{1,0:T(8,128)(2,1)} %get-tuple-element.110), kind=kOutput, calls=%fused_computation.2 | convolution fusion | flops 27921481728 | bytes 35651584 | tf_op jit(solution)/shard_map/dot_general | solution.py:29
  455.7 34.2 %convolution_convert_fusion.1 = bf16[2048,2048]{1,0:T(8,128)(2,1)} fusion(bf16[3328,2048]{1,0:T(8,128)(2,1)} %get-tuple-element.111, bf16[3328,2048]{1,0:T(8,128)(2,1)S(1)} %copy-done.49), kind=kOutput, calls=%fused_computation.1 | convolution fusion | flops 27921481728 | bytes 35651584 | tf_op jit(solution)/shard_map/dot_general | solution.py:29
  489.9 36.8 %convolution_convert_fusion = bf16[2048,2048]{1,0:T(8,128)(2,1)} fusion(bf16[3328,2048]{1,0:T(8,128)(2,1)} %get-tuple-element.111, bf16[3328,2048]{1,0:T(8,128)(2,1)} %get-tuple-element.124.refs_1_), kind=kOutput, calls=%fused_computation | convolution fusion | flops 27921481728 | bytes 35651584 | tf_op jit(solution)/shard_map/dot_general | solution.py:29
  537.6 38.9 %part_chunks.1 = (bf16[4,432,2048]{2,1,0:T(8,128)(2,1)}, bf16[4,432,2048]{2,1,0:T(8,128)(2,1)}) custom-call(bf16[3328,2048]{1,0:T(8,128)(2,1)} %get-tuple-element.118.inner_ref, bf16[2048,2048]{1,0:T(8,128)(2,1)} %down_ref.3, bf16[4,2,16,2048]{3,2,1,0:T(8,128)(2,1)S(1)} %reshape.421.small_ref), custom_call_target="tpu_custom_call" | custom-call | flops 1 | bytes 1 | tf_op jit(solution)/shard_map/part_chunks/pallas_call | solution.py:867
  579.5 15.8 %add_pairs.3.value_ref = bf16[4,432,2048]{2,1,0:T(8,128)(2,1)S(1)} custom-call(bf16[4,432,2048]{2,1,0:T(8,128)(2,1)S(1)} %copy-done.19, bf16[4,432,2048]{2,1,0:T(8,128)(2,1)} %get-tuple-element.120.other_ref), custom_call_target="tpu_custom_call" | custom-call | flops 1 | bytes 1 | tf_op jit(solution)/shard_map/add_pairs/pallas_call | solution.py:156
  605.9 154.5 %collect.1.grad_ref = f32[432,2048]{1,0:T(8,128)} custom-call(bf16[3328,2048]{1,0:T(8,128)(2,1)} %get-tuple-element.123.refs_0_, bf16[3328,2048]{1,0:T(8,128)(2,1)} %get-tuple-element.124.refs_1_, bf16[2048,2048]{1,0:T(8,128)(2,1)} %refs_2_.1, bf16[2048,2048]{1,0:T(8,128)(2,1)} %refs_3_.1, bf16[4,2,16,2048]{3,2,1,0:T(8,128)(2,1)} %reshape.424.refs_4_), custom_call_target="tpu_custom_call" | custom-call | flops 1 | bytes 1 | tf_op jit(solution)/shard_map/collect/pallas_call | solution.py:829
  777.4 13.4 %middle_back.2 = (f32[416,2048]{1,0:T(8,128)}, bf16[416,2048]{1,0:T(8,128)(2,1)}, bf16[416,2048]{1,0:T(8,128)(2,1)}, f32[1,2048]{1,0:T(1,128)}) custom-call(f32[432,2048]{1,0:T(8,128)} %collect.1.grad_ref, f32[416,2048]{1,0:T(8,128)} %copy-done.45, bf16[416,2048]{1,0:T(8,128)(2,1)} %bitcast.135, f32[1,2048]{1,0:T(1,128)} %bitcast.149, ...), custom_call_target="tpu_custom_call" | custom-call | flops 1 | bytes 1 | tf_op jit(solution)/shard_map/middle_back/pallas_call | solution.py:907
  803.7 7.5 add_pairs.4.value_ref
  822.5 5.1 middle_back.3
  829.5 63.9 %mix_back.1 = (bf16[2,208,2048]{2,1,0:T(8,128)(2,1)S(1)}, bf16[2,16,2048]{2,1,0:T(8,128)(2,1)S(1)}, bf16[2,224,512]{2,1,0:T(8,128)(2,1)S(1)}, bf16[256,4096]{1,0:T(8,128)(2,1)}) custom-call(bf16[2,208,2560]{2,1,0:T(8,128)(2,1)} %bitcast.133, bf16[2,16,2560]{2,1,0:T(8,128)(2,1)S(1)} %bitcast.123, bf16[2,208,2048]{2,1,0:T(8,128)(2,1)S(1)} %bitcast.124, ...), custom_call_target="tpu_custom_call" | custom-call | flops 1 | bytes 1 | tf_op jit(solution)/shard_map/mix_back/pallas_call | solution.py:1439
  916.7 14.6 %entry_back.2 = (f32[416,2048]{1,0:T(8,128)}, f32[1,2048]{1,0:T(1,128)}) custom-call(bf16[416,2048]{1,0:T(8,128)(2,1)} %bitcast.115, bf16[416,512]{1,0:T(8,128)(2,1)} %bitcast.137, f32[416,2048]{1,0:T(8,128)} %bitcast.130, f32[416,2048]{1,0:T(8,128)} %get-tuple-element.146.total_ref, f32[1,2048]{1,0:T(1,128)} %bitcast.147, ...), custom_call_target="tpu_custom_call" | custom-call | flops 1 | bytes 1 | tf_op jit(solution)/shard_map/entry_back/pallas_call | solution.py:945
  935.8 8.1 collective-permute-start.10
  967.7 4.9 weight_shares.6.mine_ref
  972.7 5.0 weight_shares.7.other_ref
  978.4 9.7 add_pairs.5.refs_2_
  993.6 145.2 %tail_sums.1 = (f32[256,2048]{1,0:T(8,128)}, f32[256,1024]{1,0:T(8,128)}, f32[128,2560]{1,0:T(8,128)}, f32[256,2560]{1,0:T(8,128)}, f32[16,2560]{1,0:T(8,128)}, /*index=5*/bf16[256,2560]{1,0:T(8,128)(2,1)}) custom-call(bf16[256,2048]{1,0:T(8,128)(2,1)} %convert_element_type.103.refs_0_, bf16[256,1024]{1,0:T(8,128)(2,1)} %convolution_convert_fusion.8.refs_1_, ...), custom_call_target="tpu_custom_call" | custom-call | flops 30000001024 | bytes 1 | tf_op jit(solution)/shard_map/tail_sums/pallas_call | solution.py:1154
  1169.0 7.1 widen.6
  1179.5 7.1 widen.7
  1186.6 6.5 widen.8
  (337 shorter events, 202.2 us)
Async XLA Ops:
  7.2 523.4 %copy-start = (bf16[1024,512]{1,0:T(8,128)(2,1)S(1)}, bf16[1024,512]{1,0:T(8,128)(2,1)}, u32[]{:S(2)}) copy-start(bf16[1024,512]{1,0:T(8,128)(2,1)} %param.42) | copy-start | bytes 3145732
  7.2 232.0 %all-gather.2.cloned.1.call-start = ((), (), s32[]{:S(2)}) async-start(), calls=%async_computation | async-start | bytes 15925248 | tf_op jit(solution)/shard_map/all_gather | solution.py:1551
  14.0 1135.9 %all-reduce.9.cloned.1.call-start = ((), (), s32[]{:S(2)}) async-start(), calls=%async_computation.1 | async-start | bytes 56623104 | tf_op jit(solution)/shard_map/psum | solution.py:1630
  134.1 100.4 %copy-start.56 = (f32[2,16,1024]{2,1,0:T(8,128)}, f32[2,16,1024]{2,1,0:T(8,128)S(1)}, u32[]{:S(2)}) copy-start(f32[2,16,1024]{2,1,0:T(8,128)S(1)} %copy.79) | copy-start | bytes 393220
  135.7 15.1 %copy-start.14 = (f32[2,224,896]{2,1,0:T(8,128)}, f32[2,224,896]{2,1,0:T(8,128)S(1)}, u32[]{:S(2)}) copy-start(f32[2,224,896]{2,1,0:T(8,128)S(1)} %or_select_fusion.refs_4_) | copy-start | bytes 4816900
  409.6 46.1 %copy-start.49 = (bf16[3328,2048]{1,0:T(8,128)(2,1)S(1)}, bf16[3328,2048]{1,0:T(8,128)(2,1)}, u32[]{:S(2)}) copy-start(bf16[3328,2048]{1,0:T(8,128)(2,1)} %get-tuple-element.123.refs_0_) | copy-start | bytes 40894468
  489.9 36.8 %copy-start.62 = (bf16[2,4,2,16,2048]{4,3,2,1,0:T(8,128)(2,1)S(1)}, bf16[2,4,2,16,2048]{4,3,2,1,0:T(8,128)(2,1)}, u32[]{:S(2)}) copy-start(bf16[2,4,2,16,2048]{4,3,2,1,0:T(8,128)(2,1)} %get-tuple-element.116) | copy-start | bytes 3145732
  599.6 160.9 %collective-permute-start = (bf16[432,2048]{1,0:T(8,128)(2,1)}, bf16[432,2048]{1,0:T(8,128)(2,1)}, u32[]{:S(2)}, u32[]{:S(2)}) collective-permute-start(bf16[432,2048]{1,0:T(8,128)(2,1)} %get-tuple-element.183), channel_id=1, source_target_pairs={{0,2},{1,3},{8,10},{9,11},{16,18},{17,19},{24,26},{25,27}} | collective-permute-start | bytes 5308424 | tf_op jit(solution)/shard_map/ppermute | solution.py:56
  602.1 158.3 %collective-permute-start.1 = (bf16[432,2048]{1,0:T(8,128)(2,1)}, bf16[432,2048]{1,0:T(8,128)(2,1)}, u32[]{:S(2)}, u32[]{:S(2)}) collective-permute-start(bf16[432,2048]{1,0:T(8,128)(2,1)} %get-tuple-element.182), channel_id=1, source_target_pairs={{6,4},{7,5},{14,12},{15,13},{22,20},{23,21},{30,28},{31,29}} | collective-permute-start | bytes 5308424 | tf_op jit(solution)/shard_map/ppermute | solution.py:56
  767.0 131.0 %collective-permute-start.2 = (bf16[432,2048]{1,0:T(8,128)(2,1)}, bf16[432,2048]{1,0:T(8,128)(2,1)S(1)}, u32[]{:S(2)}, u32[]{:S(2)}) collective-permute-start(bf16[432,2048]{1,0:T(8,128)(2,1)} %add_block.10), channel_id=1, source_target_pairs={{0,2},{1,3},{2,4},{3,5},{8,10},{9,11},{10,12},{11,13},{16,18},{17,... | collective-permute-start | bytes 5308424 | tf_op jit(solution)/shard_map/ppermute | solution.py:56
  774.9 123.2 %collective-permute-start.3 = (bf16[432,2048]{1,0:T(8,128)(2,1)}, bf16[432,2048]{1,0:T(8,128)(2,1)}, u32[]{:S(2)}, u32[]{:S(2)}) collective-permute-start(bf16[432,2048]{1,0:T(8,128)(2,1)} %add_block.11), channel_id=1, source_target_pairs={{4,2},{5,3},{6,4},{7,5},{12,10},{13,11},{14,12},{15,13},{20,18},{2... | collective-permute-start | bytes 5308424 | tf_op jit(solution)/shard_map/ppermute | solution.py:56
  814.7 83.4 %collective-permute-start.6 = (bf16[256,2048]{1,0:T(8,128)(2,1)}, bf16[256,2048]{1,0:T(8,128)(2,1)}, u32[]{:S(2)}, u32[]{:S(2)}) collective-permute-start(bf16[256,2048]{1,0:T(8,128)(2,1)} %get-tuple-element.185), channel_id=1, source_target_pairs={{0,2},{1,3},{8,10},{9,11},{16,18},{17,19},{24,26},{25,27}} | collective-permute-start | bytes 3145736 | tf_op jit(solution)/shard_map/ppermute | solution.py:56
  817.1 81.0 %collective-permute-start.7 = (bf16[256,2048]{1,0:T(8,128)(2,1)}, bf16[256,2048]{1,0:T(8,128)(2,1)}, u32[]{:S(2)}, u32[]{:S(2)}) collective-permute-start(bf16[256,2048]{1,0:T(8,128)(2,1)} %get-tuple-element.184), channel_id=1, source_target_pairs={{6,4},{7,5},{14,12},{15,13},{22,20},{23,21},{30,28},{31,29}} | collective-permute-start | bytes 3145736 | tf_op jit(solution)/shard_map/ppermute | solution.py:56
  829.5 66.6 %copy-start.79 = (f32[1,2048]{1,0:T(1,128)S(1)}, f32[1,2048]{1,0:T(1,128)}, u32[]{:S(2)}) copy-start(f32[1,2048]{1,0:T(1,128)} %get-tuple-element.148) | copy-start | bytes 24580
  829.5 68.5 %copy-start.80 = (f32[1,1024]{1,0:T(1,128)S(1)}, f32[1,1024]{1,0:T(1,128)}, u32[]{:S(2)}) copy-start(f32[1,1024]{1,0:T(1,128)} %get-tuple-element.152) | copy-start | bytes 12292
  903.1 29.2 %collective-permute-start.8 = (bf16[256,2048]{1,0:T(8,128)(2,1)}, bf16[256,2048]{1,0:T(8,128)(2,1)S(1)}, u32[]{:S(2)}, u32[]{:S(2)}) collective-permute-start(bf16[256,2048]{1,0:T(8,128)(2,1)} %add_block.14), channel_id=1, source_target_pairs={{0,2},{1,3},{2,4},{3,5},{8,10},{9,11},{10,12},{11,13},{16,18},{17,... | collective-permute-start | bytes 3145736 | tf_op jit(solution)/shard_map/ppermute | solution.py:56
  909.3 23.0 %collective-permute-start.9 = (bf16[256,2048]{1,0:T(8,128)(2,1)}, bf16[256,2048]{1,0:T(8,128)(2,1)}, u32[]{:S(2)}, u32[]{:S(2)}) collective-permute-start(bf16[256,2048]{1,0:T(8,128)(2,1)} %add_block.15), channel_id=1, source_target_pairs={{4,2},{5,3},{6,4},{7,5},{12,10},{13,11},{14,12},{15,13},{20,18},{2... | collective-permute-start | bytes 3145736 | tf_op jit(solution)/shard_map/ppermute | solution.py:56
  916.7 15.3 %copy-start.81 = (f32[1,1024]{1,0:T(1,128)S(1)}, f32[1,1024]{1,0:T(1,128)}, u32[]{:S(2)}) copy-start(f32[1,1024]{1,0:T(1,128)} %get-tuple-element.151) | copy-start | bytes 12292
  934.6 16.0 %slice-start = ((s8[7077888]{0:T(1024)(128)(4,1)}), s8[4194304]{0:T(1024)(128)(4,1)S(1)}, s32[]{:S(2)}) async-start(s8[7077888]{0:T(1024)(128)(4,1)} %bitcast.109), calls=%async_computation.2 | async-start | bytes 8388608
  935.8 54.8 %collective-permute-start.10 = (bf16[256,2048]{1,0:T(8,128)(2,1)}, bf16[256,2048]{1,0:T(8,128)(2,1)}, u32[]{:S(2)}, u32[]{:S(2)}) collective-permute-start(bf16[256,2048]{1,0:T(8,128)(2,1)} %add_block.16), channel_id=1, source_target_pairs={{0,2},{1,3},{2,4},{3,5},{4,6},{5,7},{8,10},{9,11},{10,12},{11,13},... | collective-permute-start | bytes 3145736 | tf_op jit(solution)/shard_map/ppermute | solution.py:56
  946.7 43.9 %collective-permute-start.11 = (bf16[256,2048]{1,0:T(8,128)(2,1)}, bf16[256,2048]{1,0:T(8,128)(2,1)}, u32[]{:S(2)}, u32[]{:S(2)}) collective-permute-start(bf16[256,2048]{1,0:T(8,128)(2,1)} %add_block.17), channel_id=1, source_target_pairs={{2,0},{3,1},{4,2},{5,3},{6,4},{7,5},{10,8},{11,9},{12,10},{13,11},... | collective-permute-start | bytes 3145736 | tf_op jit(solution)/shard_map/ppermute | solution.py:56
  952.3 197.6 %collective-permute-start.4 = (bf16[432,2048]{1,0:T(8,128)(2,1)}, bf16[432,2048]{1,0:T(8,128)(2,1)S(1)}, u32[]{:S(2)}, u32[]{:S(2)}) collective-permute-start(bf16[432,2048]{1,0:T(8,128)(2,1)} %add_block.12), channel_id=1, source_target_pairs={{0,2},{1,3},{2,4},{3,5},{4,6},{5,7},{8,10},{9,11},{10,12},{11,13},... | collective-permute-start | bytes 5308424 | tf_op jit(solution)/shard_map/ppermute | solution.py:56
  960.2 190.9 %collective-permute-start.5 = (bf16[432,2048]{1,0:T(8,128)(2,1)}, bf16[432,2048]{1,0:T(8,128)(2,1)S(1)}, u32[]{:S(2)}, u32[]{:S(2)}) collective-permute-start(bf16[432,2048]{1,0:T(8,128)(2,1)} %add_block.13), channel_id=1, source_target_pairs={{2,0},{3,1},{4,2},{5,3},{6,4},{7,5},{10,8},{11,9},{12,10},{13,11},... | collective-permute-start | bytes 5308424 | tf_op jit(solution)/shard_map/ppermute | solution.py:56
  1169.0 17.5 %slice-start.3 = ((s8[8388608]{0:T(1024)(128)(4,1)}), s8[4194304]{0:T(1024)(128)(4,1)S(1)}, s32[]{:S(2)}) async-start(s8[8388608]{0:T(1024)(128)(4,1)} %bitcast.113), calls=%async_computation.5 | async-start | bytes 8388608
  (82 other events, 369.0 us)
Sparse Core Ops, SparseCore 0:
  14.1 165.7 all-gather.1
  535.9 560.3 all-reduce.8

commit v4 on v3

--- a/solution.py
+++ b/solution.py
@@ -852,29 +852,111 @@
     )(*grads, *weights, small)
 
 
-def part_kernel(valid, inner_ref, down_ref, small_ref, mine_ref, other_ref):
-    for half, out in enumerate((mine_ref, other_ref)):
+def part_kernel(
+    valid, inner_ref, down_ref, small_ref, out_ref, mine, other, pair, core_send, core_recv, out_sem
+):
+    place, me = lax.axis_index("dp"), lax.axis_index("fsdp")
+    partner = (place, me + 1 - 2 * (me % 2))
+    mesh = pl.DeviceIdType.MESH
+    turn, tile = pl.program_id(0), pl.program_id(1)
+    turns, tiles = pl.num_programs(0), pl.num_programs(1)
+    span = small_ref.shape[-1]
+    slot = lax.rem(turn, 2)
+    columns = pl.ds(pl.multiple_of(tile * span, 128), span)
+
+    def core_copy(at_turn, at_tile):
+        where = pl.ds(pl.multiple_of(at_tile * span, 128), span)
+        return pltpu.make_async_remote_copy(
+            src_ref=other.at[lax.rem(at_turn, 2), :, where],
+            dst_ref=pair.at[at_turn, :, where],
+            send_sem=core_send.at[lax.rem(at_turn, 2), at_tile],
+            recv_sem=core_recv.at[at_turn, at_tile],
+            device_id=partner,
+            device_id_type=mesh,
+        )
+
+    def out_copy(at_turn):
+        return pltpu.make_async_copy(mine.at[at_turn], out_ref.at[at_turn], out_sem.at[at_turn])
+
+    def settle(at_turn):
+        def take(at_tile, _):
+            core_copy(at_turn, at_tile).wait_recv()
+            return 0
+
+        lax.fori_loop(0, tiles, take, 0)
+        mine[at_turn] = (mine[at_turn].astype(FULL) + pair[at_turn].astype(FULL)).astype(LOW)
+        out_copy(at_turn).start()
+
+    @pl.when((turn == 0) & (tile == 0))
+    def _():
+        barrier = pltpu.get_barrier_semaphore()
+        pl.semaphore_signal(barrier, inc=1, device_id=partner, device_id_type=mesh)
+        pl.semaphore_wait(barrier, 1)
+
+    @pl.when((turn > 0) & (tile == 0))
+    def _():
+        settle(turn - 1)
+
+    @pl.when(turn > 1)
+    def _():
+        core_copy(turn - 2, tile).wait_send()
+
+    for half in range(2):
         where = slice(half * valid, (half + 1) * valid)
-        out[0, :valid] = multiply(inner_ref[where], down_ref[...]).astype(LOW)
-        out[0, valid:] = small_ref[0, half]
+        part = multiply(inner_ref[where], down_ref[...]).astype(LOW)
+        if half == 0:
+            mine[turn, :valid, columns] = part
+            mine[turn, valid:, columns] = small_ref[0, 0]
+        else:
+            other[slot, :valid, columns] = part
+            other[slot, valid:, columns] = small_ref[0, 1]
+    core_copy(turn, tile).start()
+
+    @pl.when((turn == turns - 1) & (tile == tiles - 1))
+    def _():
+        settle(turn)
+
+        def take(at_tile, _):
+            core_copy(turn, at_tile).wait_send()
+
+            @pl.when(turn > 0)
+            def _():
+                core_copy(turn - 1, at_tile).wait_send()
+
+            return 0
+
+        lax.fori_loop(0, tiles, take, 0)
+        for at_turn in range(mine.shape[0]):
+            out_copy(at_turn).wait()
 
 
 def part_chunks(valid, inner, down, small):
     chips, _, extra, width = small.shape
     units = inner.shape[1]
     tile = math.gcd(width, 512)
-    out = pl.BlockSpec((1, valid + extra, tile), lambda p, j: (p, 0, j))
+    block = (valid + extra, width)
+    dma = pltpu.SemaphoreType.DMA
     return pl.pallas_call(
         functools.partial(part_kernel, valid),
-        out_shape=[jax.ShapeDtypeStruct((chips, valid + extra, width), LOW)] * 2,
+        out_shape=jax.ShapeDtypeStruct((chips, *block), LOW),
         grid=(chips, width // tile),
         in_specs=[
             pl.BlockSpec((2 * valid, units), lambda p, j: (p, 0)),
             pl.BlockSpec((units, tile), lambda p, j: (0, j)),
             pl.BlockSpec((1, 2, extra, tile), lambda p, j: (p, 0, 0, j)),
         ],
-        out_specs=[out] * 2,
-        compiler_params=pltpu.CompilerParams(vmem_limit_bytes=48 * MIB),
+        out_specs=pl.BlockSpec(memory_space=pl.ANY),
+        scratch_shapes=[
+            pltpu.VMEM((chips, *block), LOW),
+            pltpu.VMEM((2, *block), LOW),
+            pltpu.VMEM((chips, *block), LOW),
+            dma((2, width // tile)),
+            dma((chips, width // tile)),
+            dma((chips,)),
+        ],
+        compiler_params=pltpu.CompilerParams(
+            collective_id=11, has_side_effects=True, vmem_limit_bytes=52 * MIB
+        ),
         cost_estimate=SMALL,
         name="part_chunks",
     )(inner, down, small)
@@ -933,7 +1015,7 @@
 
     @pl.when(pl.program_id(0) == pl.num_programs(0) - 1)
     def _():
-        rows_grad, part_ref[...] = norm_back(rows_ref[...], gain_ref[...], held[...])
+        rows_grad, part_ref[...] = norm_back(rows_ref[...].astype(FULL), gain_ref[...], held[...])
         out_ref[...] = total_ref[...] + rows_grad
 
 
@@ -1242,6 +1324,80 @@
         right,
         *([] if gains is None else [gains]),
     )
+
+
+def entry_forward_kernel(rows_ref, gain_ref, weight_ref, hidden_ref, out_ref):
+    @pl.when(pl.program_id(0) == 0)
+    def _():
+        hidden_ref[...] = normalize(rows_ref[...].astype(FULL), gain_ref[...]).astype(LOW)
+
+    out_ref[...] = multiply(hidden_ref[...], weight_ref[...]).astype(LOW)
+
+
+def entry_forward(rows, gain, weight):
+    count, width = rows.shape
+    columns = weight.shape[1]
+    tile = math.gcd(columns, 512)
+    whole = pl.BlockSpec((count, width), lambda j: (0, 0))
+    return pl.pallas_call(
+        entry_forward_kernel,
+        out_shape=[
+            jax.ShapeDtypeStruct((count, width), LOW),
+            jax.ShapeDtypeStruct((count, columns), LOW),
+        ],
+        grid=(columns // tile,),
+        in_specs=[
+            whole,
+            pl.BlockSpec((1, width), lambda j: (0, 0)),
+            pl.BlockSpec((width, tile), lambda j: (0, j)),
+        ],
+        out_specs=[whole, pl.BlockSpec((count, tile), lambda j: (0, j))],
+        compiler_params=pltpu.CompilerParams(vmem_limit_bytes=48 * MIB),
+        cost_estimate=SMALL,
+        name="entry_forward",
+    )(rows, gain.reshape(1, width), weight)
+
+
+def middle_forward_kernel(mixed_ref, rows_ref, gain_ref, weight_ref, *refs):
+    mid_ref, hidden_ref = refs[-2:]
+    tile = weight_ref.shape[1]
+    where = pl.ds(pl.multiple_of(pl.program_id(0) * tile, 128), tile)
+    mid_ref[:, where] = rows_ref[:, where].astype(FULL) + multiply(mixed_ref[...], weight_ref[...])
+
+    @pl.when(pl.program_id(0) == pl.num_programs(0) - 1)
+    def _():
+        count = mid_ref.shape[0]
+        hidden_ref[:count] = normalize(mid_ref[...], gain_ref[...]).astype(LOW)
+        if len(refs) > 2:
+            hidden_ref[count:] = refs[0][...]
+
+
+def middle_forward(mixed, rows, gain, weight, below=None):
+    count, width = rows.shape
+    features = mixed.shape[1]
+    tile = math.gcd(width, 512)
+    fixed = lambda j: (0, 0)
+    extra = [] if below is None else [below]
+    total = count + sum(value.shape[0] for value in extra)
+    return pl.pallas_call(
+        middle_forward_kernel,
+        out_shape=[
+            jax.ShapeDtypeStruct((count, width), FULL),
+            jax.ShapeDtypeStruct((total, width), LOW),
+        ],
+        grid=(width // tile,),
+        in_specs=[
+            pl.BlockSpec((count, features), fixed),
+            pl.BlockSpec((count, width), fixed),
+            pl.BlockSpec((1, width), fixed),
+            pl.BlockSpec((features, tile), lambda j: (0, j)),
+        ]
+        + [pl.BlockSpec(value.shape, fixed) for value in extra],
+        out_specs=[pl.BlockSpec((count, width), fixed), pl.BlockSpec((total, width), fixed)],
+        compiler_params=pltpu.CompilerParams(vmem_limit_bytes=48 * MIB),
+        cost_estimate=SMALL,
+        name="middle_forward",
+    )(mixed, rows, gain.reshape(1, width), weight, *extra)
 
 
 def stacked(refs, columns=slice(None)):
@@ -1550,12 +1706,10 @@
     )
     backs = lax.all_gather(pack(prefix_back, action_back), "fsdp", axis=0, tiled=True)
 
-    prefix_flat, action_flat = padded(prefix_in.astype(FULL), action_in.astype(FULL))
-    prefix_hidden = normalize(prefix_flat, prefix_gain_in).astype(LOW)
-    action_hidden = normalize(action_flat, action_gain_in).astype(LOW)
-    prefix_all = multiply(prefix_hidden, prefix_qkv).astype(LOW)
+    prefix_flat, action_flat = padded(prefix_in, action_in)
+    prefix_hidden, prefix_all = entry_forward(prefix_flat, prefix_gain_in, prefix_qkv)
     prefix_all = prefix_all.reshape(items, prefix_pad, columns)
-    action_all = multiply(action_hidden, action_qkv).astype(LOW)
+    action_hidden, action_all = entry_forward(action_flat, action_gain_in, action_qkv)
     action_all = action_all.reshape(items, action_pad, columns)
     far = copies * (prefix_rows + action_rows)
 
@@ -1584,12 +1738,9 @@
     backs, prefix_mixed = lax.optimization_barrier((backs, prefix_mixed))
     action_mixed = action_mixed.reshape(action_tokens, features)
     prefix_mixed = prefix_mixed.reshape(prefix_tokens, features)
-    prefix_mid = prefix_flat + multiply(prefix_mixed, prefix_o)
-    action_mid = action_flat + multiply(action_mixed, action_o)
-
-    hidden = pack(
-        normalize(prefix_mid, prefix_gain).astype(LOW),
-        normalize(action_mid, action_gain).astype(LOW),
+    action_mid, action_ffn = middle_forward(action_mixed, action_flat, action_gain, action_o)
+    prefix_mid, hidden = middle_forward(
+        prefix_mixed, prefix_flat, prefix_gain, prefix_o, fold(action_ffn)[0]
     )
     inner, gate_grad, up_grad, all_rows, all_back, small = feed_all(
         prefix_tokens, hidden, backs, prefix_gate, prefix_up, prefix_down
@@ -1634,7 +1785,7 @@
         prefix_down,
         halves(multiply(action_inner, action_down)),
     )
-    sent, gate_grad = lax.optimization_barrier((add_pairs(11, *parts), gate_grad))
+    sent, gate_grad = lax.optimization_barrier((parts, gate_grad))
     out_sums = Relay(line, sent, lambda chip: line.chip ^ chip)
     out_sums.advance(1)
     small = halves(

time: 1220 us -> 1200 us (0.984)
  Pallas kernels: 886 us -> 928 us
  matrix products: 154 us -> 117 us
  local copies, waits for them, and re-layouts: 94.7 us -> 82.1 us
    pallas_call x1 -> x5, Pallas kernels: 38.9 us -> 68.4 us  [the longest x1 47.5 us: part_chunks(): pl.pallas_call(functools.partial(part_kernel, valid), out_shape=jax.Shape...]
    dot_general x7 -> x3, matrix products: 29.2 us -> 2.84 us  [multiply(): return jnp.dot(left, right, preferred_element_type=FULL)]
    pallas_call x1, Pallas kernels: 63.9 us -> 80.4 us  [mix_call(): pl.pallas_call(functools.partial(mix_back_kernel, scale, shares_of(shards...]
    pallas_call x3 -> x2, Pallas kernels: 33 us -> 17.2 us  [add_pairs(): pl.pallas_call(pair_kernel, out_shape=jax.ShapeDtypeStruct(mine.shape, LO...]
    unnamed x198 -> x200, local copies, waits for them, and re-layouts: 65.3 us -> 57.7 us
  transfers between devices with their start and end apart: 14 -> 14, of which waited for: 0 -> 0; matrix products, arithmetic and copies ran while one was open for 6% -> 3% of each run, Pallas kernels for 58% -> 62%
where the time goes in v4:
time: 1200 us; the launch traced here: 1190 us
  Pallas kernels  928 us (77%)
  matrix products  117 us (10%)
  local copies, waits for them, and re-layouts  82.1 us (7%)
  starting transfers between devices  30.2 us (3%)
  between operations  15.5 us (1%)
  other arithmetic  12.9 us (1%)
    pallas_call x1, Pallas kernels, collect(): pl.pallas_call(functools.partial(collect_kernel, valid, transposed, count...  156 us
    pallas_call x1, Pallas kernels, feed_all(): pl.pallas_call(functools.partial(feed_kernel, valid), out_shape=[jax.Shap...  154 us
    pallas_call x1, Pallas kernels, tail_sums(): pl.pallas_call(functools.partial(tail_kernel, CopySum.split_of(shapes)),...  150 us
    dot_general x7, matrix products, multiply_left(): lax.dot_general(left, right, (((0,), (0,)), ((), ())), preferred_element_...  113 us
    pallas_call x1, Pallas kernels, gather_shards(): pl.pallas_call(functools.partial(gather_kernel, shares_of(shards)), out_s...  110 us
    pallas_call x1, Pallas kernels, mix_call(): pl.pallas_call(functools.partial(mix_kernel, scale, features, shares_of(s...  83.3 us
    pallas_call x1, Pallas kernels, mix_call(): pl.pallas_call(functools.partial(mix_back_kernel, scale, shares_of(shards...  80.4 us
    unnamed x200, local copies, waits for them, and re-layouts  57.7 us
  transfers between devices with their start and end apart: 14, of which 0 were waited for; matrix products, arithmetic and copies ran while one was open for 3% of the time, Pallas kernels for 62%

profile of v4, /device:TPU:0, one launch (start us, length us, event | category | flops | bytes accessed | tf_op | source)
XLA Modules:
  0.0 1185.9 jit_solution(62524519455701771)
XLA Ops:
  18.1 109.8 %gather_shards.1 = (bf16[2048,2560]{1,0:T(8,128)(2,1)}, bf16[1024,2560]{1,0:T(8,128)(2,1)}, bf16[128,128]{1,0:T(8,128)(2,1)}) custom-call(bf16[256,2560]{1,0:T(8,128)(2,1)} %pad_maximum_fusion.2.refs_0_, bf16[128,2560]{1,0:T(8,128)(2,1)} %pad_maximum_fusion.3.refs_1_, bf16[16,128]{1,0:T(8,128)(2,1)} %fusion.25.refs_2_), custom_call_target="tpu_custom_call" | custom-call | flops 1 | bytes 1 | tf_op jit(solution)/shard_map/gather_shards/pallas_call | solution.py:413
  129.5 8.9 entry_forward.2
  145.8 83.3 %mix.1 = (bf16[2,208,2048]{2,1,0:T(8,128)(2,1)S(1)}, bf16[2,16,2048]{2,1,0:T(8,128)(2,1)S(1)}, bf16[4,2,224,512]{3,2,1,0:T(8,128)(2,1)}, bf16[2048,2048]{1,0:T(8,128)(2,1)}, bf16[2048,1024]{1,0:T(8,128)(2,1)}) custom-call(bf16[2,208,2560]{2,1,0:T(8,128)(2,1)} %bitcast.98, bf16[2,16,2560]{2,1,0:T(8,128)(2,1)S(1)} %bitcast.110, ...), custom_call_target="tpu_custom_call" | custom-call | flops 1 | bytes 1 | tf_op jit(solution)/shard_map/mix/pallas_call | solution.py:1573
  235.5 8.8 middle_forward.3
  245.5 154.1 %feed_all.1 = (bf16[3328,2048]{1,0:T(8,128)(2,1)}, bf16[3328,2048]{1,0:T(8,128)(2,1)}, bf16[3328,2048]{1,0:T(8,128)(2,1)}, bf16[3328,2048]{1,0:T(8,128)(2,1)}, b...) custom-call(bf16[432,2048]{1,0:T(8,128)(2,1)} %copy-done.28, ...), custom_call_target="tpu_custom_call" | custom-call | flops 1 | bytes 1 | tf_op jit(solution)/shard_map/feed_all/pallas_call | solution.py:651
  399.6 36.6 %convolution_convert_fusion.2 = bf16[2048,2048]{1,0:T(8,128)(2,1)} fusion(bf16[3328,2048]{1,0:T(8,128)(2,1)} %get-tuple-element.129.inner_ref, bf16[3328,2048]{1,0:T(8,128)(2,1)} %get-tuple-element.121), kind=kOutput, calls=%fused_computation.2 | convolution fusion | flops 27921481728 | bytes 35651584 | tf_op jit(solution)/shard_map/dot_general | solution.py:29
  436.1 34.3 %convolution_convert_fusion.1 = bf16[2048,2048]{1,0:T(8,128)(2,1)} fusion(bf16[3328,2048]{1,0:T(8,128)(2,1)} %get-tuple-element.122, bf16[3328,2048]{1,0:T(8,128)(2,1)S(1)} %copy-done.54), kind=kOutput, calls=%fused_computation.1 | convolution fusion | flops 27921481728 | bytes 35651584 | tf_op jit(solution)/shard_map/dot_general | solution.py:29
  470.5 36.5 %convolution_convert_fusion = bf16[2048,2048]{1,0:T(8,128)(2,1)} fusion(bf16[3328,2048]{1,0:T(8,128)(2,1)} %get-tuple-element.122, bf16[3328,2048]{1,0:T(8,128)(2,1)} %get-tuple-element.133.refs_1_), kind=kOutput, calls=%fused_computation | convolution fusion | flops 27921481728 | bytes 35651584 | tf_op jit(solution)/shard_map/dot_general | solution.py:29
  518.3 47.5 %part_chunks.1.value_ref = bf16[4,432,2048]{2,1,0:T(8,128)(2,1)} custom-call(bf16[3328,2048]{1,0:T(8,128)(2,1)} %get-tuple-element.129.inner_ref, bf16[2048,2048]{1,0:T(8,128)(2,1)} %down_ref.3, bf16[4,2,16,2048]{3,2,1,0:T(8,128)(2,1)S(1)} %reshape.367.small_ref), custom_call_target="tpu_custom_call" | custom-call | flops 1 | bytes 1 | tf_op jit(solution)/shard_map/part_chunks/pallas_call | solution.py:939
  576.6 156.5 %collect.1.grad_ref = f32[432,2048]{1,0:T(8,128)} custom-call(bf16[3328,2048]{1,0:T(8,128)(2,1)} %get-tuple-element.132.refs_0_, bf16[3328,2048]{1,0:T(8,128)(2,1)} %get-tuple-element.133.refs_1_, bf16[2048,2048]{1,0:T(8,128)(2,1)} %refs_2_.1, bf16[2048,2048]{1,0:T(8,128)(2,1)} %refs_3_.1, bf16[4,2,16,2048]{3,2,1,0:T(8,128)(2,1)} %reshape.370.refs_4_), custom_call_target="tpu_custom_call" | custom-call | flops 1 | bytes 1 | tf_op jit(solution)/shard_map/collect/pallas_call | solution.py:829
  746.8 14.1 %middle_back.2 = (f32[416,2048]{1,0:T(8,128)}, bf16[416,2048]{1,0:T(8,128)(2,1)}, bf16[416,2048]{1,0:T(8,128)(2,1)}, f32[1,2048]{1,0:T(1,128)}) custom-call(f32[432,2048]{1,0:T(8,128)} %collect.1.grad_ref, f32[416,2048]{1,0:T(8,128)} %get-tuple-element.115.rows_ref, bf16[416,2048]{1,0:T(8,128)(2,1)} %bitcast.129, f32[1,2048]{1,0:T(1,128)} %bitcast.121, ...), custom_call_target="tpu_custom_call" | custom-call | flops 1 | bytes 1 | tf_op jit(solution)/shard_map/middle_back/pallas_call | solution.py:989
  773.2 7.5 add_pairs.2.value_ref
  789.5 5.0 middle_back.3
  796.4 80.4 %mix_back.1 = (bf16[2,208,2048]{2,1,0:T(8,128)(2,1)S(1)}, bf16[2,16,2048]{2,1,0:T(8,128)(2,1)S(1)}, bf16[2,224,512]{2,1,0:T(8,128)(2,1)S(1)}, bf16[256,4096]{1,0:T(8,128)(2,1)}) custom-call(bf16[2,208,2560]{2,1,0:T(8,128)(2,1)} %bitcast.100, bf16[2,16,2560]{2,1,0:T(8,128)(2,1)S(1)} %bitcast.112, bf16[2,208,2048]{2,1,0:T(8,128)(2,1)S(1)} %bitcast.109, ...), custom_call_target="tpu_custom_call" | custom-call | flops 1 | bytes 1 | tf_op jit(solution)/shard_map/mix_back/pallas_call | solution.py:1595
  894.2 4.7 entry_back.3
  899.7 13.9 %entry_back.2 = (f32[416,2048]{1,0:T(8,128)}, f32[1,2048]{1,0:T(1,128)}) custom-call(bf16[416,2048]{1,0:T(8,128)(2,1)} %bitcast.106, bf16[416,512]{1,0:T(8,128)(2,1)} %bitcast.131, bf16[416,2048]{1,0:T(8,128)(2,1)} %bitcast.93, f32[416,2048]{1,0:T(8,128)} %get-tuple-element.157.total_ref, f32[1,2048]{1,0:T(1,128)} %bitcast.123, ...), custom_call_target="tpu_custom_call" | custom-call | flops 1 | bytes 1 | tf_op jit(solution)/shard_map/entry_back/pallas_call | solution.py:1027
  920.5 4.7 collective-permute-start.10
  947.9 5.0 weight_shares.6.mine_ref
  953.0 5.0 weight_shares.7.other_ref
  958.7 9.7 add_pairs.3.refs_2_
  973.1 150.2 %tail_sums.1 = (f32[256,2048]{1,0:T(8,128)}, f32[256,1024]{1,0:T(8,128)}, f32[128,2560]{1,0:T(8,128)}, f32[256,2560]{1,0:T(8,128)}, f32[16,2560]{1,0:T(8,128)}, /*index=5*/bf16[256,2560]{1,0:T(8,128)(2,1)}) custom-call(bf16[256,2048]{1,0:T(8,128)(2,1)} %convert_element_type.75.refs_0_, bf16[256,1024]{1,0:T(8,128)(2,1)} %convolution_convert_fusion.6.refs_1_, ...), custom_call_target="tpu_custom_call" | custom-call | flops 30000001024 | bytes 1 | tf_op jit(solution)/shard_map/tail_sums/pallas_call | solution.py:1236
  1146.5 7.1 widen.6
  1156.9 7.1 widen.7
  1164.0 6.5 widen.8
  (325 shorter events, 173.3 us)
Async XLA Ops:
  7.2 504.4 %copy-start = (bf16[1024,512]{1,0:T(8,128)(2,1)S(1)}, bf16[1024,512]{1,0:T(8,128)(2,1)}, u32[]{:S(2)}) copy-start(bf16[1024,512]{1,0:T(8,128)(2,1)} %param.42) | copy-start | bytes 3145732
  7.2 226.8 %all-gather.2.cloned.1.call-start = ((), (), s32[]{:S(2)}) async-start(), calls=%async_computation | async-start | bytes 15925248 | tf_op jit(solution)/shard_map/all_gather | solution.py:1707
  14.0 1118.2 %all-reduce.9.cloned.1.call-start = ((), (), s32[]{:S(2)}) async-start(), calls=%async_computation.1 | async-start | bytes 56623104 | tf_op jit(solution)/shard_map/psum | solution.py:1781
  15.0 112.9 %copy-start.62 = (bf16[2,204,2048]{2,0,1:T(2,128)(2,1)S(1)}, bf16[2,204,2048]{2,0,1:T(2,128)(2,1)}, u32[]{:S(2)}) copy-start(bf16[2,204,2048]{2,0,1:T(2,128)(2,1)} %param.23) | copy-start | bytes 5013508
  128.7 105.3 %copy-start.8 = (bf16[2,208,2048]{2,1,0:T(8,128)(2,1)}, bf16[2,208,2048]{2,1,0:T(8,128)(2,1)S(1)}, u32[]{:S(2)}) copy-start(bf16[2,208,2048]{2,1,0:T(8,128)(2,1)S(1)} %pad.25.clone) | copy-start | bytes 5111812
  140.9 89.4 %copy-start.32 = (bf16[2,16,1024]{2,1,0:T(8,128)(2,1)}, bf16[2,16,1024]{2,1,0:T(8,128)(2,1)S(1)}, u32[]{:S(2)}) copy-start(bf16[2,16,1024]{2,1,0:T(8,128)(2,1)S(1)} %pad.27.clone) | copy-start | bytes 196612
  140.9 89.4 %copy-start.52 = (f32[8,128]{1,0:T(8,128)}, f32[8,128]{1,0:T(8,128)S(1)}, u32[]{:S(2)}) copy-start(f32[8,128]{1,0:T(8,128)S(1)} %get-tuple-element.211) | copy-start | bytes 12292
  144.2 85.0 %copy-start.30 = (bf16[32,2560]{1,0:T(8,128)(2,1)}, bf16[32,2560]{1,0:T(8,128)(2,1)S(1)}, u32[]{:S(2)}) copy-start(bf16[32,2560]{1,0:T(8,128)(2,1)S(1)} %get-tuple-element.108) | copy-start | bytes 491524
  145.7 83.4 %copy-start.17 = (f32[2,224,896]{2,1,0:T(8,128)}, f32[2,224,896]{2,1,0:T(8,128)S(1)}, u32[]{:S(2)}) copy-start(f32[2,224,896]{2,1,0:T(8,128)S(1)} %or_select_fusion.refs_4_) | copy-start | bytes 4816900
  399.5 36.6 %copy-start.54 = (bf16[3328,2048]{1,0:T(8,128)(2,1)S(1)}, bf16[3328,2048]{1,0:T(8,128)(2,1)}, u32[]{:S(2)}) copy-start(bf16[3328,2048]{1,0:T(8,128)(2,1)} %get-tuple-element.132.refs_0_) | copy-start | bytes 40894468
  570.2 162.9 %collective-permute-start = (bf16[432,2048]{1,0:T(8,128)(2,1)}, bf16[432,2048]{1,0:T(8,128)(2,1)}, u32[]{:S(2)}, u32[]{:S(2)}) collective-permute-start(bf16[432,2048]{1,0:T(8,128)(2,1)} %get-tuple-element.195), channel_id=1, source_target_pairs={{0,2},{1,3},{8,10},{9,11},{16,18},{17,19},{24,26},{25,27}} | collective-permute-start | bytes 5308424 | tf_op jit(solution)/shard_map/ppermute | solution.py:56
  572.8 160.3 %collective-permute-start.1 = (bf16[432,2048]{1,0:T(8,128)(2,1)}, bf16[432,2048]{1,0:T(8,128)(2,1)}, u32[]{:S(2)}, u32[]{:S(2)}) collective-permute-start(bf16[432,2048]{1,0:T(8,128)(2,1)} %get-tuple-element.194), channel_id=1, source_target_pairs={{6,4},{7,5},{14,12},{15,13},{22,20},{23,21},{30,28},{31,29}} | collective-permute-start | bytes 5308424 | tf_op jit(solution)/shard_map/ppermute | solution.py:56
  739.4 141.2 %collective-permute-start.2 = (bf16[432,2048]{1,0:T(8,128)(2,1)}, bf16[432,2048]{1,0:T(8,128)(2,1)S(1)}, u32[]{:S(2)}, u32[]{:S(2)}) collective-permute-start(bf16[432,2048]{1,0:T(8,128)(2,1)} %add_block.10), channel_id=1, source_target_pairs={{0,2},{1,3},{2,4},{3,5},{8,10},{9,11},{10,12},{11,13},{16,18},{17,... | collective-permute-start | bytes 5308424 | tf_op jit(solution)/shard_map/ppermute | solution.py:56
  744.9 135.7 %collective-permute-start.3 = (bf16[432,2048]{1,0:T(8,128)(2,1)}, bf16[432,2048]{1,0:T(8,128)(2,1)}, u32[]{:S(2)}, u32[]{:S(2)}) collective-permute-start(bf16[432,2048]{1,0:T(8,128)(2,1)} %add_block.11), channel_id=1, source_target_pairs={{4,2},{5,3},{6,4},{7,5},{12,10},{13,11},{14,12},{15,13},{20,18},{2... | collective-permute-start | bytes 5308424 | tf_op jit(solution)/shard_map/ppermute | solution.py:56
  784.4 96.3 %collective-permute-start.6 = (bf16[256,2048]{1,0:T(8,128)(2,1)}, bf16[256,2048]{1,0:T(8,128)(2,1)}, u32[]{:S(2)}, u32[]{:S(2)}) collective-permute-start(bf16[256,2048]{1,0:T(8,128)(2,1)} %get-tuple-element.197), channel_id=1, source_target_pairs={{0,2},{1,3},{8,10},{9,11},{16,18},{17,19},{24,26},{25,27}} | collective-permute-start | bytes 3145736 | tf_op jit(solution)/shard_map/ppermute | solution.py:56
  787.2 93.4 %collective-permute-start.7 = (bf16[256,2048]{1,0:T(8,128)(2,1)}, bf16[256,2048]{1,0:T(8,128)(2,1)}, u32[]{:S(2)}, u32[]{:S(2)}) collective-permute-start(bf16[256,2048]{1,0:T(8,128)(2,1)} %get-tuple-element.196), channel_id=1, source_target_pairs={{6,4},{7,5},{14,12},{15,13},{22,20},{23,21},{30,28},{31,29}} | collective-permute-start | bytes 3145736 | tf_op jit(solution)/shard_map/ppermute | solution.py:56
  796.4 82.3 %copy-start.80 = (f32[1,2048]{1,0:T(1,128)S(1)}, f32[1,2048]{1,0:T(1,128)}, u32[]{:S(2)}) copy-start(f32[1,2048]{1,0:T(1,128)} %get-tuple-element.159) | copy-start | bytes 24580
  796.4 84.2 %copy-start.81 = (f32[1,1024]{1,0:T(1,128)S(1)}, f32[1,1024]{1,0:T(1,128)}, u32[]{:S(2)}) copy-start(f32[1,1024]{1,0:T(1,128)} %get-tuple-element.163) | copy-start | bytes 12292
  886.2 28.4 %collective-permute-start.8 = (bf16[256,2048]{1,0:T(8,128)(2,1)}, bf16[256,2048]{1,0:T(8,128)(2,1)}, u32[]{:S(2)}, u32[]{:S(2)}) collective-permute-start(bf16[256,2048]{1,0:T(8,128)(2,1)} %add_block.14), channel_id=1, source_target_pairs={{0,2},{1,3},{2,4},{3,5},{8,10},{9,11},{10,12},{11,13},{16,18},{17,... | collective-permute-start | bytes 3145736 | tf_op jit(solution)/shard_map/ppermute | solution.py:56
  892.8 21.8 %collective-permute-start.9 = (bf16[256,2048]{1,0:T(8,128)(2,1)}, bf16[256,2048]{1,0:T(8,128)(2,1)S(1)}, u32[]{:S(2)}, u32[]{:S(2)}) collective-permute-start(bf16[256,2048]{1,0:T(8,128)(2,1)} %add_block.15), channel_id=1, source_target_pairs={{4,2},{5,3},{6,4},{7,5},{12,10},{13,11},{14,12},{15,13},{20,18},{2... | collective-permute-start | bytes 3145736 | tf_op jit(solution)/shard_map/ppermute | solution.py:56
  920.5 48.0 %collective-permute-start.10 = (bf16[256,2048]{1,0:T(8,128)(2,1)}, bf16[256,2048]{1,0:T(8,128)(2,1)}, u32[]{:S(2)}, u32[]{:S(2)}) collective-permute-start(bf16[256,2048]{1,0:T(8,128)(2,1)} %add_block.16), channel_id=1, source_target_pairs={{0,2},{1,3},{2,4},{3,5},{4,6},{5,7},{8,10},{9,11},{10,12},{11,13},... | collective-permute-start | bytes 3145736 | tf_op jit(solution)/shard_map/ppermute | solution.py:56
  926.4 42.0 %collective-permute-start.11 = (bf16[256,2048]{1,0:T(8,128)(2,1)}, bf16[256,2048]{1,0:T(8,128)(2,1)}, u32[]{:S(2)}, u32[]{:S(2)}) collective-permute-start(bf16[256,2048]{1,0:T(8,128)(2,1)} %add_block.17), channel_id=1, source_target_pairs={{2,0},{3,1},{4,2},{5,3},{6,4},{7,5},{10,8},{11,9},{12,10},{13,11},... | collective-permute-start | bytes 3145736 | tf_op jit(solution)/shard_map/ppermute | solution.py:56
  932.2 200.0 %collective-permute-start.4 = (bf16[432,2048]{1,0:T(8,128)(2,1)}, bf16[432,2048]{1,0:T(8,128)(2,1)S(1)}, u32[]{:S(2)}, u32[]{:S(2)}) collective-permute-start(bf16[432,2048]{1,0:T(8,128)(2,1)} %add_block.12), channel_id=1, source_target_pairs={{0,2},{1,3},{2,4},{3,5},{4,6},{5,7},{8,10},{9,11},{10,12},{11,13},... | collective-permute-start | bytes 5308424 | tf_op jit(solution)/shard_map/ppermute | solution.py:56
  940.1 192.1 %collective-permute-start.5 = (bf16[432,2048]{1,0:T(8,128)(2,1)}, bf16[432,2048]{1,0:T(8,128)(2,1)}, u32[]{:S(2)}, u32[]{:S(2)}) collective-permute-start(bf16[432,2048]{1,0:T(8,128)(2,1)} %add_block.13), channel_id=1, source_target_pairs={{2,0},{3,1},{4,2},{5,3},{6,4},{7,5},{10,8},{11,9},{12,10},{13,11},... | collective-permute-start | bytes 5308424 | tf_op jit(solution)/shard_map/ppermute | solution.py:56
  (85 other events, 396.7 us)
Sparse Core Ops, SparseCore 0:
  14.1 166.6 all-gather.1
  516.9 574.8 all-reduce.8

commit v5 on v4

--- a/solution.py
+++ b/solution.py
@@ -1130,15 +1130,15 @@
 
 def tail_kernel(split, *refs):
     count = len(split)
-    given = count - 3
+    given = count - 7
     inputs, refs = refs[:given], refs[given:]
     summed_ref, left_ref, right_ref = refs[:3]
     totals, all_ref, refs = refs[3 : 3 + count], refs[3 + count], refs[4 + count :]
     arrived, whole, refs = refs[:count], refs[count : 2 * count], refs[2 * count :]
-    held, arrive, total, action, weights, gains, right_all = refs[:7]
-    load_sem, right_sem, line_send, line_recv = refs[7:11]
-    sums = CopySum(split, (*inputs, action, weights, gains), totals, arrived, whole, refs[11:15])
-    gather = Gather([1], [right_ref], [all_ref], refs[15:])
+    held, arrive, total, own, right_all, refs = *refs[:3], refs[3:10], refs[10], refs[11:]
+    load_sem, right_sem, line_send, line_recv = refs[:4]
+    sums = CopySum(split, (*inputs, *own), totals, arrived, whole, refs[4:8])
+    gather = Gather([1], [right_ref], [all_ref], refs[8:])
     mesh = pl.DeviceIdType.MESH
     place, me = lax.axis_index("dp"), lax.axis_index("fsdp")
     chips = lax.axis_size("fsdp") // 2
@@ -1194,8 +1194,16 @@
     fetch = pltpu.make_async_copy(all_ref, right_all, right_sem)
     fetch.start()
     fetch.wait()
-    action[...] = multiply_left(left_ref[...], right_all[...]).astype(LOW)
-    sums.send(given)
+
+    def spread(value, targets):
+        start = 0
+        for target in targets:
+            target[...] = value[:, start : start + target.shape[1]].astype(LOW)
+            start += target.shape[1]
+
+    spread(multiply_left(left_ref[...], right_all[...]), own[:3])
+    for a in range(given, given + 3):
+        sums.send(a)
     total[...] = held[chip].astype(FULL)
     for side in range(2):
 
@@ -1204,10 +1212,10 @@
             line_copy(side, chips - 1, chip).wait_recv()
             total[...] += arrive[side, chips - 2].astype(FULL)
 
-    rows = weights.shape[0]
-    weights[...] = total[:rows].astype(LOW)
-    gains[...] = total[rows:].astype(LOW)
-    for a in range(given + 1, count):
+    rows = own[3].shape[0]
+    spread(total[:rows], own[3:6])
+    spread(total[rows:], own[6:])
+    for a in range(given + 3, count):
         sums.send(a)
     for a in range(given):
         sums.finish(a)
@@ -1224,9 +1232,10 @@
         sums.finish(a)
 
 
-def tail_sums(values, summed, rows, left, right):
+def tail_sums(values, summed, rows, left, right, columns):
     chips, block = summed.shape[0], summed.shape[1:]
-    own = [(left.shape[1], right.shape[1]), (rows, block[1]), (block[0] - rows, block[1])]
+    own = [(count, width) for count in (left.shape[1], rows) for width in columns]
+    own += [(block[0] - rows, block[1])]
     shapes = [value.shape for value in values] + own
     count = len(shapes)
     dma = pltpu.SemaphoreType.DMA
@@ -1868,12 +1877,13 @@
     action_output_owned = multiply_left(
         lax.dynamic_slice_in_dim(mixed_all, line.place * rows, rows, 1), low_all
     )
-    output_owned, action_output_owned, action_qkv_owned, qkv_owned, gain_owned = tail_sums(
+    output_owned, action_output_owned, *qkv_owned, gain_owned = tail_sums(
         [output_sums.finish().astype(LOW), action_output_owned.astype(LOW)],
         sent,
         prefix_query.shape[0],
         hidden_slice,
         action_qkv_grad,
+        (features, head_size, head_size),
     )
     feed_sums, output_owned, sent = lax.optimization_barrier((feed_sums, output_owned, sent))
     out_sums.advance(3)
@@ -1890,18 +1900,14 @@
         prefix_grad,
         action_grad,
         gain_owned[cuts[0] : cuts[1]],
-        qkv_owned[:rows, :features],
-        qkv_owned[:rows, features : features + head_size],
-        qkv_owned[:rows, features + head_size :],
+        *qkv_owned[3:],
         output_owned,
         gain_owned[cuts[1] : cuts[2]],
         feed_sums[1],
         feed_sums[2],
         feed_sums[0],
         gain_owned[cuts[2] : cuts[3]],
-        action_qkv_owned[:, :features],
-        action_qkv_owned[:, features : features + head_size],
-        action_qkv_owned[:, features + head_size :],
+        *qkv_owned[:3],
         action_output_owned,
         gain_owned[cuts[3] : cuts[4]],
         *feed_sums[3:],

time: 1200 us -> 1190 us (level)
    unnamed x200 -> x216, local copies, waits for them, and re-layouts: 57.7 us -> 63.4 us
where the time goes in v5:
time: 1190 us
  Pallas kernels  928 us (78%)
  matrix products  117 us (10%)
  local copies, waits for them, and re-layouts  80.9 us (7%)
  starting transfers between devices  30.4 us (3%)
  between operations  15.5 us (1%)
  other arithmetic  12.9 us (1%)
    pallas_call x1, Pallas kernels, collect(): pl.pallas_call(functools.partial(collect_kernel, valid, transposed, count...  157 us
    pallas_call x1, Pallas kernels, feed_all(): pl.pallas_call(functools.partial(feed_kernel, valid), out_shape=[jax.Shap...  154 us
    pallas_call x1, Pallas kernels, tail_sums(): pl.pallas_call(functools.partial(tail_kernel, CopySum.split_of(shapes)),...  151 us
    dot_general x7, matrix products, multiply_left(): lax.dot_general(left, right, (((0,), (0,)), ((), ())), preferred_element_...  113 us
    pallas_call x1, Pallas kernels, gather_shards(): pl.pallas_call(functools.partial(gather_kernel, shares_of(shards)), out_s...  110 us
    pallas_call x1, Pallas kernels, mix_call(): pl.pallas_call(functools.partial(mix_kernel, scale, features, shares_of(s...  83.4 us
    pallas_call x1, Pallas kernels, mix_call(): pl.pallas_call(functools.partial(mix_back_kernel, scale, shares_of(shards...  80.3 us
    unnamed x216, local copies, waits for them, and re-layouts  63.4 us
  transfers between devices with their start and end apart: 14, of which 0 were waited for; matrix products, arithmetic and copies ran while one was open for 3% of the time, Pallas kernels for 62%

profile of v5, /device:TPU:0, one launch (start us, length us, event | category | flops | bytes accessed | tf_op | source)
XLA Modules:
  0.0 1185.5 jit_solution(14116466343136044831)
XLA Ops:
  18.1 109.8 %gather_shards.1 = (bf16[2048,2560]{1,0:T(8,128)(2,1)}, bf16[1024,2560]{1,0:T(8,128)(2,1)}, bf16[128,128]{1,0:T(8,128)(2,1)}) custom-call(bf16[256,2560]{1,0:T(8,128)(2,1)} %pad_maximum_fusion.2.refs_0_, bf16[128,2560]{1,0:T(8,128)(2,1)} %pad_maximum_fusion.3.refs_1_, bf16[16,128]{1,0:T(8,128)(2,1)} %fusion.25.refs_2_), custom_call_target="tpu_custom_call" | custom-call | flops 1 | bytes 1 | tf_op jit(solution)/shard_map/gather_shards/pallas_call | solution.py:413
  129.5 8.9 entry_forward.2
  145.7 83.4 %mix.1 = (bf16[2,208,2048]{2,1,0:T(8,128)(2,1)S(1)}, bf16[2,16,2048]{2,1,0:T(8,128)(2,1)S(1)}, bf16[4,2,224,512]{3,2,1,0:T(8,128)(2,1)}, bf16[2048,2048]{1,0:T(8,128)(2,1)}, bf16[2048,1024]{1,0:T(8,128)(2,1)}) custom-call(bf16[2,208,2560]{2,1,0:T(8,128)(2,1)} %bitcast.98, bf16[2,16,2560]{2,1,0:T(8,128)(2,1)S(1)} %bitcast.110, ...), custom_call_target="tpu_custom_call" | custom-call | flops 1 | bytes 1 | tf_op jit(solution)/shard_map/mix/pallas_call | solution.py:1582
  235.5 8.8 middle_forward.3
  245.5 154.1 %feed_all.1 = (bf16[3328,2048]{1,0:T(8,128)(2,1)}, bf16[3328,2048]{1,0:T(8,128)(2,1)}, bf16[3328,2048]{1,0:T(8,128)(2,1)}, bf16[3328,2048]{1,0:T(8,128)(2,1)}, b...) custom-call(bf16[432,2048]{1,0:T(8,128)(2,1)} %copy-done.28, ...), custom_call_target="tpu_custom_call" | custom-call | flops 1 | bytes 1 | tf_op jit(solution)/shard_map/feed_all/pallas_call | solution.py:651
  399.6 36.6 %convolution_convert_fusion.2 = bf16[2048,2048]{1,0:T(8,128)(2,1)} fusion(bf16[3328,2048]{1,0:T(8,128)(2,1)} %get-tuple-element.133.inner_ref, bf16[3328,2048]{1,0:T(8,128)(2,1)} %get-tuple-element.125), kind=kOutput, calls=%fused_computation.2 | convolution fusion | flops 27921481728 | bytes 35651584 | tf_op jit(solution)/shard_map/dot_general | solution.py:29
  436.2 34.4 %convolution_convert_fusion.1 = bf16[2048,2048]{1,0:T(8,128)(2,1)} fusion(bf16[3328,2048]{1,0:T(8,128)(2,1)} %get-tuple-element.126, bf16[3328,2048]{1,0:T(8,128)(2,1)S(1)} %copy-done.54), kind=kOutput, calls=%fused_computation.1 | convolution fusion | flops 27921481728 | bytes 35651584 | tf_op jit(solution)/shard_map/dot_general | solution.py:29
  470.6 36.5 %convolution_convert_fusion = bf16[2048,2048]{1,0:T(8,128)(2,1)} fusion(bf16[3328,2048]{1,0:T(8,128)(2,1)} %get-tuple-element.126, bf16[3328,2048]{1,0:T(8,128)(2,1)} %get-tuple-element.137.refs_1_), kind=kOutput, calls=%fused_computation | convolution fusion | flops 27921481728 | bytes 35651584 | tf_op jit(solution)/shard_map/dot_general | solution.py:29
  518.4 47.5 %part_chunks.1.value_ref = bf16[4,432,2048]{2,1,0:T(8,128)(2,1)} custom-call(bf16[3328,2048]{1,0:T(8,128)(2,1)} %get-tuple-element.133.inner_ref, bf16[2048,2048]{1,0:T(8,128)(2,1)} %down_ref.3, bf16[4,2,16,2048]{3,2,1,0:T(8,128)(2,1)S(1)} %reshape.367.small_ref), custom_call_target="tpu_custom_call" | custom-call | flops 1 | bytes 1 | tf_op jit(solution)/shard_map/part_chunks/pallas_call | solution.py:939
  576.7 156.5 %collect.1.grad_ref = f32[432,2048]{1,0:T(8,128)} custom-call(bf16[3328,2048]{1,0:T(8,128)(2,1)} %get-tuple-element.136.refs_0_, bf16[3328,2048]{1,0:T(8,128)(2,1)} %get-tuple-element.137.refs_1_, bf16[2048,2048]{1,0:T(8,128)(2,1)} %refs_2_.1, bf16[2048,2048]{1,0:T(8,128)(2,1)} %refs_3_.1, bf16[4,2,16,2048]{3,2,1,0:T(8,128)(2,1)} %reshape.370.refs_4_), custom_call_target="tpu_custom_call" | custom-call | flops 1 | bytes 1 | tf_op jit(solution)/shard_map/collect/pallas_call | solution.py:829
  746.9 14.1 %middle_back.2 = (f32[416,2048]{1,0:T(8,128)}, bf16[416,2048]{1,0:T(8,128)(2,1)}, bf16[416,2048]{1,0:T(8,128)(2,1)}, f32[1,2048]{1,0:T(1,128)}) custom-call(f32[432,2048]{1,0:T(8,128)} %collect.1.grad_ref, f32[416,2048]{1,0:T(8,128)} %get-tuple-element.119.rows_ref, bf16[416,2048]{1,0:T(8,128)(2,1)} %bitcast.129, f32[1,2048]{1,0:T(1,128)} %bitcast.121, ...), custom_call_target="tpu_custom_call" | custom-call | flops 1 | bytes 1 | tf_op jit(solution)/shard_map/middle_back/pallas_call | solution.py:989
  773.3 7.5 add_pairs.2.value_ref
  789.6 5.0 middle_back.3
  796.5 80.3 %mix_back.1 = (bf16[2,208,2048]{2,1,0:T(8,128)(2,1)S(1)}, bf16[2,16,2048]{2,1,0:T(8,128)(2,1)S(1)}, bf16[2,224,512]{2,1,0:T(8,128)(2,1)S(1)}, bf16[256,4096]{1,0:T(8,128)(2,1)}) custom-call(bf16[2,208,2560]{2,1,0:T(8,128)(2,1)} %bitcast.100, bf16[2,16,2560]{2,1,0:T(8,128)(2,1)S(1)} %bitcast.112, bf16[2,208,2048]{2,1,0:T(8,128)(2,1)S(1)} %bitcast.109, ...), custom_call_target="tpu_custom_call" | custom-call | flops 1 | bytes 1 | tf_op jit(solution)/shard_map/mix_back/pallas_call | solution.py:1604
  894.3 4.7 entry_back.3
  899.8 13.9 %entry_back.2 = (f32[416,2048]{1,0:T(8,128)}, f32[1,2048]{1,0:T(1,128)}) custom-call(bf16[416,2048]{1,0:T(8,128)(2,1)} %bitcast.106, bf16[416,512]{1,0:T(8,128)(2,1)} %bitcast.131, bf16[416,2048]{1,0:T(8,128)(2,1)} %bitcast.93, f32[416,2048]{1,0:T(8,128)} %get-tuple-element.161.total_ref, f32[1,2048]{1,0:T(1,128)} %bitcast.123, ...), custom_call_target="tpu_custom_call" | custom-call | flops 1 | bytes 1 | tf_op jit(solution)/shard_map/entry_back/pallas_call | solution.py:1027
  920.6 4.8 collective-permute-start.10
  948.3 5.0 weight_shares.6.mine_ref
  953.3 5.0 weight_shares.7.other_ref
  959.0 9.7 add_pairs.3.refs_2_
  973.4 150.7 %tail_sums.1 = (f32[256,2048]{1,0:T(8,128)}, f32[256,1024]{1,0:T(8,128)}, f32[128,2048]{1,0:T(8,128)}, f32[128,256]{1,0:T(8,128)}, f32[128,256]{1,0:T(8,128)}, /...) custom-call(bf16[256,2048]{1,0:T(8,128)(2,1)} %convert_element_type., ...), custom_call_target="tpu_custom_call" | custom-call | flops 30000001024 | bytes 1 | tf_op jit(solution)/shard_map/tail_sums/pallas_call | solution.py:1245
  1140.5 7.1 widen.6
  1150.9 7.1 widen.7
  1158.0 6.5 widen.8
  (337 shorter events, 172.3 us)
Async XLA Ops:
  7.2 504.4 %copy-start = (bf16[1024,512]{1,0:T(8,128)(2,1)S(1)}, bf16[1024,512]{1,0:T(8,128)(2,1)}, u32[]{:S(2)}) copy-start(bf16[1024,512]{1,0:T(8,128)(2,1)} %param.42) | copy-start | bytes 3145732
  7.2 226.8 %all-gather.2.cloned.1.call-start = ((), (), s32[]{:S(2)}) async-start(), calls=%async_computation | async-start | bytes 15925248 | tf_op jit(solution)/shard_map/all_gather | solution.py:1716
  14.0 1112.1 %all-reduce.9.cloned.1.call-start = ((), (), s32[]{:S(2)}) async-start(), calls=%async_computation.1 | async-start | bytes 56623104 | tf_op jit(solution)/shard_map/psum | solution.py:1790
  15.0 112.9 %copy-start.63 = (bf16[2,204,2048]{2,0,1:T(2,128)(2,1)S(1)}, bf16[2,204,2048]{2,0,1:T(2,128)(2,1)}, u32[]{:S(2)}) copy-start(bf16[2,204,2048]{2,0,1:T(2,128)(2,1)} %param.23) | copy-start | bytes 5013508
  128.7 105.3 %copy-start.8 = (bf16[2,208,2048]{2,1,0:T(8,128)(2,1)}, bf16[2,208,2048]{2,1,0:T(8,128)(2,1)S(1)}, u32[]{:S(2)}) copy-start(bf16[2,208,2048]{2,1,0:T(8,128)(2,1)S(1)} %pad.25.clone) | copy-start | bytes 5111812
  140.9 89.4 %copy-start.32 = (bf16[2,16,1024]{2,1,0:T(8,128)(2,1)}, bf16[2,16,1024]{2,1,0:T(8,128)(2,1)S(1)}, u32[]{:S(2)}) copy-start(bf16[2,16,1024]{2,1,0:T(8,128)(2,1)S(1)} %pad.27.clone) | copy-start | bytes 196612
  140.9 89.4 %copy-start.52 = (f32[8,128]{1,0:T(8,128)}, f32[8,128]{1,0:T(8,128)S(1)}, u32[]{:S(2)}) copy-start(f32[8,128]{1,0:T(8,128)S(1)} %get-tuple-element.215) | copy-start | bytes 12292
  144.1 85.0 %copy-start.30 = (bf16[32,2560]{1,0:T(8,128)(2,1)}, bf16[32,2560]{1,0:T(8,128)(2,1)S(1)}, u32[]{:S(2)}) copy-start(bf16[32,2560]{1,0:T(8,128)(2,1)S(1)} %get-tuple-element.112) | copy-start | bytes 491524
  145.7 83.4 %copy-start.17 = (f32[2,224,896]{2,1,0:T(8,128)}, f32[2,224,896]{2,1,0:T(8,128)S(1)}, u32[]{:S(2)}) copy-start(f32[2,224,896]{2,1,0:T(8,128)S(1)} %or_select_fusion.refs_4_) | copy-start | bytes 4816900
  399.6 36.6 %copy-start.54 = (bf16[3328,2048]{1,0:T(8,128)(2,1)S(1)}, bf16[3328,2048]{1,0:T(8,128)(2,1)}, u32[]{:S(2)}) copy-start(bf16[3328,2048]{1,0:T(8,128)(2,1)} %get-tuple-element.136.refs_0_) | copy-start | bytes 40894468
  570.3 162.9 %collective-permute-start = (bf16[432,2048]{1,0:T(8,128)(2,1)}, bf16[432,2048]{1,0:T(8,128)(2,1)}, u32[]{:S(2)}, u32[]{:S(2)}) collective-permute-start(bf16[432,2048]{1,0:T(8,128)(2,1)} %get-tuple-element.203), channel_id=1, source_target_pairs={{0,2},{1,3},{8,10},{9,11},{16,18},{17,19},{24,26},{25,27}} | collective-permute-start | bytes 5308424 | tf_op jit(solution)/shard_map/ppermute | solution.py:56
  572.9 160.3 %collective-permute-start.1 = (bf16[432,2048]{1,0:T(8,128)(2,1)}, bf16[432,2048]{1,0:T(8,128)(2,1)}, u32[]{:S(2)}, u32[]{:S(2)}) collective-permute-start(bf16[432,2048]{1,0:T(8,128)(2,1)} %get-tuple-element.202), channel_id=1, source_target_pairs={{6,4},{7,5},{14,12},{15,13},{22,20},{23,21},{30,28},{31,29}} | collective-permute-start | bytes 5308424 | tf_op jit(solution)/shard_map/ppermute | solution.py:56
  739.5 141.2 %collective-permute-start.2 = (bf16[432,2048]{1,0:T(8,128)(2,1)}, bf16[432,2048]{1,0:T(8,128)(2,1)S(1)}, u32[]{:S(2)}, u32[]{:S(2)}) collective-permute-start(bf16[432,2048]{1,0:T(8,128)(2,1)} %add_block.10), channel_id=1, source_target_pairs={{0,2},{1,3},{2,4},{3,5},{8,10},{9,11},{10,12},{11,13},{16,18},{17,... | collective-permute-start | bytes 5308424 | tf_op jit(solution)/shard_map/ppermute | solution.py:56
  745.0 135.6 %collective-permute-start.3 = (bf16[432,2048]{1,0:T(8,128)(2,1)}, bf16[432,2048]{1,0:T(8,128)(2,1)}, u32[]{:S(2)}, u32[]{:S(2)}) collective-permute-start(bf16[432,2048]{1,0:T(8,128)(2,1)} %add_block.11), channel_id=1, source_target_pairs={{4,2},{5,3},{6,4},{7,5},{12,10},{13,11},{14,12},{15,13},{20,18},{2... | collective-permute-start | bytes 5308424 | tf_op jit(solution)/shard_map/ppermute | solution.py:56
  784.6 96.1 %collective-permute-start.6 = (bf16[256,2048]{1,0:T(8,128)(2,1)}, bf16[256,2048]{1,0:T(8,128)(2,1)}, u32[]{:S(2)}, u32[]{:S(2)}) collective-permute-start(bf16[256,2048]{1,0:T(8,128)(2,1)} %get-tuple-element.205), channel_id=1, source_target_pairs={{0,2},{1,3},{8,10},{9,11},{16,18},{17,19},{24,26},{25,27}} | collective-permute-start | bytes 3145736 | tf_op jit(solution)/shard_map/ppermute | solution.py:56
  787.3 93.3 %collective-permute-start.7 = (bf16[256,2048]{1,0:T(8,128)(2,1)}, bf16[256,2048]{1,0:T(8,128)(2,1)}, u32[]{:S(2)}, u32[]{:S(2)}) collective-permute-start(bf16[256,2048]{1,0:T(8,128)(2,1)} %get-tuple-element.204), channel_id=1, source_target_pairs={{6,4},{7,5},{14,12},{15,13},{22,20},{23,21},{30,28},{31,29}} | collective-permute-start | bytes 3145736 | tf_op jit(solution)/shard_map/ppermute | solution.py:56
  796.5 82.2 %copy-start.85 = (f32[1,2048]{1,0:T(1,128)S(1)}, f32[1,2048]{1,0:T(1,128)}, u32[]{:S(2)}) copy-start(f32[1,2048]{1,0:T(1,128)} %get-tuple-element.163) | copy-start | bytes 24580
  796.5 84.1 %copy-start.86 = (f32[1,1024]{1,0:T(1,128)S(1)}, f32[1,1024]{1,0:T(1,128)}, u32[]{:S(2)}) copy-start(f32[1,1024]{1,0:T(1,128)} %get-tuple-element.167) | copy-start | bytes 12292
  886.2 28.5 %collective-permute-start.8 = (bf16[256,2048]{1,0:T(8,128)(2,1)}, bf16[256,2048]{1,0:T(8,128)(2,1)}, u32[]{:S(2)}, u32[]{:S(2)}) collective-permute-start(bf16[256,2048]{1,0:T(8,128)(2,1)} %add_block.14), channel_id=1, source_target_pairs={{0,2},{1,3},{2,4},{3,5},{8,10},{9,11},{10,12},{11,13},{16,18},{17,... | collective-permute-start | bytes 3145736 | tf_op jit(solution)/shard_map/ppermute | solution.py:56
  892.9 21.7 %collective-permute-start.9 = (bf16[256,2048]{1,0:T(8,128)(2,1)}, bf16[256,2048]{1,0:T(8,128)(2,1)S(1)}, u32[]{:S(2)}, u32[]{:S(2)}) collective-permute-start(bf16[256,2048]{1,0:T(8,128)(2,1)} %add_block.15), channel_id=1, source_target_pairs={{4,2},{5,3},{6,4},{7,5},{12,10},{13,11},{14,12},{15,13},{20,18},{2... | collective-permute-start | bytes 3145736 | tf_op jit(solution)/shard_map/ppermute | solution.py:56
  920.6 48.2 %collective-permute-start.10 = (bf16[256,2048]{1,0:T(8,128)(2,1)}, bf16[256,2048]{1,0:T(8,128)(2,1)}, u32[]{:S(2)}, u32[]{:S(2)}) collective-permute-start(bf16[256,2048]{1,0:T(8,128)(2,1)} %add_block.16), channel_id=1, source_target_pairs={{0,2},{1,3},{2,4},{3,5},{4,6},{5,7},{8,10},{9,11},{10,12},{11,13},... | collective-permute-start | bytes 3145736 | tf_op jit(solution)/shard_map/ppermute | solution.py:56
  926.6 42.1 %collective-permute-start.11 = (bf16[256,2048]{1,0:T(8,128)(2,1)}, bf16[256,2048]{1,0:T(8,128)(2,1)}, u32[]{:S(2)}, u32[]{:S(2)}) collective-permute-start(bf16[256,2048]{1,0:T(8,128)(2,1)} %add_block.17), channel_id=1, source_target_pairs={{2,0},{3,1},{4,2},{5,3},{6,4},{7,5},{10,8},{11,9},{12,10},{13,11},... | collective-permute-start | bytes 3145736 | tf_op jit(solution)/shard_map/ppermute | solution.py:56
  932.4 193.8 %collective-permute-start.4 = (bf16[432,2048]{1,0:T(8,128)(2,1)}, bf16[432,2048]{1,0:T(8,128)(2,1)S(1)}, u32[]{:S(2)}, u32[]{:S(2)}) collective-permute-start(bf16[432,2048]{1,0:T(8,128)(2,1)} %add_block.12), channel_id=1, source_target_pairs={{0,2},{1,3},{2,4},{3,5},{4,6},{5,7},{8,10},{9,11},{10,12},{11,13},... | collective-permute-start | bytes 5308424 | tf_op jit(solution)/shard_map/ppermute | solution.py:56
  940.4 185.7 %collective-permute-start.5 = (bf16[432,2048]{1,0:T(8,128)(2,1)}, bf16[432,2048]{1,0:T(8,128)(2,1)}, u32[]{:S(2)}, u32[]{:S(2)}) collective-permute-start(bf16[432,2048]{1,0:T(8,128)(2,1)} %add_block.13), channel_id=1, source_target_pairs={{2,0},{3,1},{4,2},{5,3},{6,4},{7,5},{10,8},{11,9},{12,10},{13,11},... | collective-permute-start | bytes 5308424 | tf_op jit(solution)/shard_map/ppermute | solution.py:56
  (90 other events, 409.3 us)
Sparse Core Ops, SparseCore 0:
  14.1 166.6 all-gather.1
  517.0 572.9 all-reduce.8
